TPU v7x, 512 devices: a whole 4x4x16 slice. The times are simulated.
512 devices in a mesh: dp: 32 (over z, core), seq: 16 (over y, x).
Axes of the slice: x: 4, y: 4, z: 16, core: 2. Of those that a mesh axis runs over, the one named last changes fastest.
Arguments:
- features: bfloat16 [32, 2048, 512], P('dp', 'seq'), may hold values from -8 to 8
- mask_token: bfloat16 [512], replicated, may hold values from -6 to 6
- w_query: bfloat16 [512, 512], replicated, may hold values from -0.25 to 0.25
- w_key: bfloat16 [512, 512], replicated, may hold values from -0.25 to 0.25
- w_value: bfloat16 [512, 512], replicated, may hold values from -0.25 to 0.25
- block_mask: int32 [32, 16, 16], P('dp'), may hold values from 0 to 1, as said below
- masked_ids: int32 [32, 1024], P('dp'), may hold values from 0 to 2047, as said below
- adjacency: int32 [32, 2048, 128], P('dp', 'seq'), may hold values from 0 to 1, as said below
- boundary_ids: int32 [32, 2, 512], P('dp', None, 'seq'), may hold values from 0 to 127, as said below
- boundary_counts: int32 [32, 2, 16], P('dp', None, 'seq'), may hold values from 1 to 32, as said below
- boundary_targets: int32 [32, 2, 512], P('dp', None, 'seq'), may hold values from 0 to 127
- grad_out: bfloat16 [32, 2048, 512], P('dp', 'seq'), may hold values from -6 to 6
Outputs:
- mixed: bfloat16 [32, 2048, 512], P('dp', 'seq')
- grad_query: float32 [512, 512], P(None, 'seq')
- grad_key: float32 [512, 512], P(None, 'seq')
- grad_value: float32 [512, 512], P(None, 'seq')
Inputs may be any that keep to these rules, and one draw needn't show every extreme that they name: `block_mask`: entries are 0 or 1; every diagonal block is 1. `masked_ids`: the ids of one cluster are distinct. `adjacency`: entries are 0 or 1; a row has no link to itself. `boundary_ids`: indices of rows within the sending device's block; the 32 slots of one block and direction are distinct; only the first boundary_counts slots are used by the receiver. `boundary_counts`: some block takes exactly 32 rows in every draw.
All inputs are finite; a program needn't handle non-finite values.
Results may differ from a plain program's by a relative error of at most 0.015.
The roundings to bfloat16 on the way count: a program that leaves them out, or rounds other values in their place, can miss the bound.
Values may be sent and summed in bfloat16 or wider, within the bound.
No kernel may reach another device: no remote copies, remote signals or barrier semaphores. Data moves between devices by JAX's collectives and lax.ppermute only.
A program may use at most 64 MiB of HBM per device.

v0:
```python
import jax
import jax.numpy as jnp
from jax import lax
from jax.sharding import PartitionSpec as P

HEADS = 16
BLK = 128


NEG_FILL = -1e30


def padded(cells, sides, width):
    for axis, dim in sides:
        count = lax.axis_size(axis)
        ends = count - 1
        head = lax.slice_in_dim(cells, 0, width, axis=dim)
        tail = lax.slice_in_dim(cells, cells.shape[dim] - width, cells.shape[dim], axis=dim)
        cells = jnp.concatenate(
            [
                lax.ppermute(tail, axis, [(i, (i + 1) % count) for i in range(ends)]),
                cells,
                lax.ppermute(head, axis, [((i + 1) % count, i) for i in range(ends)]),
            ],
            axis=dim,
        )
    return cells


def block_allowed(block_table, start, height, block_size):
    table_rows = lax.dynamic_slice_in_dim(block_table, start // block_size, height // block_size, 0)
    spread = jnp.repeat(jnp.repeat(table_rows, block_size, axis=0), block_size, axis=1)
    return spread > 0


def head_probs(query, keys, block_table, start, height, block_size):
    query_part = lax.dynamic_slice_in_dim(query, start, height, 1)
    scores = lax.dot_general(
        query_part, keys, (((0,), (0,)), ((), ())), preferred_element_type=jnp.float32
    )
    scores = scores * query.shape[0] ** (-0.5)
    allowed = block_allowed(block_table, start, height, block_size)
    scores = jnp.where(allowed, scores, NEG_FILL)
    highest = jnp.max(scores, axis=1, keepdims=True)
    expo = jnp.exp(scores - highest)
    return (query_part, expo / jnp.sum(expo, axis=1, keepdims=True))


def head_forward(query, keys, values, block_table, block_size):
    total = query.shape[1]
    height = min(512, total)
    count = total // height

    def one_block(index):
        start = index * height
        unused, probs = head_probs(query, keys, block_table, start, height, block_size)
        probs_low = probs.astype(jnp.bfloat16)
        return lax.dot_general(
            values, probs_low, (((1,), (1,)), ((), ())), preferred_element_type=jnp.float32
        ).astype(jnp.bfloat16)

    blocks = lax.map(one_block, jnp.arange(count))
    return jnp.transpose(blocks, (1, 0, 2)).reshape(query.shape[0], total)


def head_backward(query, keys, values, grad_head, block_table, block_size):
    total = query.shape[1]
    height = min(512, total)
    count = total // height
    scale = query.shape[0] ** (-0.5)

    def one_block(carry, index):
        key_acc, value_acc = carry
        start = index * height
        query_part, probs = head_probs(query, keys, block_table, start, height, block_size)
        probs_low = probs.astype(jnp.bfloat16)
        grad_part = lax.dynamic_slice_in_dim(grad_head, start, height, 1)
        grad_probs = lax.dot_general(
            grad_part, values, (((0,), (0,)), ((), ())), preferred_element_type=jnp.float32
        )
        inner = jnp.sum(grad_probs * probs, axis=1, keepdims=True)
        grad_scores = (probs * (grad_probs - inner) * scale).astype(jnp.bfloat16)
        grad_query = lax.dot_general(
            keys, grad_scores, (((1,), (1,)), ((), ())), preferred_element_type=jnp.float32
        ).astype(jnp.bfloat16)
        key_acc = key_acc + lax.dot_general(
            query_part, grad_scores, (((1,), (0,)), ((), ())), preferred_element_type=jnp.float32
        )
        value_acc = value_acc + lax.dot_general(
            grad_part, probs_low, (((1,), (0,)), ((), ())), preferred_element_type=jnp.float32
        )
        return ((key_acc, value_acc), grad_query)

    zeros = jnp.zeros(query.shape, jnp.float32)
    (key_acc, value_acc), query_blocks = lax.scan(one_block, (zeros, zeros), jnp.arange(count))
    grad_query = jnp.transpose(query_blocks, (1, 0, 2)).reshape(query.shape[0], total)
    return (grad_query, key_acc.astype(jnp.bfloat16), value_acc.astype(jnp.bfloat16))


def on_device(
    features,
    mask_token,
    w_query,
    w_key,
    w_value,
    block_mask,
    masked_ids,
    adjacency,
    boundary_ids,
    boundary_counts,
    boundary_targets,
    grad_out,
):
    seq_count = lax.axis_size("seq")
    seq_place = lax.axis_index("seq")
    rows_dev = features.shape[1]
    width = features.shape[2]
    head_size = width // HEADS
    share = width // seq_count
    tokens = features[0]
    positions = jnp.arange(rows_dev, dtype=jnp.int32)
    own_rows = seq_place * rows_dev + positions
    marked = jnp.any(masked_ids[0][:, None] == own_rows[None, :], axis=0)
    masked = jnp.where(marked[:, None], mask_token[None, :], tokens)
    table = block_mask[0]
    upstream = grad_out[0]
    value_rows = jnp.dot(masked, w_value, preferred_element_type=jnp.float32).astype(jnp.bfloat16)
    links = adjacency[0]
    local_sum = value_rows.astype(jnp.float32) + jnp.dot(
        links.astype(jnp.bfloat16), value_rows, preferred_element_type=jnp.float32
    )

    def pick_rows(row_ids):
        onehot = (row_ids[:, None] == positions[None, :]).astype(jnp.bfloat16)
        return jnp.dot(onehot, value_rows, preferred_element_type=jnp.float32).astype(jnp.bfloat16)

    outgoing = jnp.stack([pick_rows(boundary_ids[0, 1]), pick_rows(boundary_ids[0, 0])])
    extended = padded(outgoing, (("dp", 0),), 1)
    cluster_place = lax.axis_index("dp")
    cluster_count = lax.axis_size("dp")
    slots = jnp.arange(boundary_ids.shape[2], dtype=jnp.int32)
    valid_lower = (slots < boundary_counts[0, 0, 0]) & (cluster_place > 0)
    valid_upper = (slots < boundary_counts[0, 1, 0]) & (cluster_place < cluster_count - 1)
    pick_lower = (
        (boundary_targets[0, 0][None, :] == positions[:, None]) & valid_lower[None, :]
    ).astype(jnp.bfloat16)
    pick_upper = (
        (boundary_targets[0, 1][None, :] == positions[:, None]) & valid_upper[None, :]
    ).astype(jnp.bfloat16)
    border = jnp.dot(pick_lower, extended[0], preferred_element_type=jnp.float32)
    border = border + jnp.dot(pick_upper, extended[3], preferred_element_type=jnp.float32)
    degree = (
        1.0
        + jnp.sum(links, axis=1).astype(jnp.float32)
        + jnp.sum(pick_lower.astype(jnp.float32), axis=1)
        + jnp.sum(pick_upper.astype(jnp.float32), axis=1)
    )
    graph = (local_sum + border) / degree[:, None]
    scaled = upstream.astype(jnp.float32) / degree[:, None]
    spread_back = lax.dot_general(
        links.astype(jnp.float32), scaled, (((0,), (0,)), ((), ())), precision=lax.Precision.HIGHEST
    )
    graph_grad = (scaled + spread_back).astype(jnp.bfloat16)

    def heads_of(matrix_t):
        return matrix_t.reshape(HEADS, head_size, rows_dev)

    def rows_of(head_block):
        return head_block.reshape(width, rows_dev)

    def transposed(weight):
        return lax.dot_general(
            weight, masked, (((0,), (1,)), ((), ())), preferred_element_type=jnp.float32
        ).astype(jnp.bfloat16)

    query_h, key_h, value_h, upstream_h = (
        lax.all_to_all(
            heads_of(transposed(w_query)), "seq", split_axis=0, concat_axis=2, tiled=True
        ),
        lax.all_to_all(heads_of(transposed(w_key)), "seq", split_axis=0, concat_axis=2, tiled=True),
        lax.all_to_all(heads_of(value_rows.T), "seq", split_axis=0, concat_axis=2, tiled=True),
        lax.all_to_all(heads_of(upstream.T), "seq", split_axis=0, concat_axis=2, tiled=True),
    )
    attend = jax.vmap(lambda a, b, c: head_forward(a, b, c, table, BLK))(query_h, key_h, value_h)
    attend_rows = rows_of(lax.all_to_all(attend, "seq", split_axis=2, concat_axis=0, tiled=True)).T
    mixed = (attend_rows.astype(jnp.float32) + graph).astype(jnp.bfloat16)
    grad_q_heads, grad_k_heads, grad_v_heads = jax.vmap(
        lambda a, b, c, d: head_backward(a, b, c, d, table, BLK)
    )(query_h, key_h, value_h, upstream_h)
    grad_q_back, grad_k_back, grad_v_back = (
        lax.all_to_all(grad_q_heads, "seq", split_axis=2, concat_axis=0, tiled=True),
        lax.all_to_all(grad_k_heads, "seq", split_axis=2, concat_axis=0, tiled=True),
        lax.all_to_all(grad_v_heads, "seq", split_axis=2, concat_axis=0, tiled=True),
    )
    value_grad = (
        rows_of(grad_v_back).T.astype(jnp.float32) + graph_grad.astype(jnp.float32)
    ).astype(jnp.bfloat16)
    term_query = lax.dot_general(
        masked, rows_of(grad_q_back), (((0,), (1,)), ((), ())), preferred_element_type=jnp.float32
    )
    term_key = lax.dot_general(
        masked, rows_of(grad_k_back), (((0,), (1,)), ((), ())), preferred_element_type=jnp.float32
    )
    term_value = lax.dot_general(
        masked, value_grad, (((0,), (0,)), ((), ())), preferred_element_type=jnp.float32
    )
    summed = lax.psum((term_query, term_key, term_value), ("dp", "seq"))
    results = tuple(
        (lax.dynamic_slice_in_dim(item, seq_place * share, share, 1) for item in summed)
    )
    return (mixed[None], results[0], results[1], results[2])


def solution(mesh):
    placed = (
        P("dp", "seq", None),
        P(),
        P(),
        P(),
        P(),
        P("dp", None, None),
        P("dp", None),
        P("dp", "seq", None),
        P("dp", None, "seq"),
        P("dp", None, "seq"),
        P("dp", None, "seq"),
        P("dp", "seq", None),
    )
    return jax.shard_map(
        on_device,
        mesh=mesh,
        in_specs=placed,
        out_specs=(P("dp", "seq", None), P(None, "seq"), P(None, "seq"), P(None, "seq")),
        check_vma=False,
    )
```

profile of v0, /device:TPU:1, one launch (start us, length us, event | category | flops | bytes accessed | tf_op | source)
XLA Modules:
  0.0 721.9 jit_solution(3149969000276558266)
XLA Ops:
  10.2 7.6 %all-to-all-start.2 = ((bf16[16,32,128]{2,1,0:T(8,128)(2,1)}), bf16[16,32,128]{2,1,0:T(8,128)(2,1)S(1)}, u32[]{:S(2)}, u32[]{:S(2)}) async-start(bf16[16,32,128]{2,1,0:T(8,128)(2,1)} %bitcast.22), calls=%async_computation.2 | async-start | bytes 262144 | tf_op jit(solution)/shard_map/all_to_all | solution.py:181
  18.7 4.7 collective-permute-start.1
  36.1 6.9 all-to-all-start.1
  43.0 6.9 all-to-all-done.1
  49.9 3.5 all-to-all-start
  53.4 6.8 all-to-all-done
  60.2 4.0 all-to-all-start.4
  64.2 6.8 all-to-all-done.4
  71.1 77.9 %while.33 = (s32[]{:T(128)}, f32[1,32,2048]{2,1,0:T(8,128)S(1)}, f32[1,32,2048]{2,1,0:T(8,128)S(1)}, bf16[4,1,32,512]{3,2,1,0:T(8,128)(2,1)S(1)}, s32[4]{0:T(128...) while((s32[]{:T(128)}, f32[1,32,2048]{2,1,0:T(8,128)S(1)}, ...), condition=%wide.region_12.13_spmd.clone, body=%wide.region_8.12_spmd.clone.sunk | while | flops 354695776 | bytes 72948608 | solution.py:95
  81.1 4.1 fusion.123
  100.6 4.1 fusion.123
  120.0 4.1 fusion.123
  139.5 4.1 fusion.123
  150.2 11.5 %reduce.29 = bf16[2048,32]{1,0:T(8,128)(2,1)S(1)} reduce(bf16[2048,1,32]{2,1,0:T(2,128)(2,1)S(1)} %bitcast.311, bf16[]{:T(256)} %broadcast.210), dimensions={1}, to_apply=%bitcast.212.reduce_sub_computation | reduce | bytes 262146
  162.9 3.7 all-to-all-start.7
  167.4 11.5 %reduce.27 = bf16[2048,32]{1,0:T(8,128)(2,1)S(1)} reduce(bf16[2048,1,32]{2,1,0:T(2,128)(2,1)S(1)} %bitcast.313, bf16[]{:T(256)} %broadcast.210), dimensions={1}, to_apply=%bitcast.208.reduce_sub_computation | reduce | bytes 262146
  180.9 11.6 %reduce.28 = bf16[2048,32]{1,0:T(8,128)(2,1)S(1)} reduce(bf16[2048,1,32]{2,1,0:T(2,128)(2,1)S(1)} %bitcast.314, bf16[]{:T(256)} %broadcast.210), dimensions={1}, to_apply=%bitcast.210.reduce_sub_computation | reduce | bytes 262146
  193.6 6.6 all-to-all-start.5
  213.3 4.1 all-to-all-done.6
  220.1 36.2 %while.32 = (s32[]{:T(128)}, bf16[4,1,32,512]{3,2,1,0:T(8,128)(2,1)S(1)}, s32[4]{0:T(128)S(1)}, s32[16,16]{1,0:T(8,128)S(1)}, bf16[1,32,2048]{2,1,0:T(8,128)(2,1...) while((s32[]{:T(128)}, ...), condition=%wide.region_4.5_spmd, body=%wide.region_1.4_spmd.sunk | while | flops 142621792 | bytes 15035170 | solution.py:62
  257.2 11.5 %reduce.26 = bf16[2048,32]{1,0:T(8,128)(2,1)S(1)} reduce(bf16[2048,1,32]{2,1,0:T(2,128)(2,1)S(1)} %bitcast.312, bf16[]{:T(256)} %broadcast.210), dimensions={1}, to_apply=%bitcast.206.reduce_sub_computation | reduce | bytes 262146
  269.9 3.5 all-to-all-start.3
  273.7 6.5 all-to-all-done.3
  283.5 427.0 %all-reduce.3.cloned.1.call-done = (f32[512,512]{0,1:T(8,128)}, f32[512,512]{0,1:T(8,128)}, f32[512,512]{0,1:T(8,128)}) async-done(((f32[512,512]{0,1:T(8,128)}, f32[512,512]{0,1:T(8,128)}, f32[512,512]{0,1:T(8,128)}), (f32[512,512]{0,1:T(8,128)}, f32[512,512]{0,1:T(8,128)}, f32[512,512]{0,1:T(8,128)})) %all-reduce.3.cloned.1.call-update) | async-done | bytes 3145744 | tf_op jit(solution)/shard_map/psum | solution.py:207
  (195 shorter events, 140.3 us)
Async XLA Ops:
  7.2 28.1 %copy-start.5 = (bf16[1,128,512]{2,1,0:T(8,128)(2,1)S(1)}, bf16[1,128,512]{2,1,0:T(8,128)(2,1)}, u32[]{:S(2)}) copy-start(bf16[1,128,512]{2,1,0:T(8,128)(2,1)} %param.27) | copy-start | bytes 393220
  7.2 63.9 %copy-start.6 = (s32[1,16,16]{2,1,0:T(8,128)S(1)}, s32[1,16,16]{2,1,0:T(8,128)}, u32[]{:S(2)}) copy-start(s32[1,16,16]{2,1,0:T(8,128)} %param.21) | copy-start | bytes 3076
  10.2 25.9 %all-to-all-start.2 = ((bf16[16,32,128]{2,1,0:T(8,128)(2,1)}), bf16[16,32,128]{2,1,0:T(8,128)(2,1)S(1)}, u32[]{:S(2)}, u32[]{:S(2)}) async-start(bf16[16,32,128]{2,1,0:T(8,128)(2,1)} %bitcast.22), calls=%async_computation.2 | async-start | bytes 262144 | tf_op jit(solution)/shard_map/all_to_all | solution.py:181
  18.7 254.7 %collective-permute-start.1 = (bf16[1,32,512]{2,1,0:T(8,128)(2,1)S(1)}, bf16[1,32,512]{2,1,0:T(8,128)(2,1)S(1)}, u32[]{:S(2)}, u32[]{:S(2)}) collective-permute-start(bf16[1,32,512]{2,1,0:T(8,128)(2,1)S(1)} %fusion.48), channel_id=1, source_target_pairs={{16,0},{32,16},{48,32},{64,48},{80,64},{96,80},{112,96},{128,112},... | collective-permute-start | bytes 98312 | tf_op jit(solution)/shard_map/ppermute | solution.py:23
  23.6 258.2 %collective-permute-start = (bf16[1,32,512]{2,1,0:T(8,128)(2,1)S(1)}, bf16[1,32,512]{2,1,0:T(8,128)(2,1)}, u32[]{:S(2)}, u32[]{:S(2)}) collective-permute-start(bf16[1,32,512]{2,1,0:T(8,128)(2,1)S(1)} %fusion.47), channel_id=1, source_target_pairs={{0,16},{16,32},{32,48},{48,64},{64,80},{80,96},{96,112},{112,128},... | collective-permute-start | bytes 98312 | tf_op jit(solution)/shard_map/ppermute | solution.py:21
  36.1 13.8 %all-to-all-start.1 = ((bf16[16,32,128]{2,1,0:T(8,128)(2,1)}), bf16[16,32,128]{2,1,0:T(8,128)(2,1)S(1)}, u32[]{:S(2)}, u32[]{:S(2)}) async-start(bf16[16,32,128]{2,1,0:T(8,128)(2,1)} %bitcast.18), calls=%async_computation.1 | async-start | bytes 262144 | tf_op jit(solution)/shard_map/all_to_all | solution.py:180
  49.9 10.3 %all-to-all-start = ((bf16[16,32,128]{2,1,0:T(8,128)(2,1)}), bf16[16,32,128]{2,1,0:T(8,128)(2,1)S(1)}, u32[]{:S(2)}, u32[]{:S(2)}) async-start(bf16[16,32,128]{2,1,0:T(8,128)(2,1)} %bitcast.14), calls=%async_computation | async-start | bytes 262144 | tf_op jit(solution)/shard_map/all_to_all | solution.py:177
  60.2 10.8 %all-to-all-start.4 = ((bf16[16,32,128]{2,1,0:T(8,128)(2,1)}), bf16[16,32,128]{2,1,0:T(8,128)(2,1)S(1)}, u32[]{:S(2)}, u32[]{:S(2)}) async-start(bf16[16,32,128]{2,1,0:T(8,128)(2,1)} %bitcast.45), calls=%async_computation.4 | async-start | bytes 262144 | tf_op jit(solution)/shard_map/all_to_all | solution.py:182
  78.4 1.9 copy-start.1
  81.1 4.1 copy-start.2
  97.9 1.9 copy-start.1
  100.5 4.1 copy-start.2
  117.4 1.9 copy-start.1
  120.0 4.1 copy-start.2
  136.8 1.9 copy-start.1
  139.5 4.1 copy-start.2
  162.9 30.7 %all-to-all-start.7 = ((bf16[16,2,2048]{2,1,0:T(2,128)(2,1)}), bf16[16,2,2048]{2,1,0:T(2,128)(2,1)S(1)}, u32[]{:S(2)}, u32[]{:S(2)}) async-start(bf16[16,2,2048]{2,1,0:T(2,128)(2,1)} %reshape.349), calls=%async_computation.7 | async-start | bytes 262144 | tf_op jit(solution)/shard_map/all_to_all | solution.py:193
  180.1 21.7 %copy-start.4 = (s32[1,128,128]{2,1,0:T(8,128)S(1)}, s32[1,128,128]{2,1,0:T(8,128)}, u32[]{:S(2)}) copy-start(s32[1,128,128]{2,1,0:T(8,128)} %param.23) | copy-start | bytes 196612
  180.9 21.5 %copy-start.3 = (bf16[1,128,512]{2,1,0:T(8,128)(2,1)S(1)}, bf16[1,128,512]{2,1,0:T(8,128)(2,1)}, u32[]{:S(2)}) copy-start(bf16[1,128,512]{2,1,0:T(8,128)(2,1)} %param.16) | copy-start | bytes 393220
  180.9 21.5 %copy-start.7 = (bf16[512]{0:T(512)(128)(2,1)S(1)}, bf16[512]{0:T(512)(128)(2,1)}, u32[]{:S(2)}) copy-start(bf16[512]{0:T(512)(128)(2,1)} %param.17) | copy-start | bytes 3076
  193.6 13.4 %all-to-all-start.5 = ((bf16[16,2,2048]{2,1,0:T(2,128)(2,1)}), bf16[16,2,2048]{2,1,0:T(2,128)(2,1)S(1)}, u32[]{:S(2)}, u32[]{:S(2)}) async-start(bf16[16,2,2048]{2,1,0:T(2,128)(2,1)} %reshape.345), calls=%async_computation.5 | async-start | bytes 262144 | tf_op jit(solution)/shard_map/all_to_all | solution.py:191
  207.1 10.3 %all-to-all-start.6 = ((bf16[16,2,2048]{2,1,0:T(2,128)(2,1)}), bf16[16,2,2048]{2,1,0:T(2,128)(2,1)S(1)}, u32[]{:S(2)}, u32[]{:S(2)}) async-start(bf16[16,2,2048]{2,1,0:T(2,128)(2,1)} %reshape.347), calls=%async_computation.6 | async-start | bytes 262144 | tf_op jit(solution)/shard_map/all_to_all | solution.py:192
  210.6 499.9 %all-reduce.3.cloned.1.call-start = ((), (), s32[]{:S(2)}) async-start(), calls=%async_computation.8 | async-start | bytes 6291456 | tf_op jit(solution)/shard_map/psum | solution.py:207
  269.9 10.3 %all-to-all-start.3 = ((bf16[16,2,2048]{2,1,0:T(2,128)(2,1)}), bf16[16,2,2048]{2,1,0:T(2,128)(2,1)S(1)}, u32[]{:S(2)}, u32[]{:S(2)}) async-start(bf16[16,2,2048]{2,1,0:T(2,128)(2,1)} %reshape.343), calls=%async_computation.3 | async-start | bytes 262144 | tf_op jit(solution)/shard_map/all_to_all | solution.py:185
  (1 other events, 1.1 us)
Sparse Core Ops, SparseCore 0:
  220.2 490.1 all-reduce.2
where the time goes:
time: 726 us; the launch traced here: 722 us
  waiting for transfers between devices  461 us (63%)
  local copies, waits for them, and re-layouts  69.2 us (10%)
  matrix products  62.9 us (9%)
  other arithmetic  61.8 us (9%)
  starting transfers between devices  45.9 us (6%)
  between operations  14.8 us (2%)
    psum x1, waiting for transfers between devices, on_device(): summed = lax.psum((term_query, term_key, term_value), ('dp', 'seq'))  427 us
    unnamed x8, other arithmetic  46.2 us
    broadcast_in_dim x8, local copies, waits for them, and re-layouts, block_allowed(): jnp.repeat(jnp.repeat(table_rows, block_size, axis=0), block_size, axis=1)  27.7 us
    dot_general x4, matrix products, one_block(): lax.dot_general(grad_part, probs_low, (((1,), (0,)), ((), ())), preferred...  16.3 us
    dot_general x8, matrix products, head_probs(): lax.dot_general(query_part, keys, (((0,), (0,)), ((), ())), preferred_ele...  15.3 us
  transfers between devices with their start and end apart: 11, of which 7 were waited for; matrix products, arithmetic and copies ran while one was open for 25% of the time, Pallas kernels for 0%

commit v1 on v0

v1 whole, which is shorter than its diff:
```python
import jax
import jax.numpy as jnp
from jax import lax
from jax.experimental import pallas as pl
from jax.experimental.pallas import tpu as pltpu
from jax.sharding import PartitionSpec as P

HEADS = 16
NB = 16
BLK = 128
HD = 32
ROWS = 128
WIDTH = 512
UNROLL = 4
SLOTS = NB * NB + UNROLL
SCALE = HD**-0.5
LOG2E = 1.4426950408889634
EXP_SCALE = SCALE * LOG2E
LOWEST = -3e38
BF = jnp.bfloat16
F32 = jnp.float32
CHIPS = 16
CHUNK = 12

SM = pl.BlockSpec(memory_space=pltpu.SMEM)
VM = pl.BlockSpec(memory_space=pltpu.VMEM)


def attach(targets, counts_ref, place_ref, side):
    slots = targets.shape[1]
    rows = lax.broadcasted_iota(jnp.int32, (ROWS, slots), 0)
    slot = lax.broadcasted_iota(jnp.int32, (ROWS, slots), 1)
    inside = (place_ref[0] > 0) if side == 0 else (place_ref[0] < place_ref[2] - 1)
    limit = jnp.where(inside, counts_ref[0, side, 0], 0)
    return jnp.where((targets == rows) & (slot < limit), 1.0, 0.0)


def rows_kernel(
    place_ref, counts_ref, tokens_ref, token_ref, wq_ref, wk_ref, wv_ref, ids_ref, links_ref,
    sends_ref, targets_ref, grad_ref, masked_ref, heads_ref, out_ref, local_ref, degree_ref,
):
    own = place_ref[1] * ROWS + lax.broadcasted_iota(jnp.int32, (ROWS, 128), 0)
    hit = own < 0
    for part in range(ids_ref.shape[1] // 128):
        hit = hit | (own == ids_ref[:, part * 128 : (part + 1) * 128])
    marked = jnp.max(jnp.where(hit, 1.0, 0.0), axis=1, keepdims=True) > 0
    masked = jnp.where(marked, token_ref[...].astype(F32), tokens_ref[0].astype(F32)).astype(BF)
    masked_ref[...] = masked

    links_low = links_ref[0].astype(F32).astype(BF)
    value_wide = jnp.dot(masked, wv_ref[...], preferred_element_type=F32)
    value = value_wide.astype(BF)
    local_ref[...] = value.astype(F32) + jnp.dot(links_low, value, preferred_element_type=F32)
    pick = lax.broadcasted_iota(jnp.int32, (ROWS, 32), 0)
    for side in range(2):
        onehot = jnp.where(sends_ref[0, side : side + 1, :] == pick, 1.0, 0.0).astype(BF)
        out_ref[side] = lax.dot_general(
            onehot, value, (((0,), (0,)), ((), ())), preferred_element_type=F32
        ).astype(BF)

    degree = 1.0 + jnp.sum(links_ref[0].astype(F32), axis=1, keepdims=True)
    for side in range(2):
        links_here = attach(targets_ref[0, side : side + 1, :], counts_ref, place_ref, side)
        degree = degree + jnp.sum(links_here, axis=1, keepdims=True)
    degree_ref[...] = degree

    scaled = (grad_ref[0].astype(F32) / degree).T
    high = scaled.astype(BF)
    rest = scaled - high.astype(F32)
    mid = rest.astype(BF)
    low = (rest - mid.astype(F32)).astype(BF)
    spread = jnp.dot(low, links_low, preferred_element_type=F32)
    spread = spread + jnp.dot(mid, links_low, preferred_element_type=F32)
    spread = spread + jnp.dot(high, links_low, preferred_element_type=F32)
    graph_grad = (scaled + spread).astype(BF)

    key = jnp.dot(masked, wk_ref[...], preferred_element_type=F32).T.astype(BF)
    query = jnp.dot(masked, wq_ref[...], preferred_element_type=F32).T.astype(BF)
    value_t = value_wide.T.astype(BF)
    grad_t = grad_ref[0].astype(F32).T.astype(BF)
    for place, item in enumerate((key, value_t, query, grad_t, graph_grad)):
        for head in range(HEADS):
            heads_ref[head, place * HD : (place + 1) * HD, :] = item[head * HD : (head + 1) * HD]


def list_kernel(mask_ref, list_ref, count_ref):
    def row(i, n):
        for j in range(NB):
            list_ref[n] = i * NB + j
            n = n + mask_ref[0, i, j]
        return n

    n = lax.fori_loop(0, NB, row, jnp.int32(0))
    for u in range(UNROLL):
        list_ref[n + u] = NB * NB
    count_ref[0] = n


def attention_kernel(
    list_ref, count_ref, x_ref, att_ref, grad_ref, keys, duo, expo, gprob, peak, top, total, inner,
    out_acc, q_acc, k_acc, v_acc,
):
    steps = lax.div(count_ref[0] + (UNROLL - 1), jnp.int32(UNROLL))
    duo[...] = jnp.zeros_like(duo)
    k_acc[...] = jnp.zeros_like(k_acc)
    v_acc[...] = jnp.zeros_like(v_acc)
    for b in range(NB):
        keys[b] = x_ref[b, 0:64, :].T
        duo[b, 0:HD, 0:BLK] = x_ref[b, 64:96, :]
        duo[b, HD : 2 * HD, BLK : 2 * BLK] = x_ref[b, 96:128, :]

    def pair(step, u):
        p = step * UNROLL + u
        index = list_ref[p]
        return p, lax.shift_right_logical(index, 4), lax.bitwise_and(index, 15)

    def scores(step, carry):
        before, m, l, d = carry
        parts = []
        for u in range(UNROLL):
            p, i, j = pair(step, u)
            both = jnp.dot(keys[j], duo[i], preferred_element_type=F32)
            s = both[:, :BLK]
            parts.append((p, i, s, both[:, BLK:], jnp.max(s, axis=0, keepdims=True)))
        for p, i, s, g, high in parts:
            same = i == before
            m_old = jnp.where(same, m, LOWEST)
            m = jnp.maximum(m_old, high)
            fade = jnp.exp2((m_old - m) * EXP_SCALE)
            e = jnp.exp2((s - m) * EXP_SCALE)
            l = jnp.where(same, l, 0.0) * fade + jnp.sum(e, axis=0, keepdims=True)
            d = jnp.where(same, d, 0.0) * fade + jnp.sum(e * g, axis=0, keepdims=True)
            expo[p] = e
            gprob[p] = g
            peak[p] = m
            top[i] = m
            total[i] = l
            inner[i] = d
            before = i
        return before, m, l, d

    zero = jnp.zeros((1, BLK), F32)
    lax.fori_loop(0, steps, scores, (jnp.int32(-1), zero, zero, zero))

    def grads(step, carry):
        before, o, q = carry
        for u in range(UNROLL):
            p, i, j = pair(step, u)
            share = 1.0 / total[i]
            prob = expo[p] * (jnp.exp2((peak[p] - top[i]) * EXP_SCALE) * share)
            low = prob.astype(BF)
            ds = (prob * (gprob[p] - inner[i] * share) * SCALE).astype(BF)
            same = i == before
            o = jnp.where(same, o, 0.0) + jnp.dot(
                x_ref[j, 32:64, :], low, preferred_element_type=F32
            )
            q = jnp.where(same, q, 0.0) + jnp.dot(
                x_ref[j, 0:32, :], ds, preferred_element_type=F32
            )
            out_acc[i] = o
            q_acc[i] = q
            k_acc[j] += lax.dot_general(
                duo[i, 0:HD, 0:BLK], ds, (((1,), (1,)), ((), ())), preferred_element_type=F32
            )
            v_acc[j] += lax.dot_general(
                duo[i, HD : 2 * HD, BLK : 2 * BLK], low, (((1,), (1,)), ((), ())),
                preferred_element_type=F32,
            )
            before = i
        return before, o, q

    wide = jnp.zeros((HD, BLK), F32)
    lax.fori_loop(0, steps, grads, (jnp.int32(-1), wide, wide))

    for b in range(NB):
        cols = slice(b * BLK, (b + 1) * BLK)
        att_ref[b] = out_acc[b].astype(BF)
        grad_ref[0:32, cols] = q_acc[b].astype(BF)
        grad_ref[32:64, cols] = k_acc[b].astype(BF)
        grad_ref[64:96, cols] = (
            v_acc[b].astype(BF).astype(F32) + x_ref[b, 128:160, :].astype(F32)
        ).astype(BF)


def weights_kernel(place_ref, grad_ref, masked_ref, keep_ref, send_ref):
    core = lax.bitwise_and(place_ref[0], 1)
    both = jnp.dot(
        grad_ref[...], masked_ref[...].reshape(NB * ROWS, WIDTH), preferred_element_type=F32
    )
    for half, first in ((0, True), (1, False)):
        for lane in range(2):
            for r in range(8):
                piece = both[
                    r * CHUNK : (r + 1) * CHUNK,
                    (half * 2 + lane) * 128 : (half * 2 + lane + 1) * 128,
                ]
                slot = lane * 8 + r

                @pl.when(core == half)
                def _():
                    keep_ref[slot] = piece

                @pl.when(core != half)
                def _():
                    send_ref[slot] = piece


def output_kernel(place_ref, own_ref, other_ref, q_ref, k_ref, v_ref, full):
    core = lax.bitwise_and(place_ref[0], 1)
    for half in range(2):
        mine = core == half
        for lane in range(2):
            for r in range(8):
                slot = lane * 8 + r
                full[
                    r * CHUNK : (r + 1) * CHUNK,
                    (half * 2 + lane) * 128 : (half * 2 + lane + 1) * 128,
                ] = jnp.where(mine, own_ref[slot], other_ref[slot])
    for lane in range(4):
        block = full[:, lane * 128 : (lane + 1) * 128].T
        for place, ref in enumerate((q_ref, k_ref, v_ref)):
            ref[lane * 128 : (lane + 1) * 128, :] = block[:, place * HD : (place + 1) * HD]


def mixed_kernel(
    place_ref, counts_ref, targets_ref, att_ref, local_ref, degree_ref, lower_ref, upper_ref,
    mixed_ref,
):
    border = jnp.zeros((ROWS, WIDTH), F32)
    for side, ref in ((0, lower_ref), (1, upper_ref)):
        here = attach(targets_ref[0, side : side + 1, :], counts_ref, place_ref, side)
        border = border + jnp.dot(here.astype(BF), ref[0], preferred_element_type=F32)
    graph = (local_ref[...] + border) / degree_ref[...]
    attended = att_ref[...].reshape(WIDTH, ROWS).astype(F32).T
    mixed_ref[0] = (attended + graph).astype(BF)


def call(kernel, name, shapes, in_specs, scratch=(), limit=32, flops=0, moved=0):
    out = tuple(jax.ShapeDtypeStruct(shape, kind) for shape, kind in shapes)
    return pl.pallas_call(
        kernel,
        out_shape=out,
        in_specs=in_specs,
        out_specs=tuple(VM for _ in out),
        scratch_shapes=scratch,
        compiler_params=pltpu.CompilerParams(vmem_limit_bytes=limit * 1024 * 1024),
        cost_estimate=pl.CostEstimate(flops=flops, bytes_accessed=moved, transcendentals=0),
        name=name,
    )


def on_device(
    features, mask_token, w_query, w_key, w_value, block_mask, masked_ids, adjacency, boundary_ids,
    boundary_counts, boundary_targets, grad_out,
):
    clusters = lax.axis_size("dp")
    place = jnp.stack(
        [lax.axis_index("dp"), lax.axis_index("seq"), jnp.int32(clusters)]
    ).astype(jnp.int32)

    masked, heads, outgoing, local, degree = call(
        rows_kernel,
        "rows",
        [
            ((ROWS, WIDTH), BF),
            ((HEADS, 5 * HD, ROWS), BF),
            ((2, 32, WIDTH), BF),
            ((ROWS, WIDTH), F32),
            ((ROWS, 1), F32),
        ],
        [SM, SM] + [VM] * 10,
        flops=400_000_000,
        moved=3_000_000,
    )(
        place, boundary_counts, features, mask_token[None], w_query, w_key, w_value, masked_ids,
        adjacency, boundary_ids, boundary_targets, grad_out,
    )

    x = lax.all_to_all(heads, "seq", split_axis=0, concat_axis=0, tiled=True)
    spread = jnp.broadcast_to(masked[None], (NB, ROWS, WIDTH))
    masked_all = lax.all_to_all(spread, "seq", split_axis=0, concat_axis=0, tiled=True)
    up = [(c, c + 1) for c in range(clusters - 1)]
    lower = lax.ppermute(outgoing[0:1], "dp", up)
    upper = lax.ppermute(outgoing[1:2], "dp", [(b, a) for a, b in up])

    pairs, count = pl.pallas_call(
        list_kernel,
        out_shape=(
            jax.ShapeDtypeStruct((SLOTS + 4,), jnp.int32),
            jax.ShapeDtypeStruct((1,), jnp.int32),
        ),
        in_specs=[SM],
        out_specs=(SM, SM),
        cost_estimate=pl.CostEstimate(flops=1_000_000, bytes_accessed=2_000_000, transcendentals=0),
        name="pair_list",
    )(block_mask)

    attended, grads = call(
        attention_kernel,
        "attention",
        [((NB, HD, BLK), BF), ((3 * HD, NB * BLK), BF)],
        [SM, SM, VM],
        scratch=[
            pltpu.VMEM((NB, BLK, 2 * HD), BF),
            pltpu.VMEM((NB + 1, 2 * HD, 2 * BLK), BF),
            pltpu.VMEM((SLOTS, BLK, BLK), F32),
            pltpu.VMEM((SLOTS, BLK, BLK), F32),
            pltpu.VMEM((SLOTS, 1, BLK), F32),
            pltpu.VMEM((NB + 1, 1, BLK), F32),
            pltpu.VMEM((NB + 1, 1, BLK), F32),
            pltpu.VMEM((NB + 1, 1, BLK), F32),
            pltpu.VMEM((NB + 1, HD, BLK), F32),
            pltpu.VMEM((NB + 1, HD, BLK), F32),
            pltpu.VMEM((NB, HD, BLK), F32),
            pltpu.VMEM((NB, HD, BLK), F32),
        ],
        limit=48,
        flops=5_000_000_000,
        moved=20_000_000,
    )(pairs, count, x)

    back = lax.all_to_all(attended, "seq", split_axis=0, concat_axis=0, tiled=True)
    (mixed,) = call(
        mixed_kernel,
        "mixed",
        [((1, ROWS, WIDTH), BF)],
        [SM, SM] + [VM] * 6,
        flops=20_000_000,
        moved=1_000_000,
    )(place, boundary_counts, boundary_targets, back, local, degree, lower, upper)

    keep, send = call(
        weights_kernel,
        "weights",
        [((CHIPS, CHUNK, 128), F32), ((CHIPS, CHUNK, 128), F32)],
        [SM, VM, VM],
        flops=200_000_000,
        moved=3_000_000,
    )(place, grads, masked_all)

    swap = [(c, c ^ 1) for c in range(clusters)]
    groups = [[chip * 2 + core for chip in range(clusters // 2)] for core in range(2)]
    pair_sum = keep + lax.ppermute(send, "dp", swap)
    terms = lax.all_to_all(
        pair_sum, "dp", split_axis=0, concat_axis=0, tiled=True, axis_index_groups=groups
    )
    reduced = jnp.broadcast_to(jnp.sum(terms, axis=0, keepdims=True), terms.shape)
    half = lax.all_to_all(
        reduced, "dp", split_axis=0, concat_axis=0, tiled=True, axis_index_groups=groups
    )
    other = lax.ppermute(half, "dp", swap)
    grad_query, grad_key, grad_value = call(
        output_kernel,
        "outputs",
        [((WIDTH, HD), F32)] * 3,
        [SM, VM, VM],
        scratch=[pltpu.VMEM((3 * HD, WIDTH), F32)],
        flops=1_000_000,
        moved=1_000_000,
    )(place, half, other)
    return mixed, grad_query, grad_key, grad_value


def solution(mesh):
    placed = (
        P("dp", "seq", None),
        P(),
        P(),
        P(),
        P(),
        P("dp", None, None),
        P("dp", None),
        P("dp", "seq", None),
        P("dp", None, "seq"),
        P("dp", None, "seq"),
        P("dp", None, "seq"),
        P("dp", "seq", None),
    )
    return jax.shard_map(
        on_device,
        mesh=mesh,
        in_specs=placed,
        out_specs=(P("dp", "seq", None), P(None, "seq"), P(None, "seq"), P(None, "seq")),
        check_vma=False,
    )
```

time: 726 us -> 138 us (0.19)
  waiting for transfers between devices: 461 us -> 16.1 us
  blocking collectives: 0 us -> 65.1 us
  matrix products: 62.9 us -> 0 us
  other arithmetic: 61.8 us -> 0.11 us
  local copies, waits for them, and re-layouts: 69.2 us -> 13.7 us
  starting transfers between devices: 45.9 us -> 25.9 us
  Pallas kernels: 0 us -> 15.1 us
  between operations: 14.8 us -> 0.76 us
    psum x1 -> x0, waiting for transfers between devices: 427 us -> none  [on_device(): summed = lax.psum((term_query, term_key, term_value), ('dp', 'seq'))]
    all_to_all x0 -> x3, blocking collectives: none -> 65.1 us  [the longest x1 28.6 us: on_device(): lax.all_to_all(pair_sum, 'dp', split_axis=0, concat_axis=0, tiled=True, a...]
    dot_general x40 -> x0, matrix products: 62.9 us -> none  [the longest x4 16.3 us: one_block(): lax.dot_general(grad_part, probs_low, (((1,), (0,)), ((), ())), preferred...]
    unnamed x8 -> x0, other arithmetic: 46.2 us -> none
    all_to_all x8 -> x2, starting transfers between devices: 39.3 us -> 7.23 us  [the longest x1 3.72 us: on_device(): lax.all_to_all(spread, 'seq', split_axis=0, concat_axis=0, tiled=True)]
    broadcast_in_dim x16 -> x3, local copies, waits for them, and re-layouts: 27.9 us -> 2.23 us  [the longest x1 1.53 us: on_device(): spread = jnp.broadcast_to(masked[None], (NB, ROWS, WIDTH))]
    all_to_all x8 -> x2, waiting for transfers between devices: 34.3 us -> 14.2 us  [the longest x1 14.2 us: on_device(): lax.all_to_all(spread, 'seq', split_axis=0, concat_axis=0, tiled=True)]
    pallas_call x0 -> x6, Pallas kernels: none -> 15.1 us  [the longest x1 8.34 us: on_device(): call(attention_kernel, 'attention', [((NB, HD, BLK), BF), ((3 * HD, NB *...]
  transfers between devices with their start and end apart: 11 -> 6, of which waited for: 7 -> 3; matrix products, arithmetic and copies ran while one was open for 25% -> 0% of each run, Pallas kernels for 0% -> 8%
where the time goes in v1:
time: 138 us; the launch traced here: 137 us
  blocking collectives  65.1 us (47%)
  starting transfers between devices  25.9 us (19%)
  waiting for transfers between devices  16.1 us (12%)
  Pallas kernels  15.1 us (11%)
  local copies, waits for them, and re-layouts  13.7 us (10%)
    all_to_all x1, blocking collectives, on_device(): lax.all_to_all(pair_sum, 'dp', split_axis=0, concat_axis=0, tiled=True, a...  28.6 us
    all_to_all x1, blocking collectives, on_device(): lax.all_to_all(reduced, 'dp', split_axis=0, concat_axis=0, tiled=True, ax...  18.3 us
    all_to_all x1, blocking collectives, on_device(): x = lax.all_to_all(heads, 'seq', split_axis=0, concat_axis=0, tiled=True)  18.2 us
    all_to_all x1, waiting for transfers between devices, on_device(): lax.all_to_all(spread, 'seq', split_axis=0, concat_axis=0, tiled=True)  14.2 us
    unnamed x26, local copies, waits for them, and re-layouts  11.5 us
    pallas_call x1, Pallas kernels, on_device(): call(attention_kernel, 'attention', [((NB, HD, BLK), BF), ((3 * HD, NB *...  8.34 us
    ppermute x1, starting transfers between devices, on_device(): pair_sum = keep + lax.ppermute(send, 'dp', swap)  7.52 us
    ppermute x1, starting transfers between devices, on_device(): other = lax.ppermute(half, 'dp', swap)  5.6 us
  transfers between devices with their start and end apart: 6, of which 3 were waited for; matrix products, arithmetic and copies ran while one was open for 0% of the time, Pallas kernels for 8%

profile of v1, /device:TPU:1, one launch (start us, length us, event | category | flops | bytes accessed | tf_op | source)
XLA Modules:
  0.0 136.8 jit_solution(13321054707036332061)
XLA Ops:
  2.1 1.0 copy-done
  3.2 1.0 copy-done.1
  4.2 1.0 copy-done.2
  5.3 0.9 copy-done.3
  6.2 0.9 copy-done.4
  10.0 1.4 %rows.1 = (bf16[128,512]{1,0:T(8,128)(2,1)S(1)}, bf16[16,160,128]{2,1,0:T(8,128)(2,1)S(1)}, bf16[2,32,512]{2,1,0:T(8,128)(2,1)S(1)}, f32[128,512]{1,0:T(8,128)S(1)}, f32[128,1]{1,0:T(8,128)S(1)}) custom-call(s32[3]{0:T(128)S(1)} %pad_add_fusion.place_ref, s32[1,2,1]{2,1,0:T(2,128)S(1)} %copy.17.counts_ref, bf16[1,128,512]{2,1,0:T(8,128)(2,1)S(1)} %copy-done.3, ...), custom_call_target="tpu_custom_call" | custom-call | flops 400000000 | bytes 3000000 | tf_op jit(solution)/shard_map/rows/pallas_call | solution.py:261
  11.4 18.2 %all_to_all.25.x_ref = bf16[16,160,128]{2,1,0:T(8,128)(2,1)S(1)} all-to-all(bf16[16,160,128]{2,1,0:T(8,128)(2,1)S(1)} %get-tuple-element.20), channel_id=1, replica_groups=mesh['dp'=32,'seq'=16] {'seq'}, dimensions={0} | all-to-all | bytes 1310720 | tf_op jit(solution)/shard_map/all_to_all | solution.py:279
  29.6 1.5 %broadcast_in_dim.7 = bf16[16,128,512]{2,1,0:T(8,128)(2,1)} broadcast(bf16[128,512]{1,0:T(8,128)(2,1)S(1)} %get-tuple-element.26), dimensions={1,2} | broadcast | bytes 2228224 | tf_op jit(solution)/shard_map/broadcast_in_dim | solution.py:280
  31.2 3.7 %all-to-all-start.2 = ((bf16[16,128,512]{2,1,0:T(8,128)(2,1)}), bf16[16,128,512]{2,1,0:T(8,128)(2,1)S(1)}, u32[]{:S(2)}, u32[]{:S(2)}) async-start(bf16[16,128,512]{2,1,0:T(8,128)(2,1)} %broadcast_in_dim.7), calls=%async_computation.2 | async-start | bytes 4194304 | tf_op jit(solution)/shard_map/all_to_all | solution.py:281
  34.9 1.9 %pair_list.1 = (s32[264]{0:T(512)}, s32[1]{0:T(128)}) custom-call(s32[1,16,16]{2,1,0:T(8,128)} %mask_ref.1), custom_call_target="tpu_custom_call" | custom-call | flops 1000000 | bytes 2000000 | tf_op jit(solution)/shard_map/pair_list/pallas_call | solution.py:286
  37.4 8.3 %attention.1 = (bf16[16,32,128]{2,1,0:T(8,128)(2,1)}, bf16[96,2048]{1,0:T(8,128)(2,1)S(1)}) custom-call(s32[264]{0:T(512)S(1)} %copy-done.10, s32[1]{0:T(128)} %get-tuple-element.19.count_ref, bf16[16,160,128]{2,1,0:T(8,128)(2,1)S(1)} %all_to_all.25.x_ref), custom_call_target="tpu_custom_call" | custom-call | flops 5000000000 | bytes 20000000 | tf_op jit(solution)/shard_map/attention/pallas_call | solution.py:298
  45.8 14.2 %all-to-all-done.2.masked_ref = bf16[16,128,512]{2,1,0:T(8,128)(2,1)S(1)} async-done(((bf16[16,128,512]{2,1,0:T(8,128)(2,1)}), bf16[16,128,512]{2,1,0:T(8,128)(2,1)S(1)}, u32[]{:S(2)}, u32[]{:S(2)}) %all-to-all-start.2) | async-done | bytes 2097184 | tf_op jit(solution)/shard_map/all_to_all | solution.py:281
  59.9 1.1 weights.1
  61.1 7.5 %collective-permute-start.2 = (f32[16,12,128]{2,1,0:T(8,128)S(1)}, f32[16,12,128]{2,1,0:T(8,128)S(1)}, u32[]{:S(2)}, u32[]{:S(2)}) collective-permute-start(f32[16,12,128]{2,1,0:T(8,128)S(1)} %get-tuple-element.28), channel_id=1, source_target_pairs={{0,16},{16,0},{32,48},{48,32},{64,80},{80,64},{96,112},{112,96},{1... | collective-permute-start | bytes 294920 | tf_op jit(solution)/shard_map/ppermute | solution.py:343
  68.6 1.0 collective-permute-done.2
  69.6 28.6 %all_to_all.26 = f32[16,12,128]{2,1,0:T(8,128)S(1)} all-to-all(f32[16,12,128]{2,1,0:T(8,128)S(1)} %add.3), channel_id=1, replica_groups={{0,32,64,96,128,160,192,224,256,288,320,352,384,416,448,480},{16,48,80,..., dimensions={0} | all-to-all | bytes 196608 | tf_op jit(solution)/shard_map/all_to_all | solution.py:344
  98.3 18.3 %all_to_all.27.own_ref = f32[16,12,128]{2,1,0:T(8,128)S(1)} all-to-all(f32[16,12,128]{2,1,0:T(8,128)S(1)} %broadcast_in_dim.8), channel_id=1, replica_groups={{0,32,64,96,128,160,192,224,256,288,320,352,384,416,448,480},{16,48,80,..., dimensions={0} | all-to-all | bytes 196608 | tf_op jit(solution)/shard_map/all_to_all | solution.py:348
  116.5 3.5 %all-to-all-start.1 = ((bf16[16,32,128]{2,1,0:T(8,128)(2,1)}), bf16[16,32,128]{2,1,0:T(8,128)(2,1)S(1)}, u32[]{:S(2)}, u32[]{:S(2)}) async-start(bf16[16,32,128]{2,1,0:T(8,128)(2,1)} %get-tuple-element.21), calls=%async_computation.1 | async-start | bytes 262144 | tf_op jit(solution)/shard_map/all_to_all | solution.py:322
  120.0 5.6 %collective-permute-start.3 = (f32[16,12,128]{2,1,0:T(8,128)S(1)}, f32[16,12,128]{2,1,0:T(8,128)S(1)}, u32[]{:S(2)}, u32[]{:S(2)}) collective-permute-start(f32[16,12,128]{2,1,0:T(8,128)S(1)} %all_to_all.27.own_ref), channel_id=1, source_target_pairs={{0,16},{16,0},{32,48},{48,32},{64,80},{80,64},{96,112},{112,96},{1... | collective-permute-start | bytes 294920 | tf_op jit(solution)/shard_map/ppermute | solution.py:351
  125.7 1.9 %collective-permute-start.1 = (bf16[1,32,512]{2,1,0:T(8,128)(2,1)S(1)}, bf16[1,32,512]{2,1,0:T(8,128)(2,1)S(1)}, u32[]{:S(2)}, u32[]{:S(2)}) collective-permute-start(bf16[1,32,512]{2,1,0:T(8,128)(2,1)S(1)} %get-tuple-element.36), channel_id=1, source_target_pairs={{16,0},{32,16},{48,32},{64,48},{80,64},{96,80},{112,96},{128,112},... | collective-permute-start | bytes 98312 | tf_op jit(solution)/shard_map/ppermute | solution.py:284
  127.6 3.6 %collective-permute-start = (bf16[1,32,512]{2,1,0:T(8,128)(2,1)S(1)}, bf16[1,32,512]{2,1,0:T(8,128)(2,1)S(1)}, u32[]{:S(2)}, u32[]{:S(2)}) collective-permute-start(bf16[1,32,512]{2,1,0:T(8,128)(2,1)S(1)} %get-tuple-element.37), channel_id=1, source_target_pairs={{0,16},{16,32},{32,48},{48,64},{64,80},{80,96},{96,112},{112,128},... | collective-permute-start | bytes 98312 | tf_op jit(solution)/shard_map/ppermute | solution.py:283
  131.3 1.0 collective-permute-done.lower_ref
  132.3 1.4 %mixed.1 = bf16[1,128,512]{2,1,0:T(8,128)(2,1)} custom-call(s32[3]{0:T(128)S(1)} %pad_add_fusion.place_ref, s32[1,2,1]{2,1,0:T(2,128)S(1)} %copy.17.counts_ref, s32[1,2,32]{2,1,0:T(2,128)S(1)} %copy-done.8, bf16[16,32,128]{2,1,0:T(8,128)(2,1)S(1)} %all-to-all-done.1.att_ref, f32[128,512]{1,0:T(8,128)S(1)} %get-tuple-element.22.local_ref, ...), custom_call_target="tpu_custom_call" | custom-call | flops 20000000 | bytes 1000000 | tf_op jit(solution)/shard_map/mixed/pallas_call | solution.py:323
  133.7 0.9 outputs.1
  (30 shorter events, 7.4 us)
Async XLA Ops:
  2.1 1.0 copy-start
  3.2 1.0 copy-start.1
  4.2 1.0 copy-start.2
  5.3 0.9 copy-start.3
  6.2 0.9 copy-start.4
  7.1 0.8 copy-start.5
  7.9 0.7 copy-start.6
  8.6 0.7 copy-start.7
  9.3 0.7 copy-start.9
  31.2 28.8 %all-to-all-start.2 = ((bf16[16,128,512]{2,1,0:T(8,128)(2,1)}), bf16[16,128,512]{2,1,0:T(8,128)(2,1)S(1)}, u32[]{:S(2)}, u32[]{:S(2)}) async-start(bf16[16,128,512]{2,1,0:T(8,128)(2,1)} %broadcast_in_dim.7), calls=%async_computation.2 | async-start | bytes 4194304 | tf_op jit(solution)/shard_map/all_to_all | solution.py:281
  36.8 0.7 copy-start.10
  45.8 86.5 %copy-start.8 = (s32[1,2,32]{2,1,0:T(2,128)S(1)}, s32[1,2,32]{2,1,0:T(2,128)}, u32[]{:S(2)}) copy-start(s32[1,2,32]{2,1,0:T(2,128)} %targets_ref.3) | copy-start | bytes 772
  61.1 8.5 %collective-permute-start.2 = (f32[16,12,128]{2,1,0:T(8,128)S(1)}, f32[16,12,128]{2,1,0:T(8,128)S(1)}, u32[]{:S(2)}, u32[]{:S(2)}) collective-permute-start(f32[16,12,128]{2,1,0:T(8,128)S(1)} %get-tuple-element.28), channel_id=1, source_target_pairs={{0,16},{16,0},{32,48},{48,32},{64,80},{80,64},{96,112},{112,96},{1... | collective-permute-start | bytes 294920 | tf_op jit(solution)/shard_map/ppermute | solution.py:343
  116.5 15.7 %all-to-all-start.1 = ((bf16[16,32,128]{2,1,0:T(8,128)(2,1)}), bf16[16,32,128]{2,1,0:T(8,128)(2,1)S(1)}, u32[]{:S(2)}, u32[]{:S(2)}) async-start(bf16[16,32,128]{2,1,0:T(8,128)(2,1)} %get-tuple-element.21), calls=%async_computation.1 | async-start | bytes 262144 | tf_op jit(solution)/shard_map/all_to_all | solution.py:322
  120.0 13.6 %collective-permute-start.3 = (f32[16,12,128]{2,1,0:T(8,128)S(1)}, f32[16,12,128]{2,1,0:T(8,128)S(1)}, u32[]{:S(2)}, u32[]{:S(2)}) collective-permute-start(f32[16,12,128]{2,1,0:T(8,128)S(1)} %all_to_all.27.own_ref), channel_id=1, source_target_pairs={{0,16},{16,0},{32,48},{48,32},{64,80},{80,64},{96,112},{112,96},{1... | collective-permute-start | bytes 294920 | tf_op jit(solution)/shard_map/ppermute | solution.py:351
  125.7 5.6 %collective-permute-start.1 = (bf16[1,32,512]{2,1,0:T(8,128)(2,1)S(1)}, bf16[1,32,512]{2,1,0:T(8,128)(2,1)S(1)}, u32[]{:S(2)}, u32[]{:S(2)}) collective-permute-start(bf16[1,32,512]{2,1,0:T(8,128)(2,1)S(1)} %get-tuple-element.36), channel_id=1, source_target_pairs={{16,0},{32,16},{48,32},{64,48},{80,64},{96,80},{112,96},{128,112},... | collective-permute-start | bytes 98312 | tf_op jit(solution)/shard_map/ppermute | solution.py:284
  127.6 4.7 %collective-permute-start = (bf16[1,32,512]{2,1,0:T(8,128)(2,1)S(1)}, bf16[1,32,512]{2,1,0:T(8,128)(2,1)S(1)}, u32[]{:S(2)}, u32[]{:S(2)}) collective-permute-start(bf16[1,32,512]{2,1,0:T(8,128)(2,1)S(1)} %get-tuple-element.37), channel_id=1, source_target_pairs={{0,16},{16,32},{32,48},{48,64},{64,80},{80,96},{96,112},{112,128},... | collective-permute-start | bytes 98312 | tf_op jit(solution)/shard_map/ppermute | solution.py:283

commit v2 on v1

--- a/solution.py
+++ b/solution.py
@@ -26,42 +26,62 @@
 VM = pl.BlockSpec(memory_space=pltpu.VMEM)
 
 
-def attach(targets, counts_ref, place_ref, side):
+def attach(targets, counts, side):
     slots = targets.shape[1]
     rows = lax.broadcasted_iota(jnp.int32, (ROWS, slots), 0)
     slot = lax.broadcasted_iota(jnp.int32, (ROWS, slots), 1)
-    inside = (place_ref[0] > 0) if side == 0 else (place_ref[0] < place_ref[2] - 1)
-    limit = jnp.where(inside, counts_ref[0, side, 0], 0)
+    place = lax.axis_index("dp")
+    inside = (place > 0) if side == 0 else (place < lax.axis_size("dp") - 1)
+    limit = jnp.where(inside, counts, 0)
     return jnp.where((targets == rows) & (slot < limit), 1.0, 0.0)
 
 
-def rows_kernel(
-    place_ref, counts_ref, tokens_ref, token_ref, wq_ref, wk_ref, wv_ref, ids_ref, links_ref,
-    sends_ref, targets_ref, grad_ref, masked_ref, heads_ref, out_ref, local_ref, degree_ref,
-):
-    own = place_ref[1] * ROWS + lax.broadcasted_iota(jnp.int32, (ROWS, 128), 0)
+def rows_kernel(*refs):
+    sources, refs = refs[:11], refs[11:]
+    masked_ref, heads_ref, lower_ref, upper_ref, local_ref, degree_ref, pick_ref = refs[:7]
+    holds, sems = refs[7:18], refs[18]
+    copies = [
+        pltpu.make_async_copy(source, hold, sems.at[n])
+        for n, (source, hold) in enumerate(zip(sources, holds))
+    ]
+    for copy in copies:
+        copy.start()
+    (
+        ids_ref, counts_ref, token_ref, tokens_ref, wv_ref, links_ref, sends_ref, targets_ref,
+        grad_ref, wk_ref, wq_ref,
+    ) = holds
+    for copy in copies[:5]:
+        copy.wait()
+    own = lax.axis_index("seq") * ROWS + lax.broadcasted_iota(jnp.int32, (ROWS, 128), 0)
     hit = own < 0
     for part in range(ids_ref.shape[1] // 128):
         hit = hit | (own == ids_ref[:, part * 128 : (part + 1) * 128])
     marked = jnp.max(jnp.where(hit, 1.0, 0.0), axis=1, keepdims=True) > 0
-    masked = jnp.where(marked, token_ref[...].astype(F32), tokens_ref[0].astype(F32)).astype(BF)
-    masked_ref[...] = masked
-
-    links_low = links_ref[0].astype(F32).astype(BF)
+    masked = jnp.where(marked, token_ref[...].reshape(1, WIDTH).astype(F32), tokens_ref[0].astype(F32)).astype(BF)
+    for lane in range(4):
+        masked_ref[lane * 128 : (lane + 1) * 128, :] = masked[:, lane * 128 : (lane + 1) * 128]
+
     value_wide = jnp.dot(masked, wv_ref[...], preferred_element_type=F32)
     value = value_wide.astype(BF)
+    for copy in copies[5:]:
+        copy.wait()
+    links_low = links_ref[0].astype(F32).astype(BF)
     local_ref[...] = value.astype(F32) + jnp.dot(links_low, value, preferred_element_type=F32)
-    pick = lax.broadcasted_iota(jnp.int32, (ROWS, 32), 0)
-    for side in range(2):
-        onehot = jnp.where(sends_ref[0, side : side + 1, :] == pick, 1.0, 0.0).astype(BF)
-        out_ref[side] = lax.dot_general(
+    slots = sends_ref.shape[2]
+    rows = lax.broadcasted_iota(jnp.int32, (ROWS, slots), 0)
+    for side, ref in ((0, lower_ref), (1, upper_ref)):
+        onehot = jnp.where(sends_ref[0, side : side + 1, :] == rows, 1.0, 0.0).astype(BF)
+        ref[0] = lax.dot_general(
             onehot, value, (((0,), (0,)), ((), ())), preferred_element_type=F32
         ).astype(BF)
 
     degree = 1.0 + jnp.sum(links_ref[0].astype(F32), axis=1, keepdims=True)
     for side in range(2):
-        links_here = attach(targets_ref[0, side : side + 1, :], counts_ref, place_ref, side)
-        degree = degree + jnp.sum(links_here, axis=1, keepdims=True)
+        here = attach(
+            targets_ref[0, side : side + 1, :], counts_ref[0, :, side : side + 1], side
+        )
+        pick_ref[:, side * slots : (side + 1) * slots] = here.astype(BF)
+        degree = degree + jnp.sum(here, axis=1, keepdims=True)
     degree_ref[...] = degree
 
     scaled = (grad_ref[0].astype(F32) / degree).T
@@ -83,24 +103,18 @@
             heads_ref[head, place * HD : (place + 1) * HD, :] = item[head * HD : (head + 1) * HD]
 
 
-def list_kernel(mask_ref, list_ref, count_ref):
-    def row(i, n):
-        for j in range(NB):
-            list_ref[n] = i * NB + j
-            n = n + mask_ref[0, i, j]
-        return n
-
-    n = lax.fori_loop(0, NB, row, jnp.int32(0))
-    for u in range(UNROLL):
-        list_ref[n + u] = NB * NB
-    count_ref[0] = n
-
-
 def attention_kernel(
-    list_ref, count_ref, x_ref, att_ref, grad_ref, keys, duo, expo, gprob, peak, top, total, inner,
+    mask_ref, x_ref, masked_ref, back_ref, grad_ref, list_ref, keys, duo, expo, gprob, peak, top, total, inner,
     out_acc, q_acc, k_acc, v_acc,
 ):
-    steps = lax.div(count_ref[0] + (UNROLL - 1), jnp.int32(UNROLL))
+    count = jnp.int32(0)
+    for i in range(NB):
+        for j in range(NB):
+            list_ref[count] = i * NB + j
+            count = count + mask_ref[0, i, j]
+    for u in range(UNROLL):
+        list_ref[count + u] = NB * NB
+    steps = lax.div(count + (UNROLL - 1), jnp.int32(UNROLL))
     duo[...] = jnp.zeros_like(duo)
     k_acc[...] = jnp.zeros_like(k_acc)
     v_acc[...] = jnp.zeros_like(v_acc)
@@ -174,7 +188,8 @@
 
     for b in range(NB):
         cols = slice(b * BLK, (b + 1) * BLK)
-        att_ref[b] = out_acc[b].astype(BF)
+        back_ref[b, 0:WIDTH, :] = masked_ref[...]
+        back_ref[b, WIDTH : WIDTH + HD, :] = out_acc[b].astype(BF)
         grad_ref[0:32, cols] = q_acc[b].astype(BF)
         grad_ref[32:64, cols] = k_acc[b].astype(BF)
         grad_ref[64:96, cols] = (
@@ -182,56 +197,49 @@
         ).astype(BF)
 
 
-def weights_kernel(place_ref, grad_ref, masked_ref, keep_ref, send_ref):
-    core = lax.bitwise_and(place_ref[0], 1)
-    both = jnp.dot(
-        grad_ref[...], masked_ref[...].reshape(NB * ROWS, WIDTH), preferred_element_type=F32
-    )
-    for half, first in ((0, True), (1, False)):
-        for lane in range(2):
-            for r in range(8):
-                piece = both[
-                    r * CHUNK : (r + 1) * CHUNK,
-                    (half * 2 + lane) * 128 : (half * 2 + lane + 1) * 128,
-                ]
-                slot = lane * 8 + r
-
-                @pl.when(core == half)
-                def _():
-                    keep_ref[slot] = piece
-
-                @pl.when(core != half)
-                def _():
-                    send_ref[slot] = piece
-
-
-def output_kernel(place_ref, own_ref, other_ref, q_ref, k_ref, v_ref, full):
-    core = lax.bitwise_and(place_ref[0], 1)
-    for half in range(2):
-        mine = core == half
-        for lane in range(2):
-            for r in range(8):
-                slot = lane * 8 + r
-                full[
-                    r * CHUNK : (r + 1) * CHUNK,
-                    (half * 2 + lane) * 128 : (half * 2 + lane + 1) * 128,
-                ] = jnp.where(mine, own_ref[slot], other_ref[slot])
-    for lane in range(4):
-        block = full[:, lane * 128 : (lane + 1) * 128].T
-        for place, ref in enumerate((q_ref, k_ref, v_ref)):
-            ref[lane * 128 : (lane + 1) * 128, :] = block[:, place * HD : (place + 1) * HD]
-
-
-def mixed_kernel(
-    place_ref, counts_ref, targets_ref, att_ref, local_ref, degree_ref, lower_ref, upper_ref,
-    mixed_ref,
-):
-    border = jnp.zeros((ROWS, WIDTH), F32)
-    for side, ref in ((0, lower_ref), (1, upper_ref)):
-        here = attach(targets_ref[0, side : side + 1, :], counts_ref, place_ref, side)
-        border = border + jnp.dot(here.astype(BF), ref[0], preferred_element_type=F32)
+def weights_kernel(grad_ref, masked_ref, keep_ref, send_ref, att_ref):
+    core = lax.bitwise_and(lax.axis_index("dp"), 1)
+    masked = jnp.concatenate(
+        [
+            jnp.concatenate(
+                [masked_ref[b, lane * 128 : (lane + 1) * 128, :] for b in range(NB)], axis=0
+            )
+            for lane in range(4)
+        ],
+        axis=1,
+    )
+    both = jnp.dot(grad_ref[...], masked, preferred_element_type=F32)
+    for head in range(HEADS):
+        att_ref[head * HD : (head + 1) * HD, :] = masked_ref[head, WIDTH : WIDTH + HD, :]
+    own_low = core == 0
+    for lane in range(2):
+        low = both[:, lane * 128 : (lane + 1) * 128]
+        high = both[:, (lane + 2) * 128 : (lane + 3) * 128]
+        keep = jnp.where(own_low, low, high)
+        send = jnp.where(own_low, high, low)
+        for r in range(8):
+            keep_ref[lane * 8 + r] = keep[r * CHUNK : (r + 1) * CHUNK]
+            send_ref[lane * 8 + r] = send[r * CHUNK : (r + 1) * CHUNK]
+
+
+def output_kernel(own_ref, other_ref, q_ref, k_ref, v_ref, full):
+    own_low = lax.bitwise_and(lax.axis_index("dp"), 1) == 0
+    for lane in range(2):
+        for r in range(8):
+            own = own_ref[lane * 8 + r]
+            other = other_ref[lane * 8 + r]
+            rows = slice(r * CHUNK, (r + 1) * CHUNK)
+            full[rows, lane * 128 : (lane + 1) * 128] = jnp.where(own_low, own, other)
+            full[rows, (lane + 2) * 128 : (lane + 3) * 128] = jnp.where(own_low, other, own)
+    for place, ref in enumerate((q_ref, k_ref, v_ref)):
+        ref[...] = full[place * HD : (place + 1) * HD, :]
+
+
+def mixed_kernel(pick_ref, att_ref, local_ref, degree_ref, lower_ref, upper_ref, mixed_ref):
+    rows = jnp.concatenate([lower_ref[0], upper_ref[0]], axis=0)
+    border = jnp.dot(pick_ref[...], rows, preferred_element_type=F32)
     graph = (local_ref[...] + border) / degree_ref[...]
-    attended = att_ref[...].reshape(WIDTH, ROWS).astype(F32).T
+    attended = att_ref[...].astype(F32).T
     mixed_ref[0] = (attended + graph).astype(BF)
 
 
@@ -254,53 +262,42 @@
     boundary_counts, boundary_targets, grad_out,
 ):
     clusters = lax.axis_size("dp")
-    place = jnp.stack(
-        [lax.axis_index("dp"), lax.axis_index("seq"), jnp.int32(clusters)]
-    ).astype(jnp.int32)
-
-    masked, heads, outgoing, local, degree = call(
+    slots = boundary_ids.shape[2]
+    sources = (
+        masked_ids, boundary_counts.transpose(0, 2, 1), mask_token, features, w_value,
+        adjacency, boundary_ids, boundary_targets, grad_out, w_key, w_query,
+    )
+    masked, heads, send_lower, send_upper, local, degree, pick = call(
         rows_kernel,
         "rows",
         [
-            ((ROWS, WIDTH), BF),
+            ((WIDTH, ROWS), BF),
             ((HEADS, 5 * HD, ROWS), BF),
-            ((2, 32, WIDTH), BF),
+            ((1, slots, WIDTH), BF),
+            ((1, slots, WIDTH), BF),
             ((ROWS, WIDTH), F32),
             ((ROWS, 1), F32),
+            ((ROWS, 2 * slots), BF),
         ],
-        [SM, SM] + [VM] * 10,
+        [pl.BlockSpec(memory_space=pltpu.HBM)] * len(sources),
+        scratch=[pltpu.VMEM(item.shape, item.dtype) for item in sources]
+        + [pltpu.SemaphoreType.DMA((len(sources),))],
         flops=400_000_000,
         moved=3_000_000,
-    )(
-        place, boundary_counts, features, mask_token[None], w_query, w_key, w_value, masked_ids,
-        adjacency, boundary_ids, boundary_targets, grad_out,
-    )
+    )(*[pltpu.with_memory_space_constraint(item, pltpu.HBM) for item in sources])
 
     x = lax.all_to_all(heads, "seq", split_axis=0, concat_axis=0, tiled=True)
-    spread = jnp.broadcast_to(masked[None], (NB, ROWS, WIDTH))
-    masked_all = lax.all_to_all(spread, "seq", split_axis=0, concat_axis=0, tiled=True)
     up = [(c, c + 1) for c in range(clusters - 1)]
-    lower = lax.ppermute(outgoing[0:1], "dp", up)
-    upper = lax.ppermute(outgoing[1:2], "dp", [(b, a) for a, b in up])
-
-    pairs, count = pl.pallas_call(
-        list_kernel,
-        out_shape=(
-            jax.ShapeDtypeStruct((SLOTS + 4,), jnp.int32),
-            jax.ShapeDtypeStruct((1,), jnp.int32),
-        ),
-        in_specs=[SM],
-        out_specs=(SM, SM),
-        cost_estimate=pl.CostEstimate(flops=1_000_000, bytes_accessed=2_000_000, transcendentals=0),
-        name="pair_list",
-    )(block_mask)
-
-    attended, grads = call(
+    lower = lax.ppermute(send_lower, "dp", up)
+    upper = lax.ppermute(send_upper, "dp", [(b, a) for a, b in up])
+
+    back, grads = call(
         attention_kernel,
         "attention",
-        [((NB, HD, BLK), BF), ((3 * HD, NB * BLK), BF)],
-        [SM, SM, VM],
+        [((NB, WIDTH + HD, BLK), BF), ((3 * HD, NB * BLK), BF)],
+        [SM, VM, VM],
         scratch=[
+            pltpu.SMEM((SLOTS + UNROLL,), jnp.int32),
             pltpu.VMEM((NB, BLK, 2 * HD), BF),
             pltpu.VMEM((NB + 1, 2 * HD, 2 * BLK), BF),
             pltpu.VMEM((SLOTS, BLK, BLK), F32),
@@ -317,26 +314,25 @@
         limit=48,
         flops=5_000_000_000,
         moved=20_000_000,
-    )(pairs, count, x)
-
-    back = lax.all_to_all(attended, "seq", split_axis=0, concat_axis=0, tiled=True)
+    )(block_mask, x, masked)
+
+    back = lax.all_to_all(back, "seq", split_axis=0, concat_axis=0, tiled=True)
+    keep, send, attended = call(
+        weights_kernel,
+        "weights",
+        [((CHIPS, CHUNK, 128), F32), ((CHIPS, CHUNK, 128), F32), ((WIDTH, ROWS), BF)],
+        [VM, VM],
+        flops=200_000_000,
+        moved=3_000_000,
+    )(grads, back)
     (mixed,) = call(
         mixed_kernel,
         "mixed",
         [((1, ROWS, WIDTH), BF)],
-        [SM, SM] + [VM] * 6,
+        [VM] * 6,
         flops=20_000_000,
         moved=1_000_000,
-    )(place, boundary_counts, boundary_targets, back, local, degree, lower, upper)
-
-    keep, send = call(
-        weights_kernel,
-        "weights",
-        [((CHIPS, CHUNK, 128), F32), ((CHIPS, CHUNK, 128), F32)],
-        [SM, VM, VM],
-        flops=200_000_000,
-        moved=3_000_000,
-    )(place, grads, masked_all)
+    )(pick, attended, local, degree, lower, upper)
 
     swap = [(c, c ^ 1) for c in range(clusters)]
     groups = [[chip * 2 + core for chip in range(clusters // 2)] for core in range(2)]
@@ -352,13 +348,13 @@
     grad_query, grad_key, grad_value = call(
         output_kernel,
         "outputs",
-        [((WIDTH, HD), F32)] * 3,
-        [SM, VM, VM],
+        [((HD, WIDTH), F32)] * 3,
+        [VM, VM],
         scratch=[pltpu.VMEM((3 * HD, WIDTH), F32)],
         flops=1_000_000,
         moved=1_000_000,
-    )(place, half, other)
-    return mixed, grad_query, grad_key, grad_value
+    )(half, other)
+    return mixed, grad_query.T, grad_key.T, grad_value.T
 
 
 def solution(mesh):

time: 138 us -> 129 us (0.935)
  blocking collectives: 65.1 us -> 94.8 us
  local copies, waits for them, and re-layouts: 13.7 us -> 0.02 us
  waiting for transfers between devices: 16.1 us -> 4.26 us
  starting transfers between devices: 25.9 us -> 15.8 us
  Pallas kernels: 15.1 us -> 12.6 us
    all_to_all x0 -> x1, blocking collectives: none -> 31.8 us  [on_device(): back = lax.all_to_all(back, 'seq', split_axis=0, concat_axis=0, tiled=True)]
    all_to_all x2 -> x0, waiting for transfers between devices: 14.2 us -> none  [the longest x1 14.2 us: on_device(): lax.all_to_all(spread, 'seq', split_axis=0, concat_axis=0, tiled=True)]
    unnamed x26 -> x2, local copies, waits for them, and re-layouts: 11.5 us -> 0.01 us
    all_to_all x2 -> x0, starting transfers between devices: 7.23 us -> none  [the longest x1 3.72 us: on_device(): lax.all_to_all(spread, 'seq', split_axis=0, concat_axis=0, tiled=True)]
    ppermute x1, starting transfers between devices: 7.52 us -> 5.16 us  [on_device(): pair_sum = keep + lax.ppermute(send, 'dp', swap)]
    ppermute x2, waiting for transfers between devices: 0.99 us -> 3.3 us  [the longest x1 3.29 us: on_device(): upper = lax.ppermute(send_upper, 'dp', [(b, a) for a, b in up])]
    broadcast_in_dim x2 -> x0, local copies, waits for them, and re-layouts: 2.21 us -> none  [the longest x1 1.53 us: on_device(): spread = jnp.broadcast_to(masked[None], (NB, ROWS, WIDTH))]
    all_to_all x1, blocking collectives: 28.6 us -> 26.5 us  [on_device(): lax.all_to_all(pair_sum, 'dp', split_axis=0, concat_axis=0, tiled=True, a...]
  transfers between devices with their start and end apart: 6 -> 4, of which waited for: 3 -> 2; matrix products, arithmetic and copies ran while one was open for 0% -> 0% of each run, Pallas kernels for 8% -> 1%
where the time goes in v2:
time: 129 us; the launch traced here: 128 us
  blocking collectives  94.8 us (73%)
  starting transfers between devices  15.8 us (12%)
  Pallas kernels  12.6 us (10%)
  waiting for transfers between devices  4.26 us (3%)
    all_to_all x1, blocking collectives, on_device(): back = lax.all_to_all(back, 'seq', split_axis=0, concat_axis=0, tiled=True)  31.8 us
    all_to_all x1, blocking collectives, on_device(): lax.all_to_all(pair_sum, 'dp', split_axis=0, concat_axis=0, tiled=True, a...  26.5 us
    all_to_all x1, blocking collectives, on_device(): lax.all_to_all(reduced, 'dp', split_axis=0, concat_axis=0, tiled=True, ax...  18.3 us
    all_to_all x1, blocking collectives, on_device(): x = lax.all_to_all(heads, 'seq', split_axis=0, concat_axis=0, tiled=True)  18.2 us
    pallas_call x1, Pallas kernels, on_device(): call(attention_kernel, 'attention', [((NB, WIDTH + HD, BLK), BF), ((3 * H...  8.18 us
    ppermute x1, starting transfers between devices, on_device(): other = lax.ppermute(half, 'dp', swap)  5.59 us
    ppermute x1, starting transfers between devices, on_device(): pair_sum = keep + lax.ppermute(send, 'dp', swap)  5.16 us
    ppermute x1, waiting for transfers between devices, on_device(): upper = lax.ppermute(send_upper, 'dp', [(b, a) for a, b in up])  3.29 us
  transfers between devices with their start and end apart: 4, of which 2 were waited for; matrix products, arithmetic and copies ran while one was open for 0% of the time, Pallas kernels for 1%

profile of v2, /device:TPU:1, one launch (start us, length us, event | category | flops | bytes accessed | tf_op | source)
XLA Modules:
  0.0 128.2 jit_solution(3504588254742799309)
XLA Ops:
  0.6 0.0 copy-start
  0.6 2.5 %rows.1 = (bf16[512,128]{1,0:T(8,128)(2,1)S(1)}, bf16[16,160,128]{2,1,0:T(8,128)(2,1)S(1)}, bf16[1,32,512]{2,1,0:T(8,128)(2,1)S(1)}, bf16[1,32,512]{2,1,0:T(8,12...) custom-call(s32[1,1024]{1,0:T(1,128)} %refs_0_.1, s32[1,1,2]{2,1,0:T(1,128)} %bitcast.4, ...), custom_call_target="tpu_custom_call" | custom-call | flops 400000000 | bytes 3000000 | tf_op jit(solution)/shard_map/rows/pallas_call | solution.py:270
  3.1 18.2 %all_to_all.20.x_ref = bf16[16,160,128]{2,1,0:T(8,128)(2,1)S(1)} all-to-all(bf16[16,160,128]{2,1,0:T(8,128)(2,1)S(1)} %get-tuple-element.20), channel_id=1, replica_groups=mesh['dp'=32,'seq'=16] {'seq'}, dimensions={0} | all-to-all | bytes 1310720 | tf_op jit(solution)/shard_map/all_to_all | solution.py:289
  21.3 0.0 copy-done
  21.3 8.2 %attention.1 = (bf16[16,544,128]{2,1,0:T(8,128)(2,1)S(1)}, bf16[96,2048]{1,0:T(8,128)(2,1)S(1)}) custom-call(s32[1,16,16]{2,1,0:T(8,128)S(1)} %copy-done, bf16[16,160,128]{2,1,0:T(8,128)(2,1)S(1)} %all_to_all.20.x_ref, bf16[512,128]{1,0:T(8,128)(2,1)S(1)} %get-tuple-element.21.masked_ref), custom_call_target="tpu_custom_call" | custom-call | flops 5000000000 | bytes 20000000 | tf_op jit(solution)/shard_map/attention/pallas_call | solution.py:294
  29.5 31.8 %all_to_all.21.masked_ref = bf16[16,544,128]{2,1,0:T(8,128)(2,1)S(1)} all-to-all(bf16[16,544,128]{2,1,0:T(8,128)(2,1)S(1)} %get-tuple-element.23), channel_id=1, replica_groups=mesh['dp'=32,'seq'=16] {'seq'}, dimensions={0} | all-to-all | bytes 4456448 | tf_op jit(solution)/shard_map/all_to_all | solution.py:319
  61.3 0.5 weights.1
  61.8 5.2 %collective-permute-start.2 = (f32[16,12,128]{2,1,0:T(8,128)S(1)}, f32[16,12,128]{2,1,0:T(8,128)S(1)}, u32[]{:S(2)}, u32[]{:S(2)}) collective-permute-start(f32[16,12,128]{2,1,0:T(8,128)S(1)} %get-tuple-element.30), channel_id=1, source_target_pairs={{0,16},{16,0},{32,48},{48,32},{64,80},{80,64},{96,112},{112,96},{1... | collective-permute-start | bytes 294920 | tf_op jit(solution)/shard_map/ppermute | solution.py:339
  67.0 1.0 collective-permute-done.2
  68.0 26.5 %all_to_all.22 = f32[16,12,128]{2,1,0:T(8,128)S(1)} all-to-all(f32[16,12,128]{2,1,0:T(8,128)S(1)} %add.3), channel_id=1, replica_groups={{0,32,64,96,128,160,192,224,256,288,320,352,384,416,448,480},{16,48,80,..., dimensions={0} | all-to-all | bytes 196608 | tf_op jit(solution)/shard_map/all_to_all | solution.py:340
  94.5 18.3 %all_to_all.23.own_ref = f32[16,12,128]{2,1,0:T(8,128)S(1)} all-to-all(f32[16,12,128]{2,1,0:T(8,128)S(1)} %broadcast_in_dim.2), channel_id=1, replica_groups={{0,32,64,96,128,160,192,224,256,288,320,352,384,416,448,480},{16,48,80,..., dimensions={0} | all-to-all | bytes 196608 | tf_op jit(solution)/shard_map/all_to_all | solution.py:344
  112.8 5.6 %collective-permute-start.3 = (f32[16,12,128]{2,1,0:T(8,128)S(1)}, f32[16,12,128]{2,1,0:T(8,128)S(1)}, u32[]{:S(2)}, u32[]{:S(2)}) collective-permute-start(f32[16,12,128]{2,1,0:T(8,128)S(1)} %all_to_all.23.own_ref), channel_id=1, source_target_pairs={{0,16},{16,0},{32,48},{48,32},{64,80},{80,64},{96,112},{112,96},{1... | collective-permute-start | bytes 294920 | tf_op jit(solution)/shard_map/ppermute | solution.py:347
  118.4 3.1 %collective-permute-start = (bf16[1,32,512]{2,1,0:T(8,128)(2,1)S(1)}, bf16[1,32,512]{2,1,0:T(8,128)(2,1)S(1)}, u32[]{:S(2)}, u32[]{:S(2)}) collective-permute-start(bf16[1,32,512]{2,1,0:T(8,128)(2,1)S(1)} %get-tuple-element.27), channel_id=1, source_target_pairs={{0,16},{16,32},{32,48},{48,64},{64,80},{80,96},{96,112},{112,128},... | collective-permute-start | bytes 98312 | tf_op jit(solution)/shard_map/ppermute | solution.py:291
  121.5 1.9 %collective-permute-start.1 = (bf16[1,32,512]{2,1,0:T(8,128)(2,1)S(1)}, bf16[1,32,512]{2,1,0:T(8,128)(2,1)S(1)}, u32[]{:S(2)}, u32[]{:S(2)}) collective-permute-start(bf16[1,32,512]{2,1,0:T(8,128)(2,1)S(1)} %get-tuple-element.28), channel_id=1, source_target_pairs={{16,0},{32,16},{48,32},{64,48},{80,64},{96,80},{112,96},{128,112},... | collective-permute-start | bytes 98312 | tf_op jit(solution)/shard_map/ppermute | solution.py:292
  123.4 0.0 collective-permute-done.lower_ref
  123.4 3.3 %collective-permute-done.1.upper_ref = bf16[1,32,512]{2,1,0:T(8,128)(2,1)S(1)} collective-permute-done((bf16[1,32,512]{2,1,0:T(8,128)(2,1)S(1)}, bf16[1,32,512]{2,1,0:T(8,128)(2,1)S(1)}, u32[]{:S(2)}, u32[]{:S(2)}) %collective-permute-start.1) | collective-permute-done | bytes 32800 | tf_op jit(solution)/shard_map/ppermute | solution.py:292
  126.7 0.8 mixed.1
  127.5 0.0 collective-permute-done.3.other_ref
  127.5 0.7 outputs.1
  (3 shorter events, 0.1 us)
Async XLA Ops:
  0.6 20.7 %copy-start = (s32[1,16,16]{2,1,0:T(8,128)S(1)}, s32[1,16,16]{2,1,0:T(8,128)}, u32[]{:S(2)}) copy-start(s32[1,16,16]{2,1,0:T(8,128)} %mask_ref.1) | copy-start | bytes 3076
  61.8 6.1 %collective-permute-start.2 = (f32[16,12,128]{2,1,0:T(8,128)S(1)}, f32[16,12,128]{2,1,0:T(8,128)S(1)}, u32[]{:S(2)}, u32[]{:S(2)}) collective-permute-start(f32[16,12,128]{2,1,0:T(8,128)S(1)} %get-tuple-element.30), channel_id=1, source_target_pairs={{0,16},{16,0},{32,48},{48,32},{64,80},{80,64},{96,112},{112,96},{1... | collective-permute-start | bytes 294920 | tf_op jit(solution)/shard_map/ppermute | solution.py:339
  112.8 14.8 %collective-permute-start.3 = (f32[16,12,128]{2,1,0:T(8,128)S(1)}, f32[16,12,128]{2,1,0:T(8,128)S(1)}, u32[]{:S(2)}, u32[]{:S(2)}) collective-permute-start(f32[16,12,128]{2,1,0:T(8,128)S(1)} %all_to_all.23.own_ref), channel_id=1, source_target_pairs={{0,16},{16,0},{32,48},{48,32},{64,80},{80,64},{96,112},{112,96},{1... | collective-permute-start | bytes 294920 | tf_op jit(solution)/shard_map/ppermute | solution.py:347
  118.4 5.0 %collective-permute-start = (bf16[1,32,512]{2,1,0:T(8,128)(2,1)S(1)}, bf16[1,32,512]{2,1,0:T(8,128)(2,1)S(1)}, u32[]{:S(2)}, u32[]{:S(2)}) collective-permute-start(bf16[1,32,512]{2,1,0:T(8,128)(2,1)S(1)} %get-tuple-element.27), channel_id=1, source_target_pairs={{0,16},{16,32},{32,48},{48,64},{64,80},{80,96},{96,112},{112,128},... | collective-permute-start | bytes 98312 | tf_op jit(solution)/shard_map/ppermute | solution.py:291
  121.5 5.2 %collective-permute-start.1 = (bf16[1,32,512]{2,1,0:T(8,128)(2,1)S(1)}, bf16[1,32,512]{2,1,0:T(8,128)(2,1)S(1)}, u32[]{:S(2)}, u32[]{:S(2)}) collective-permute-start(bf16[1,32,512]{2,1,0:T(8,128)(2,1)S(1)} %get-tuple-element.28), channel_id=1, source_target_pairs={{16,0},{32,16},{48,32},{64,48},{80,64},{96,80},{112,96},{128,112},... | collective-permute-start | bytes 98312 | tf_op jit(solution)/shard_map/ppermute | solution.py:292

commit v3 on v2

--- a/solution.py
+++ b/solution.py
@@ -11,7 +11,7 @@
 HD = 32
 ROWS = 128
 WIDTH = 512
-UNROLL = 4
+UNROLL = 16
 SLOTS = NB * NB + UNROLL
 SCALE = HD**-0.5
 LOG2E = 1.4426950408889634
@@ -19,11 +19,16 @@
 LOWEST = -3e38
 BF = jnp.bfloat16
 F32 = jnp.float32
-CHIPS = 16
-CHUNK = 12
+NEAR = 4
+CHUNK = 48
 
 SM = pl.BlockSpec(memory_space=pltpu.SMEM)
 VM = pl.BlockSpec(memory_space=pltpu.VMEM)
+ANY = pl.BlockSpec(memory_space=pl.ANY)
+
+
+def group_of(place):
+    return (place // 4 % 2) * 2 + place % 2
 
 
 def attach(targets, counts, side):
@@ -38,8 +43,8 @@
 
 def rows_kernel(*refs):
     sources, refs = refs[:11], refs[11:]
-    masked_ref, heads_ref, lower_ref, upper_ref, local_ref, degree_ref, pick_ref = refs[:7]
-    holds, sems = refs[7:18], refs[18]
+    heads_ref, lower_ref, upper_ref, local_ref, degree_ref, pick_ref = refs[:6]
+    holds, sems = refs[6:17], refs[17]
     copies = [
         pltpu.make_async_copy(source, hold, sems.at[n])
         for n, (source, hold) in enumerate(zip(sources, holds))
@@ -58,8 +63,9 @@
         hit = hit | (own == ids_ref[:, part * 128 : (part + 1) * 128])
     marked = jnp.max(jnp.where(hit, 1.0, 0.0), axis=1, keepdims=True) > 0
     masked = jnp.where(marked, token_ref[...].reshape(1, WIDTH).astype(F32), tokens_ref[0].astype(F32)).astype(BF)
-    for lane in range(4):
-        masked_ref[lane * 128 : (lane + 1) * 128, :] = masked[:, lane * 128 : (lane + 1) * 128]
+    for head in range(HEADS):
+        group = group_of(head)
+        heads_ref[head, 0:BLK, :] = masked[:, group * 128 : (group + 1) * 128]
 
     value_wide = jnp.dot(masked, wv_ref[...], preferred_element_type=F32)
     value = value_wide.astype(BF)
@@ -100,11 +106,17 @@
     grad_t = grad_ref[0].astype(F32).T.astype(BF)
     for place, item in enumerate((key, value_t, query, grad_t, graph_grad)):
         for head in range(HEADS):
-            heads_ref[head, place * HD : (place + 1) * HD, :] = item[head * HD : (head + 1) * HD]
+            heads_ref[head, BLK + place * HD : BLK + (place + 1) * HD, :] = item[
+                head * HD : (head + 1) * HD
+            ]
+
+
+def columns_kernel(graph_ref, x_ref, columns_ref):
+    columns_ref[...] = x_ref[:, 0:BLK, :]
 
 
 def attention_kernel(
-    mask_ref, x_ref, masked_ref, back_ref, grad_ref, list_ref, keys, duo, expo, gprob, peak, top, total, inner,
+    mask_ref, x_ref, back_ref, grad_ref, list_ref, keys, duo, expo, gprob, peak, top, total, inner,
     out_acc, q_acc, k_acc, v_acc,
 ):
     count = jnp.int32(0)
@@ -119,9 +131,9 @@
     k_acc[...] = jnp.zeros_like(k_acc)
     v_acc[...] = jnp.zeros_like(v_acc)
     for b in range(NB):
-        keys[b] = x_ref[b, 0:64, :].T
-        duo[b, 0:HD, 0:BLK] = x_ref[b, 64:96, :]
-        duo[b, HD : 2 * HD, BLK : 2 * BLK] = x_ref[b, 96:128, :]
+        keys[b] = x_ref[b, BLK : BLK + 64, :].T
+        duo[b, 0:HD, 0:BLK] = x_ref[b, BLK + 64 : BLK + 96, :]
+        duo[b, HD : 2 * HD, BLK : 2 * BLK] = x_ref[b, BLK + 96 : BLK + 128, :]
 
     def pair(step, u):
         p = step * UNROLL + u
@@ -166,10 +178,10 @@
             ds = (prob * (gprob[p] - inner[i] * share) * SCALE).astype(BF)
             same = i == before
             o = jnp.where(same, o, 0.0) + jnp.dot(
-                x_ref[j, 32:64, :], low, preferred_element_type=F32
+                x_ref[j, BLK + 32 : BLK + 64, :], low, preferred_element_type=F32
             )
             q = jnp.where(same, q, 0.0) + jnp.dot(
-                x_ref[j, 0:32, :], ds, preferred_element_type=F32
+                x_ref[j, BLK : BLK + 32, :], ds, preferred_element_type=F32
             )
             out_acc[i] = o
             q_acc[i] = q
@@ -188,62 +200,57 @@
 
     for b in range(NB):
         cols = slice(b * BLK, (b + 1) * BLK)
-        back_ref[b, 0:WIDTH, :] = masked_ref[...]
-        back_ref[b, WIDTH : WIDTH + HD, :] = out_acc[b].astype(BF)
+        back_ref[b] = out_acc[b].astype(BF)
         grad_ref[0:32, cols] = q_acc[b].astype(BF)
         grad_ref[32:64, cols] = k_acc[b].astype(BF)
         grad_ref[64:96, cols] = (
-            v_acc[b].astype(BF).astype(F32) + x_ref[b, 128:160, :].astype(F32)
+            v_acc[b].astype(BF).astype(F32) + x_ref[b, BLK + 128 : BLK + 160, :].astype(F32)
         ).astype(BF)
 
 
-def weights_kernel(grad_ref, masked_ref, keep_ref, send_ref, att_ref):
-    core = lax.bitwise_and(lax.axis_index("dp"), 1)
-    masked = jnp.concatenate(
-        [
-            jnp.concatenate(
-                [masked_ref[b, lane * 128 : (lane + 1) * 128, :] for b in range(NB)], axis=0
-            )
-            for lane in range(4)
-        ],
-        axis=1,
-    )
-    both = jnp.dot(grad_ref[...], masked, preferred_element_type=F32)
-    for head in range(HEADS):
-        att_ref[head * HD : (head + 1) * HD, :] = masked_ref[head, WIDTH : WIDTH + HD, :]
-    own_low = core == 0
-    for lane in range(2):
-        low = both[:, lane * 128 : (lane + 1) * 128]
-        high = both[:, (lane + 2) * 128 : (lane + 3) * 128]
-        keep = jnp.where(own_low, low, high)
-        send = jnp.where(own_low, high, low)
-        for r in range(8):
-            keep_ref[lane * 8 + r] = keep[r * CHUNK : (r + 1) * CHUNK]
-            send_ref[lane * 8 + r] = send[r * CHUNK : (r + 1) * CHUNK]
-
-
-def output_kernel(own_ref, other_ref, q_ref, k_ref, v_ref, full):
-    own_low = lax.bitwise_and(lax.axis_index("dp"), 1) == 0
-    for lane in range(2):
-        for r in range(8):
-            own = own_ref[lane * 8 + r]
-            other = other_ref[lane * 8 + r]
-            rows = slice(r * CHUNK, (r + 1) * CHUNK)
-            full[rows, lane * 128 : (lane + 1) * 128] = jnp.where(own_low, own, other)
-            full[rows, (lane + 2) * 128 : (lane + 3) * 128] = jnp.where(own_low, other, own)
+def weights_kernel(
+    grad_ref, own_ref, down_ref, right_ref, far_ref, part_ref, full,
+):
+    group = group_of(lax.axis_index("seq"))
+    pairs = (((own_ref, 0), (down_ref, 2)), ((right_ref, 1), (far_ref, 3)))
+    for pair in pairs:
+        columns = [ref[...].reshape(NB * ROWS, 128) for ref, _ in pair]
+        both = jnp.dot(
+            grad_ref[...], jnp.concatenate(columns, axis=1), preferred_element_type=F32
+        )
+        for n, (_, flip) in enumerate(pair):
+            full[lax.bitwise_xor(group, flip)] = both[:, n * 128 : (n + 1) * 128]
+    for lane in range(4):
+        for half in range(2):
+            part_ref[lane * 2 + half] = full[lane, half * CHUNK : (half + 1) * CHUNK, :]
+
+
+def chip_kernel(back_ref, both_ref, sum_ref):
+    start = lax.bitwise_and(lax.axis_index("dp"), 1) * NEAR
+    sum_ref[...] = both_ref[pl.ds(start, NEAR)] + both_ref[pl.ds(2 * NEAR + start, NEAR)]
+
+
+def output_kernel(all_ref, q_ref, k_ref, v_ref, full):
+    for lane in range(4):
+        for half in range(2):
+            rows = slice(half * CHUNK, (half + 1) * CHUNK)
+            full[rows, lane * 128 : (lane + 1) * 128] = all_ref[lane * 2 + half]
     for place, ref in enumerate((q_ref, k_ref, v_ref)):
         ref[...] = full[place * HD : (place + 1) * HD, :]
 
 
-def mixed_kernel(pick_ref, att_ref, local_ref, degree_ref, lower_ref, upper_ref, mixed_ref):
+def graph_kernel(pick_ref, local_ref, degree_ref, lower_ref, upper_ref, graph_ref):
     rows = jnp.concatenate([lower_ref[0], upper_ref[0]], axis=0)
     border = jnp.dot(pick_ref[...], rows, preferred_element_type=F32)
-    graph = (local_ref[...] + border) / degree_ref[...]
-    attended = att_ref[...].astype(F32).T
-    mixed_ref[0] = (attended + graph).astype(BF)
-
-
-def call(kernel, name, shapes, in_specs, scratch=(), limit=32, flops=0, moved=0):
+    graph_ref[...] = (local_ref[...] + border) / degree_ref[...]
+
+
+def mixed_kernel(att_ref, graph_ref, mixed_ref):
+    attended = att_ref[...].reshape(WIDTH, ROWS).astype(F32).T
+    mixed_ref[0] = (attended + graph_ref[...]).astype(BF)
+
+
+def call(kernel, name, shapes, in_specs, scratch=(), limit=16, flops=0, moved=0):
     out = tuple(jax.ShapeDtypeStruct(shape, kind) for shape, kind in shapes)
     return pl.pallas_call(
         kernel,
@@ -267,12 +274,11 @@
         masked_ids, boundary_counts.transpose(0, 2, 1), mask_token, features, w_value,
         adjacency, boundary_ids, boundary_targets, grad_out, w_key, w_query,
     )
-    masked, heads, send_lower, send_upper, local, degree, pick = call(
+    heads, send_lower, send_upper, local, degree, pick = call(
         rows_kernel,
         "rows",
         [
-            ((WIDTH, ROWS), BF),
-            ((HEADS, 5 * HD, ROWS), BF),
+            ((HEADS, BLK + 5 * HD, ROWS), BF),
             ((1, slots, WIDTH), BF),
             ((1, slots, WIDTH), BF),
             ((ROWS, WIDTH), F32),
@@ -290,12 +296,44 @@
     up = [(c, c + 1) for c in range(clusters - 1)]
     lower = lax.ppermute(send_lower, "dp", up)
     upper = lax.ppermute(send_upper, "dp", [(b, a) for a, b in up])
+    (graph,) = call(
+        graph_kernel,
+        "graph",
+        [((ROWS, WIDTH), F32)],
+        [VM] * 5,
+        flops=20_000_000,
+        moved=1_000_000,
+    )(pick, local, degree, lower, upper)
+    (columns,) = call(
+        columns_kernel,
+        "columns",
+        [((NB, BLK, 128), BF)],
+        [ANY, VM],
+        flops=100_000,
+        moved=1_000_000,
+    )(graph, x)
+
+    def neighbour(down, right, odd):
+        def turn(n):
+            return ((n + odd) ^ 1) - odd
+
+        return lax.ppermute(
+            columns,
+            "seq",
+            [
+                (4 * y + x, 4 * ((turn(y) if down else y) % 4) + (turn(x) if right else x) % 4)
+                for y in range(4)
+                for x in range(4)
+            ],
+        )
+
+    parts = [columns, neighbour(1, 0, 0), neighbour(0, 1, 0), neighbour(1, 1, 1)]
 
     back, grads = call(
         attention_kernel,
         "attention",
-        [((NB, WIDTH + HD, BLK), BF), ((3 * HD, NB * BLK), BF)],
-        [SM, VM, VM],
+        [((NB, HD, BLK), BF), ((3 * HD, NB * BLK), BF)],
+        [SM, VM],
         scratch=[
             pltpu.SMEM((SLOTS + UNROLL,), jnp.int32),
             pltpu.VMEM((NB, BLK, 2 * HD), BF),
@@ -311,49 +349,70 @@
             pltpu.VMEM((NB, HD, BLK), F32),
             pltpu.VMEM((NB, HD, BLK), F32),
         ],
-        limit=48,
+        limit=44,
         flops=5_000_000_000,
         moved=20_000_000,
-    )(block_mask, x, masked)
+    )(block_mask, x)
 
     back = lax.all_to_all(back, "seq", split_axis=0, concat_axis=0, tiled=True)
-    keep, send, attended = call(
+    (part,) = call(
         weights_kernel,
         "weights",
-        [((CHIPS, CHUNK, 128), F32), ((CHIPS, CHUNK, 128), F32), ((WIDTH, ROWS), BF)],
-        [VM, VM],
+        [((2 * NEAR, CHUNK, 128), F32)],
+        [VM] * 5,
+        scratch=[pltpu.VMEM((4, 3 * HD, 128), F32)],
         flops=200_000_000,
         moved=3_000_000,
-    )(grads, back)
+    )(grads, *parts)
     (mixed,) = call(
         mixed_kernel,
         "mixed",
         [((1, ROWS, WIDTH), BF)],
-        [VM] * 6,
+        [VM, VM],
         flops=20_000_000,
         moved=1_000_000,
-    )(pick, attended, local, degree, lower, upper)
-
-    swap = [(c, c ^ 1) for c in range(clusters)]
-    groups = [[chip * 2 + core for chip in range(clusters // 2)] for core in range(2)]
-    pair_sum = keep + lax.ppermute(send, "dp", swap)
-    terms = lax.all_to_all(
-        pair_sum, "dp", split_axis=0, concat_axis=0, tiled=True, axis_index_groups=groups
-    )
-    reduced = jnp.broadcast_to(jnp.sum(terms, axis=0, keepdims=True), terms.shape)
-    half = lax.all_to_all(
-        reduced, "dp", split_axis=0, concat_axis=0, tiled=True, axis_index_groups=groups
-    )
-    other = lax.ppermute(half, "dp", swap)
+    )(back, graph)
+
+    cores = [[c, c + 1] for c in range(0, clusters, 2)]
+    span = 2 * NEAR
+    near = [
+        [g * span + 2 * n + core for n in range(NEAR)]
+        for g in range(clusters // span)
+        for core in range(2)
+    ]
+    far = [[g * span + n for g in range(clusters // span)] for n in range(span)]
+
+    def exchange(item, groups):
+        return lax.all_to_all(
+            item, "dp", split_axis=0, concat_axis=0, tiled=True, axis_index_groups=groups
+        )
+
+    def gather(item, groups):
+        return lax.all_gather(item, "dp", axis=0, tiled=True, axis_index_groups=groups)
+
+    def copies(item, count):
+        return jnp.broadcast_to(jnp.sum(item, axis=0, keepdims=True), (count,) + item.shape[1:])
+
+    (chip_sum,) = call(
+        chip_kernel,
+        "chip_sum",
+        [((NEAR, CHUNK, 128), F32)],
+        [ANY, VM],
+        flops=100_000,
+        moved=300_000,
+    )(back, gather(part, cores))
+    terms = exchange(chip_sum, near)
+    terms = exchange(copies(terms, clusters // span), far)
+    reduced = gather(exchange(copies(terms, NEAR), near), cores)
     grad_query, grad_key, grad_value = call(
         output_kernel,
         "outputs",
         [((HD, WIDTH), F32)] * 3,
-        [VM, VM],
+        [VM],
         scratch=[pltpu.VMEM((3 * HD, WIDTH), F32)],
         flops=1_000_000,
         moved=1_000_000,
-    )(half, other)
+    )(reduced)
     return mixed, grad_query.T, grad_key.T, grad_value.T
 
 

time: 129 us -> 112 us (0.87)
  blocking collectives: 94.8 us -> 51.7 us
  starting transfers between devices: 15.8 us -> 31.5 us
  waiting for transfers between devices: 4.26 us -> 13.4 us
  local copies, waits for them, and re-layouts: 0.02 us -> 3.03 us
  Pallas kernels: 12.6 us -> 11.3 us
    all_to_all x4 -> x2, blocking collectives: 94.8 us -> 34 us  [exchange(): lax.all_to_all(item, 'dp', split_axis=0, concat_axis=0, tiled=True, axis_...]
    all_gather x0 -> x2, blocking collectives: none -> 17.7 us  [gather(): lax.all_gather(item, 'dp', axis=0, tiled=True, axis_index_groups=groups)]
    all_to_all x0 -> x3, starting transfers between devices: none -> 17.4 us  [the longest x1 7.59 us: on_device(): x = lax.all_to_all(heads, 'seq', split_axis=0, concat_axis=0, tiled=True)]
    all_to_all x0 -> x3, waiting for transfers between devices: none -> 9.79 us  [the longest x1 5.87 us: on_device(): x = lax.all_to_all(heads, 'seq', split_axis=0, concat_axis=0, tiled=True)]
    ppermute x2 -> x3, starting transfers between devices: 10.7 us -> 7.79 us  [neighbour(): lax.ppermute(columns, 'seq', [(4 * y + x, 4 * ((turn(y) if down else y) %...]
    unnamed x2 -> x8, local copies, waits for them, and re-layouts: 0.01 us -> 2.38 us
    pallas_call x5 -> x8, Pallas kernels: 12.6 us -> 11.3 us  [the longest x1 5.65 us: on_device(): call(attention_kernel, 'attention', [((NB, HD, BLK), BF), ((3 * HD, NB *...]
    ppermute x1, starting transfers between devices: 3.09 us -> 4.39 us  [on_device(): lower = lax.ppermute(send_lower, 'dp', up)]
  transfers between devices with their start and end apart: 4 -> 8, of which waited for: 2 -> 3; matrix products, arithmetic and copies ran while one was open for 0% -> 0% of each run, Pallas kernels for 1% -> 6%
where the time goes in v3:
time: 112 us
  blocking collectives  51.7 us (46%)
  starting transfers between devices  31.5 us (28%)
  waiting for transfers between devices  13.4 us (12%)
  Pallas kernels  11.3 us (10%)
  local copies, waits for them, and re-layouts  3.03 us (3%)
    all_to_all x2, blocking collectives, exchange(): lax.all_to_all(item, 'dp', split_axis=0, concat_axis=0, tiled=True, axis_...  34 us
    all_gather x2, blocking collectives, gather(): lax.all_gather(item, 'dp', axis=0, tiled=True, axis_index_groups=groups)  17.7 us
    ppermute x3, starting transfers between devices, neighbour(): lax.ppermute(columns, 'seq', [(4 * y + x, 4 * ((turn(y) if down else y) %...  7.79 us
    all_to_all x1, starting transfers between devices, on_device(): x = lax.all_to_all(heads, 'seq', split_axis=0, concat_axis=0, tiled=True)  7.59 us
    all_to_all x1, starting transfers between devices, on_device(): back = lax.all_to_all(back, 'seq', split_axis=0, concat_axis=0, tiled=True)  6.47 us
    all_to_all x1, waiting for transfers between devices, on_device(): x = lax.all_to_all(heads, 'seq', split_axis=0, concat_axis=0, tiled=True)  5.87 us
    pallas_call x1, Pallas kernels, on_device(): call(attention_kernel, 'attention', [((NB, HD, BLK), BF), ((3 * HD, NB *...  5.65 us
    ppermute x1, starting transfers between devices, on_device(): lower = lax.ppermute(send_lower, 'dp', up)  4.39 us
  transfers between devices with their start and end apart: 8, of which 3 were waited for; matrix products, arithmetic and copies ran while one was open for 0% of the time, Pallas kernels for 6%

profile of v3, /device:TPU:1, one launch (start us, length us, event | category | flops | bytes accessed | tf_op | source)
XLA Modules:
  0.0 111.7 jit_solution(9845684539824050951)
XLA Ops:
  0.6 3.5 %rows.1 = (bf16[16,288,128]{2,1,0:T(8,128)(2,1)}, bf16[1,32,512]{2,1,0:T(8,128)(2,1)S(1)}, bf16[1,32,512]{2,1,0:T(8,128)(2,1)S(1)}, f32[128,512]{1,0:T(8,128)S(1...) custom-call(s32[1,1024]{1,0:T(1,128)} %refs_0_.1, s32[1,1,2]{2,1,0:T(1,128)} %bitcast.4, bf16[512]{0:T(512)(128)(2,1)} %refs_2_.1, ...), custom_call_target="tpu_custom_call" | custom-call | flops 400000000 | bytes 3000000 | tf_op jit(solution)/shard_map/rows/pallas_call | solution.py:277
  4.1 7.6 %all-to-all-start = ((bf16[16,288,128]{2,1,0:T(8,128)(2,1)}), bf16[16,288,128]{2,1,0:T(8,128)(2,1)S(1)}, u32[]{:S(2)}, u32[]{:S(2)}) async-start(bf16[16,288,128]{2,1,0:T(8,128)(2,1)} %get-tuple-element.15), calls=%async_computation | async-start | bytes 2359296 | tf_op jit(solution)/shard_map/all_to_all | solution.py:295
  11.7 4.4 %collective-permute-start = (bf16[1,32,512]{2,1,0:T(8,128)(2,1)S(1)}, bf16[1,32,512]{2,1,0:T(8,128)(2,1)S(1)}, u32[]{:S(2)}, u32[]{:S(2)}) collective-permute-start(bf16[1,32,512]{2,1,0:T(8,128)(2,1)S(1)} %get-tuple-element.20), channel_id=1, source_target_pairs={{0,16},{16,32},{32,48},{48,64},{64,80},{80,96},{96,112},{112,128},... | collective-permute-start | bytes 98312 | tf_op jit(solution)/shard_map/ppermute | solution.py:297
  16.1 1.9 %collective-permute-start.1 = (bf16[1,32,512]{2,1,0:T(8,128)(2,1)S(1)}, bf16[1,32,512]{2,1,0:T(8,128)(2,1)S(1)}, u32[]{:S(2)}, u32[]{:S(2)}) collective-permute-start(bf16[1,32,512]{2,1,0:T(8,128)(2,1)S(1)} %get-tuple-element.21), channel_id=1, source_target_pairs={{16,0},{32,16},{48,32},{64,48},{80,64},{96,80},{112,96},{128,112},... | collective-permute-start | bytes 98312 | tf_op jit(solution)/shard_map/ppermute | solution.py:298
  18.1 3.6 %collective-permute-done.1.upper_ref = bf16[1,32,512]{2,1,0:T(8,128)(2,1)S(1)} collective-permute-done((bf16[1,32,512]{2,1,0:T(8,128)(2,1)S(1)}, bf16[1,32,512]{2,1,0:T(8,128)(2,1)S(1)}, u32[]{:S(2)}, u32[]{:S(2)}) %collective-permute-start.1) | collective-permute-done | bytes 32800 | tf_op jit(solution)/shard_map/ppermute | solution.py:298
  21.8 5.9 %all-to-all-done.x_ref = bf16[16,288,128]{2,1,0:T(8,128)(2,1)S(1)} async-done(((bf16[16,288,128]{2,1,0:T(8,128)(2,1)}), bf16[16,288,128]{2,1,0:T(8,128)(2,1)S(1)}, u32[]{:S(2)}, u32[]{:S(2)}) %all-to-all-start) | async-done | bytes 1179680 | tf_op jit(solution)/shard_map/all_to_all | solution.py:295
  27.7 2.7 %collective-permute-start.4 = (bf16[16,128,128]{2,1,0:T(8,128)(2,1)S(1)}, bf16[16,128,128]{2,1,0:T(8,128)(2,1)S(1)}, u32[]{:S(2)}, u32[]{:S(2)}) collective-permute-start(bf16[16,128,128]{2,1,0:T(8,128)(2,1)S(1)} %columns.1.own_ref), channel_id=1, source_target_pairs={{0,15},{1,14},{2,13},{3,12},{4,11},{5,10},{6,9},{7,8},{8,7},{9,6},... | collective-permute-start | bytes 1572872 | tf_op jit(solution)/shard_map/ppermute | solution.py:320
  30.4 1.9 %collective-permute-start.3 = (bf16[16,128,128]{2,1,0:T(8,128)(2,1)S(1)}, bf16[16,128,128]{2,1,0:T(8,128)(2,1)S(1)}, u32[]{:S(2)}, u32[]{:S(2)}) collective-permute-start(bf16[16,128,128]{2,1,0:T(8,128)(2,1)S(1)} %columns.1.own_ref), channel_id=1, source_target_pairs={{0,1},{1,0},{2,3},{3,2},{4,5},{5,4},{6,7},{7,6},{8,9},{9,8},{10,11... | collective-permute-start | bytes 1572872 | tf_op jit(solution)/shard_map/ppermute | solution.py:320
  32.4 3.2 %collective-permute-start.2 = (bf16[16,128,128]{2,1,0:T(8,128)(2,1)S(1)}, bf16[16,128,128]{2,1,0:T(8,128)(2,1)S(1)}, u32[]{:S(2)}, u32[]{:S(2)}) collective-permute-start(bf16[16,128,128]{2,1,0:T(8,128)(2,1)S(1)} %columns.1.own_ref), channel_id=1, source_target_pairs={{0,4},{1,5},{2,6},{3,7},{4,0},{5,1},{6,2},{7,3},{8,12},{9,13},{10,... | collective-permute-start | bytes 1572872 | tf_op jit(solution)/shard_map/ppermute | solution.py:320
  35.6 5.7 %attention.1 = (bf16[16,32,128]{2,1,0:T(8,128)(2,1)S(1)}, bf16[96,2048]{1,0:T(8,128)(2,1)S(1)}) custom-call(s32[1,16,16]{2,1,0:T(8,128)S(1)} %copy-done.3, bf16[16,288,128]{2,1,0:T(8,128)(2,1)S(1)} %all-to-all-done.x_ref), custom_call_target="tpu_custom_call" | custom-call | flops 5000000000 | bytes 20000000 | tf_op jit(solution)/shard_map/attention/pallas_call | solution.py:332
  41.2 0.7 copy-done
  42.0 0.7 copy-done.2
  42.6 6.5 %all-to-all-start.1 = ((bf16[16,32,128]{2,1,0:T(8,128)(2,1)}), bf16[16,32,128]{2,1,0:T(8,128)(2,1)S(1)}, u32[]{:S(2)}, u32[]{:S(2)}) async-start(bf16[16,32,128]{2,1,0:T(8,128)(2,1)} %copy-done.2), calls=%async_computation.1 | async-start | bytes 262144 | tf_op jit(solution)/shard_map/all_to_all | solution.py:357
  49.1 1.0 copy-done.1
  50.1 0.5 weights.1
  50.6 6.9 %all_gather.6.both_ref = f32[16,48,128]{2,1,0:T(8,128)S(1)} all-gather(f32[8,48,128]{2,1,0:T(8,128)S(1)} %weights.1), channel_id=1, replica_groups={{0,16},{32,48},{64,80},{96,112},{128,144},{160,176},{192,208},{224,240}..., dimensions={0}, use_global_device_ids=true | all-gather | bytes 589824 | tf_op jit(solution)/shard_map/all_gather | solution.py:391
  57.6 10.2 %all_to_all.25 = f32[4,48,128]{2,1,0:T(8,128)S(1)} all-to-all(f32[4,48,128]{2,1,0:T(8,128)S(1)} %chip_sum.1), channel_id=1, replica_groups={{0,32,64,96},{16,48,80,112},{128,160,192,224},{144,176,208,240},{256,28..., dimensions={0} | all-to-all | bytes 196608 | tf_op jit(solution)/shard_map/all_to_all | solution.py:386
  67.8 23.8 %all_to_all.26 = f32[4,48,128]{2,1,0:T(8,128)S(1)} all-to-all(f32[4,48,128]{2,1,0:T(8,128)S(1)} %broadcast_in_dim.4), channel_id=1, replica_groups={{0,128,256,384},{16,144,272,400},{32,160,288,416},{48,176,304,432},{64,..., dimensions={0} | all-to-all | bytes 196608 | tf_op jit(solution)/shard_map/all_to_all | solution.py:386
  91.6 0.6 broadcast_in_dim.5
  92.3 3.3 %all-to-all-start.4 = ((f32[4,48,128]{2,1,0:T(8,128)}), f32[4,48,128]{2,1,0:T(8,128)S(1)}, u32[]{:S(2)}, u32[]{:S(2)}) async-start(f32[4,48,128]{2,1,0:T(8,128)} %broadcast_in_dim.5), calls=%async_computation.4 | async-start | bytes 196608 | tf_op jit(solution)/shard_map/all_to_all | solution.py:386
  95.6 0.8 mixed.1
  96.3 3.9 %all-to-all-done.4 = f32[4,48,128]{2,1,0:T(8,128)S(1)} async-done(((f32[4,48,128]{2,1,0:T(8,128)}), f32[4,48,128]{2,1,0:T(8,128)S(1)}, u32[]{:S(2)}, u32[]{:S(2)}) %all-to-all-start.4) | async-done | bytes 98336 | tf_op jit(solution)/shard_map/all_to_all | solution.py:386
  100.2 10.8 %all_gather.7.all_ref = f32[8,48,128]{2,1,0:T(8,128)S(1)} all-gather(f32[4,48,128]{2,1,0:T(8,128)S(1)} %all-to-all-done.4), channel_id=1, replica_groups={{0,16},{32,48},{64,80},{96,112},{128,144},{160,176},{192,208},{224,240}..., dimensions={0}, use_global_device_ids=true | all-gather | bytes 294912 | tf_op jit(solution)/shard_map/all_gather | solution.py:391
  111.0 0.7 outputs.1
  (16 shorter events, 0.3 us)
Async XLA Ops:
  4.1 23.6 %all-to-all-start = ((bf16[16,288,128]{2,1,0:T(8,128)(2,1)}), bf16[16,288,128]{2,1,0:T(8,128)(2,1)S(1)}, u32[]{:S(2)}, u32[]{:S(2)}) async-start(bf16[16,288,128]{2,1,0:T(8,128)(2,1)} %get-tuple-element.15), calls=%async_computation | async-start | bytes 2359296 | tf_op jit(solution)/shard_map/all_to_all | solution.py:295
  11.7 6.3 %collective-permute-start = (bf16[1,32,512]{2,1,0:T(8,128)(2,1)S(1)}, bf16[1,32,512]{2,1,0:T(8,128)(2,1)S(1)}, u32[]{:S(2)}, u32[]{:S(2)}) collective-permute-start(bf16[1,32,512]{2,1,0:T(8,128)(2,1)S(1)} %get-tuple-element.20), channel_id=1, source_target_pairs={{0,16},{16,32},{32,48},{48,64},{64,80},{80,96},{96,112},{112,128},... | collective-permute-start | bytes 98312 | tf_op jit(solution)/shard_map/ppermute | solution.py:297
  16.1 5.5 %collective-permute-start.1 = (bf16[1,32,512]{2,1,0:T(8,128)(2,1)S(1)}, bf16[1,32,512]{2,1,0:T(8,128)(2,1)S(1)}, u32[]{:S(2)}, u32[]{:S(2)}) collective-permute-start(bf16[1,32,512]{2,1,0:T(8,128)(2,1)S(1)} %get-tuple-element.21), channel_id=1, source_target_pairs={{16,0},{32,16},{48,32},{64,48},{80,64},{96,80},{112,96},{128,112},... | collective-permute-start | bytes 98312 | tf_op jit(solution)/shard_map/ppermute | solution.py:298
  21.7 13.9 %copy-start.3 = (s32[1,16,16]{2,1,0:T(8,128)S(1)}, s32[1,16,16]{2,1,0:T(8,128)}, u32[]{:S(2)}) copy-start(s32[1,16,16]{2,1,0:T(8,128)} %mask_ref.1) | copy-start | bytes 3076
  27.7 21.4 %collective-permute-start.4 = (bf16[16,128,128]{2,1,0:T(8,128)(2,1)S(1)}, bf16[16,128,128]{2,1,0:T(8,128)(2,1)S(1)}, u32[]{:S(2)}, u32[]{:S(2)}) collective-permute-start(bf16[16,128,128]{2,1,0:T(8,128)(2,1)S(1)} %columns.1.own_ref), channel_id=1, source_target_pairs={{0,15},{1,14},{2,13},{3,12},{4,11},{5,10},{6,9},{7,8},{8,7},{9,6},... | collective-permute-start | bytes 1572872 | tf_op jit(solution)/shard_map/ppermute | solution.py:320
  30.4 18.7 %collective-permute-start.3 = (bf16[16,128,128]{2,1,0:T(8,128)(2,1)S(1)}, bf16[16,128,128]{2,1,0:T(8,128)(2,1)S(1)}, u32[]{:S(2)}, u32[]{:S(2)}) collective-permute-start(bf16[16,128,128]{2,1,0:T(8,128)(2,1)S(1)} %columns.1.own_ref), channel_id=1, source_target_pairs={{0,1},{1,0},{2,3},{3,2},{4,5},{5,4},{6,7},{7,6},{8,9},{9,8},{10,11... | collective-permute-start | bytes 1572872 | tf_op jit(solution)/shard_map/ppermute | solution.py:320
  32.4 16.7 %collective-permute-start.2 = (bf16[16,128,128]{2,1,0:T(8,128)(2,1)S(1)}, bf16[16,128,128]{2,1,0:T(8,128)(2,1)S(1)}, u32[]{:S(2)}, u32[]{:S(2)}) collective-permute-start(bf16[16,128,128]{2,1,0:T(8,128)(2,1)S(1)} %columns.1.own_ref), channel_id=1, source_target_pairs={{0,4},{1,5},{2,6},{3,7},{4,0},{5,1},{6,2},{7,3},{8,12},{9,13},{10,... | collective-permute-start | bytes 1572872 | tf_op jit(solution)/shard_map/ppermute | solution.py:320
  41.2 0.7 copy-start
  42.0 0.7 copy-start.2
  42.6 15.0 %all-to-all-start.1 = ((bf16[16,32,128]{2,1,0:T(8,128)(2,1)}), bf16[16,32,128]{2,1,0:T(8,128)(2,1)S(1)}, u32[]{:S(2)}, u32[]{:S(2)}) async-start(bf16[16,32,128]{2,1,0:T(8,128)(2,1)} %copy-done.2), calls=%async_computation.1 | async-start | bytes 262144 | tf_op jit(solution)/shard_map/all_to_all | solution.py:357
  49.1 1.0 copy-start.1
  92.3 8.0 %all-to-all-start.4 = ((f32[4,48,128]{2,1,0:T(8,128)}), f32[4,48,128]{2,1,0:T(8,128)S(1)}, u32[]{:S(2)}, u32[]{:S(2)}) async-start(f32[4,48,128]{2,1,0:T(8,128)} %broadcast_in_dim.5), calls=%async_computation.4 | async-start | bytes 196608 | tf_op jit(solution)/shard_map/all_to_all | solution.py:386

commit v4 on v3

--- a/solution.py
+++ b/solution.py
@@ -225,9 +225,20 @@
             part_ref[lane * 2 + half] = full[lane, half * CHUNK : (half + 1) * CHUNK, :]
 
 
-def chip_kernel(back_ref, both_ref, sum_ref):
+def chip_kernel(both_ref, sum_ref):
     start = lax.bitwise_and(lax.axis_index("dp"), 1) * NEAR
     sum_ref[...] = both_ref[pl.ds(start, NEAR)] + both_ref[pl.ds(2 * NEAR + start, NEAR)]
+
+
+def near_kernel(terms_ref, att_ref, sum_ref, att_out):
+    att_out[...] = att_ref[...]
+    sum_ref[...] = (terms_ref[0] + terms_ref[1]) + (terms_ref[2] + terms_ref[3])
+
+
+def far_kernel(back_ref, terms_ref, copies_ref):
+    total = (terms_ref[0] + terms_ref[1]) + (terms_ref[2] + terms_ref[3])
+    for n in range(NEAR):
+        copies_ref[n] = total
 
 
 def output_kernel(all_ref, q_ref, k_ref, v_ref, full):
@@ -354,7 +365,6 @@
         moved=20_000_000,
     )(block_mask, x)
 
-    back = lax.all_to_all(back, "seq", split_axis=0, concat_axis=0, tiled=True)
     (part,) = call(
         weights_kernel,
         "weights",
@@ -364,6 +374,50 @@
         flops=200_000_000,
         moved=3_000_000,
     )(grads, *parts)
+    cores = [[c, c + 1] for c in range(0, clusters, 2)]
+    span = 2 * NEAR
+    near = [
+        [g * span + 2 * n + core for n in range(NEAR)]
+        for g in range(clusters // span)
+        for core in range(2)
+    ]
+    far = [[g * span + n for g in range(clusters // span)] for n in range(span)]
+
+    def exchange(item, groups):
+        return lax.all_to_all(
+            item, "dp", split_axis=0, concat_axis=0, tiled=True, axis_index_groups=groups
+        )
+
+    def gather(item, groups):
+        return lax.all_gather(item, "dp", axis=0, tiled=True, axis_index_groups=groups)
+
+    (chip_sum,) = call(
+        chip_kernel,
+        "chip_sum",
+        [((NEAR, CHUNK, 128), F32)],
+        [VM],
+        flops=100_000,
+        moved=300_000,
+    )(gather(part, cores))
+    near_sum, back = call(
+        near_kernel,
+        "near_sum",
+        [((CHUNK, 128), F32), ((NB, HD, BLK), BF)],
+        [VM, VM],
+        flops=100_000,
+        moved=300_000,
+    )(exchange(chip_sum, near), back)
+    back = lax.all_to_all(back, "seq", split_axis=0, concat_axis=0, tiled=True)
+    terms = lax.all_gather(near_sum, "dp", axis=0, tiled=False, axis_index_groups=far)
+    (copies,) = call(
+        far_kernel,
+        "far_sum",
+        [((NEAR, CHUNK, 128), F32)],
+        [ANY, VM],
+        flops=100_000,
+        moved=300_000,
+    )(back, terms)
+    reduced = gather(exchange(copies, near), cores)
     (mixed,) = call(
         mixed_kernel,
         "mixed",
@@ -373,37 +427,6 @@
         moved=1_000_000,
     )(back, graph)
 
-    cores = [[c, c + 1] for c in range(0, clusters, 2)]
-    span = 2 * NEAR
-    near = [
-        [g * span + 2 * n + core for n in range(NEAR)]
-        for g in range(clusters // span)
-        for core in range(2)
-    ]
-    far = [[g * span + n for g in range(clusters // span)] for n in range(span)]
-
-    def exchange(item, groups):
-        return lax.all_to_all(
-            item, "dp", split_axis=0, concat_axis=0, tiled=True, axis_index_groups=groups
-        )
-
-    def gather(item, groups):
-        return lax.all_gather(item, "dp", axis=0, tiled=True, axis_index_groups=groups)
-
-    def copies(item, count):
-        return jnp.broadcast_to(jnp.sum(item, axis=0, keepdims=True), (count,) + item.shape[1:])
-
-    (chip_sum,) = call(
-        chip_kernel,
-        "chip_sum",
-        [((NEAR, CHUNK, 128), F32)],
-        [ANY, VM],
-        flops=100_000,
-        moved=300_000,
-    )(back, gather(part, cores))
-    terms = exchange(chip_sum, near)
-    terms = exchange(copies(terms, clusters // span), far)
-    reduced = gather(exchange(copies(terms, NEAR), near), cores)
     grad_query, grad_key, grad_value = call(
         output_kernel,
         "outputs",

time: 112 us -> 107 us (0.955)
  blocking collectives: 51.7 us -> 48.2 us
  local copies, waits for them, and re-layouts: 3.03 us -> 0.01 us
  waiting for transfers between devices: 13.4 us -> 15.6 us
  starting transfers between devices: 31.5 us -> 29.7 us
  Pallas kernels: 11.3 us -> 12.6 us
    all_to_all x2 -> x1, blocking collectives: 34 us -> 13.5 us  [exchange(): lax.all_to_all(item, 'dp', split_axis=0, concat_axis=0, tiled=True, axis_...]
    all_gather x0 -> x1, blocking collectives: none -> 20.2 us  [on_device(): lax.all_gather(near_sum, 'dp', axis=0, tiled=False, axis_index_groups=far)]
    all_gather x2, blocking collectives: 17.7 us -> 14.5 us  [gather(): lax.all_gather(item, 'dp', axis=0, tiled=True, axis_index_groups=groups)]
    unnamed x8 -> x2, local copies, waits for them, and re-layouts: 2.38 us -> 0.01 us
    ppermute x3, waiting for transfers between devices: 0.01 us -> 2.19 us  [neighbour(): lax.ppermute(columns, 'seq', [(4 * y + x, 4 * ((turn(y) if down else y) %...]
    all_to_all x1, starting transfers between devices: 6.47 us -> 4.55 us  [on_device(): back = lax.all_to_all(back, 'seq', split_axis=0, concat_axis=0, tiled=True)]
    pallas_call x1 -> x3, Pallas kernels: 0.01 us -> 1.33 us  [the longest x1 0.67 us: on_device(): call(near_kernel, 'near_sum', [((CHUNK, 128), F32), ((NB, HD, BLK), BF)],...]
  transfers between devices with their start and end apart: 8 -> 8, of which waited for: 3 -> 5; matrix products, arithmetic and copies ran while one was open for 0% -> 0% of each run, Pallas kernels for 6% -> 6%
where the time goes in v4:
time: 107 us
  blocking collectives  48.2 us (45%)
  starting transfers between devices  29.7 us (28%)
  waiting for transfers between devices  15.6 us (15%)
  Pallas kernels  12.6 us (12%)
    all_gather x1, blocking collectives, on_device(): lax.all_gather(near_sum, 'dp', axis=0, tiled=False, axis_index_groups=far)  20.2 us
    all_gather x2, blocking collectives, gather(): lax.all_gather(item, 'dp', axis=0, tiled=True, axis_index_groups=groups)  14.5 us
    all_to_all x1, blocking collectives, exchange(): lax.all_to_all(item, 'dp', split_axis=0, concat_axis=0, tiled=True, axis_...  13.5 us
    ppermute x3, starting transfers between devices, neighbour(): lax.ppermute(columns, 'seq', [(4 * y + x, 4 * ((turn(y) if down else y) %...  7.79 us
    all_to_all x1, starting transfers between devices, on_device(): x = lax.all_to_all(heads, 'seq', split_axis=0, concat_axis=0, tiled=True)  7.59 us
    all_to_all x1, waiting for transfers between devices, on_device(): x = lax.all_to_all(heads, 'seq', split_axis=0, concat_axis=0, tiled=True)  5.87 us
    pallas_call x1, Pallas kernels, on_device(): call(attention_kernel, 'attention', [((NB, HD, BLK), BF), ((3 * HD, NB *...  5.66 us
    all_to_all x1, starting transfers between devices, on_device(): back = lax.all_to_all(back, 'seq', split_axis=0, concat_axis=0, tiled=True)  4.55 us
  transfers between devices with their start and end apart: 8, of which 5 were waited for; matrix products, arithmetic and copies ran while one was open for 0% of the time, Pallas kernels for 6%

profile of v4, /device:TPU:1, one launch (start us, length us, event | category | flops | bytes accessed | tf_op | source)
XLA Modules:
  0.0 106.8 jit_solution(1717856507014341869)
XLA Ops:
  0.6 3.5 %rows.1 = (bf16[16,288,128]{2,1,0:T(8,128)(2,1)}, bf16[1,32,512]{2,1,0:T(8,128)(2,1)S(1)}, bf16[1,32,512]{2,1,0:T(8,128)(2,1)S(1)}, f32[128,512]{1,0:T(8,128)S(1...) custom-call(s32[1,1024]{1,0:T(1,128)} %refs_0_.1, s32[1,1,2]{2,1,0:T(1,128)} %bitcast.6, bf16[512]{0:T(512)(128)(2,1)} %refs_2_.1, ...), custom_call_target="tpu_custom_call" | custom-call | flops 400000000 | bytes 3000000 | tf_op jit(solution)/shard_map/rows/pallas_call | solution.py:288
  4.1 7.6 %all-to-all-start = ((bf16[16,288,128]{2,1,0:T(8,128)(2,1)}), bf16[16,288,128]{2,1,0:T(8,128)(2,1)S(1)}, u32[]{:S(2)}, u32[]{:S(2)}) async-start(bf16[16,288,128]{2,1,0:T(8,128)(2,1)} %get-tuple-element.17), calls=%async_computation | async-start | bytes 2359296 | tf_op jit(solution)/shard_map/all_to_all | solution.py:306
  11.7 4.4 %collective-permute-start = (bf16[1,32,512]{2,1,0:T(8,128)(2,1)S(1)}, bf16[1,32,512]{2,1,0:T(8,128)(2,1)S(1)}, u32[]{:S(2)}, u32[]{:S(2)}) collective-permute-start(bf16[1,32,512]{2,1,0:T(8,128)(2,1)S(1)} %get-tuple-element.22), channel_id=1, source_target_pairs={{0,16},{16,32},{32,48},{48,64},{64,80},{80,96},{96,112},{112,128},... | collective-permute-start | bytes 98312 | tf_op jit(solution)/shard_map/ppermute | solution.py:308
  16.1 1.9 %collective-permute-start.1 = (bf16[1,32,512]{2,1,0:T(8,128)(2,1)S(1)}, bf16[1,32,512]{2,1,0:T(8,128)(2,1)S(1)}, u32[]{:S(2)}, u32[]{:S(2)}) collective-permute-start(bf16[1,32,512]{2,1,0:T(8,128)(2,1)S(1)} %get-tuple-element.23), channel_id=1, source_target_pairs={{16,0},{32,16},{48,32},{64,48},{80,64},{96,80},{112,96},{128,112},... | collective-permute-start | bytes 98312 | tf_op jit(solution)/shard_map/ppermute | solution.py:309
  18.1 3.6 %collective-permute-done.1.upper_ref = bf16[1,32,512]{2,1,0:T(8,128)(2,1)S(1)} collective-permute-done((bf16[1,32,512]{2,1,0:T(8,128)(2,1)S(1)}, bf16[1,32,512]{2,1,0:T(8,128)(2,1)S(1)}, u32[]{:S(2)}, u32[]{:S(2)}) %collective-permute-start.1) | collective-permute-done | bytes 32800 | tf_op jit(solution)/shard_map/ppermute | solution.py:309
  21.8 5.9 %all-to-all-done.x_ref = bf16[16,288,128]{2,1,0:T(8,128)(2,1)S(1)} async-done(((bf16[16,288,128]{2,1,0:T(8,128)(2,1)}), bf16[16,288,128]{2,1,0:T(8,128)(2,1)S(1)}, u32[]{:S(2)}, u32[]{:S(2)}) %all-to-all-start) | async-done | bytes 1179680 | tf_op jit(solution)/shard_map/all_to_all | solution.py:306
  27.7 2.7 %collective-permute-start.4 = (bf16[16,128,128]{2,1,0:T(8,128)(2,1)S(1)}, bf16[16,128,128]{2,1,0:T(8,128)(2,1)S(1)}, u32[]{:S(2)}, u32[]{:S(2)}) collective-permute-start(bf16[16,128,128]{2,1,0:T(8,128)(2,1)S(1)} %columns.1.own_ref), channel_id=1, source_target_pairs={{0,15},{1,14},{2,13},{3,12},{4,11},{5,10},{6,9},{7,8},{8,7},{9,6},... | collective-permute-start | bytes 1572872 | tf_op jit(solution)/shard_map/ppermute | solution.py:331
  30.4 1.9 %collective-permute-start.3 = (bf16[16,128,128]{2,1,0:T(8,128)(2,1)S(1)}, bf16[16,128,128]{2,1,0:T(8,128)(2,1)S(1)}, u32[]{:S(2)}, u32[]{:S(2)}) collective-permute-start(bf16[16,128,128]{2,1,0:T(8,128)(2,1)S(1)} %columns.1.own_ref), channel_id=1, source_target_pairs={{0,1},{1,0},{2,3},{3,2},{4,5},{5,4},{6,7},{7,6},{8,9},{9,8},{10,11... | collective-permute-start | bytes 1572872 | tf_op jit(solution)/shard_map/ppermute | solution.py:331
  32.4 3.2 %collective-permute-start.2 = (bf16[16,128,128]{2,1,0:T(8,128)(2,1)S(1)}, bf16[16,128,128]{2,1,0:T(8,128)(2,1)S(1)}, u32[]{:S(2)}, u32[]{:S(2)}) collective-permute-start(bf16[16,128,128]{2,1,0:T(8,128)(2,1)S(1)} %columns.1.own_ref), channel_id=1, source_target_pairs={{0,4},{1,5},{2,6},{3,7},{4,0},{5,1},{6,2},{7,3},{8,12},{9,13},{10,... | collective-permute-start | bytes 1572872 | tf_op jit(solution)/shard_map/ppermute | solution.py:331
  35.6 5.7 %attention.1 = (bf16[16,32,128]{2,1,0:T(8,128)(2,1)S(1)}, bf16[96,2048]{1,0:T(8,128)(2,1)S(1)}) custom-call(s32[1,16,16]{2,1,0:T(8,128)S(1)} %copy-done, bf16[16,288,128]{2,1,0:T(8,128)(2,1)S(1)} %all-to-all-done.x_ref), custom_call_target="tpu_custom_call" | custom-call | flops 5000000000 | bytes 20000000 | tf_op jit(solution)/shard_map/attention/pallas_call | solution.py:343
  41.2 1.0 collective-permute-done.4.far_ref
  42.3 1.2 %collective-permute-done.2.down_ref = bf16[16,128,128]{2,1,0:T(8,128)(2,1)S(1)} collective-permute-done((bf16[16,128,128]{2,1,0:T(8,128)(2,1)S(1)}, bf16[16,128,128]{2,1,0:T(8,128)(2,1)S(1)}, u32[]{:S(2)}, u32[]{:S(2)}) %collective-permute-start.2) | collective-permute-done | bytes 524320 | tf_op jit(solution)/shard_map/ppermute | solution.py:331
  43.4 0.5 weights.1
  43.9 6.9 %all_gather.12.both_ref = f32[16,48,128]{2,1,0:T(8,128)S(1)} all-gather(f32[8,48,128]{2,1,0:T(8,128)S(1)} %weights.1), channel_id=1, replica_groups={{0,16},{32,48},{64,80},{96,112},{128,144},{160,176},{192,208},{224,240}..., dimensions={0}, use_global_device_ids=true | all-gather | bytes 589824 | tf_op jit(solution)/shard_map/all_gather | solution.py:392
  50.8 13.5 %all_to_all.20.terms_ref = f32[4,48,128]{2,1,0:T(8,128)S(1)} all-to-all(f32[4,48,128]{2,1,0:T(8,128)S(1)} %chip_sum.1), channel_id=1, replica_groups={{0,32,64,96},{16,48,80,112},{128,160,192,224},{144,176,208,240},{256,28..., dimensions={0} | all-to-all | bytes 196608 | tf_op jit(solution)/shard_map/all_to_all | solution.py:387
  64.4 0.7 near_sum.1
  65.0 4.6 %all-to-all-start.2 = ((bf16[16,32,128]{2,1,0:T(8,128)(2,1)}), bf16[16,32,128]{2,1,0:T(8,128)(2,1)S(1)}, u32[]{:S(2)}, u32[]{:S(2)}) async-start(bf16[16,32,128]{2,1,0:T(8,128)(2,1)} %get-tuple-element.25), calls=%async_computation.2 | async-start | bytes 262144 | tf_op jit(solution)/shard_map/all_to_all | solution.py:410
  69.6 20.2 %all-gather = f32[192,128]{1,0:T(8,128)S(1)} all-gather(f32[48,128]{1,0:T(8,128)S(1)} %get-tuple-element.26), channel_id=2, replica_groups={{0,128,256,384},{16,144,272,400},{32,160,288,416},{48,176,304,432},{64,..., dimensions={0}, use_global_device_ids=true | all-gather | bytes 122880 | tf_op jit(solution)/shard_map/all_gather | solution.py:411
  89.8 0.7 far_sum.1
  90.4 3.5 %all-to-all-start.3 = ((f32[4,48,128]{2,1,0:T(8,128)}), f32[4,48,128]{2,1,0:T(8,128)S(1)}, u32[]{:S(2)}, u32[]{:S(2)}) async-start(f32[4,48,128]{2,1,0:T(8,128)} %far_sum.1), calls=%async_computation.3 | async-start | bytes 196608 | tf_op jit(solution)/shard_map/all_to_all | solution.py:387
  93.9 0.8 mixed.1
  94.7 3.9 %all-to-all-done.3 = f32[4,48,128]{2,1,0:T(8,128)S(1)} async-done(((f32[4,48,128]{2,1,0:T(8,128)}), f32[4,48,128]{2,1,0:T(8,128)S(1)}, u32[]{:S(2)}, u32[]{:S(2)}) %all-to-all-start.3) | async-done | bytes 98336 | tf_op jit(solution)/shard_map/all_to_all | solution.py:387
  98.6 7.6 %all_gather.15.all_ref = f32[8,48,128]{2,1,0:T(8,128)S(1)} all-gather(f32[4,48,128]{2,1,0:T(8,128)S(1)} %all-to-all-done.3), channel_id=1, replica_groups={{0,16},{32,48},{64,80},{96,112},{128,144},{160,176},{192,208},{224,240}..., dimensions={0}, use_global_device_ids=true | all-gather | bytes 294912 | tf_op jit(solution)/shard_map/all_gather | solution.py:392
  106.2 0.7 outputs.1
  (8 shorter events, 0.2 us)
Async XLA Ops:
  4.1 23.6 %all-to-all-start = ((bf16[16,288,128]{2,1,0:T(8,128)(2,1)}), bf16[16,288,128]{2,1,0:T(8,128)(2,1)S(1)}, u32[]{:S(2)}, u32[]{:S(2)}) async-start(bf16[16,288,128]{2,1,0:T(8,128)(2,1)} %get-tuple-element.17), calls=%async_computation | async-start | bytes 2359296 | tf_op jit(solution)/shard_map/all_to_all | solution.py:306
  11.7 6.3 %collective-permute-start = (bf16[1,32,512]{2,1,0:T(8,128)(2,1)S(1)}, bf16[1,32,512]{2,1,0:T(8,128)(2,1)S(1)}, u32[]{:S(2)}, u32[]{:S(2)}) collective-permute-start(bf16[1,32,512]{2,1,0:T(8,128)(2,1)S(1)} %get-tuple-element.22), channel_id=1, source_target_pairs={{0,16},{16,32},{32,48},{48,64},{64,80},{80,96},{96,112},{112,128},... | collective-permute-start | bytes 98312 | tf_op jit(solution)/shard_map/ppermute | solution.py:308
  16.1 5.5 %collective-permute-start.1 = (bf16[1,32,512]{2,1,0:T(8,128)(2,1)S(1)}, bf16[1,32,512]{2,1,0:T(8,128)(2,1)S(1)}, u32[]{:S(2)}, u32[]{:S(2)}) collective-permute-start(bf16[1,32,512]{2,1,0:T(8,128)(2,1)S(1)} %get-tuple-element.23), channel_id=1, source_target_pairs={{16,0},{32,16},{48,32},{64,48},{80,64},{96,80},{112,96},{128,112},... | collective-permute-start | bytes 98312 | tf_op jit(solution)/shard_map/ppermute | solution.py:309
  21.7 13.9 %copy-start = (s32[1,16,16]{2,1,0:T(8,128)S(1)}, s32[1,16,16]{2,1,0:T(8,128)}, u32[]{:S(2)}) copy-start(s32[1,16,16]{2,1,0:T(8,128)} %mask_ref.1) | copy-start | bytes 3076
  27.7 14.5 %collective-permute-start.4 = (bf16[16,128,128]{2,1,0:T(8,128)(2,1)S(1)}, bf16[16,128,128]{2,1,0:T(8,128)(2,1)S(1)}, u32[]{:S(2)}, u32[]{:S(2)}) collective-permute-start(bf16[16,128,128]{2,1,0:T(8,128)(2,1)S(1)} %columns.1.own_ref), channel_id=1, source_target_pairs={{0,15},{1,14},{2,13},{3,12},{4,11},{5,10},{6,9},{7,8},{8,7},{9,6},... | collective-permute-start | bytes 1572872 | tf_op jit(solution)/shard_map/ppermute | solution.py:331
  30.4 11.8 %collective-permute-start.3 = (bf16[16,128,128]{2,1,0:T(8,128)(2,1)S(1)}, bf16[16,128,128]{2,1,0:T(8,128)(2,1)S(1)}, u32[]{:S(2)}, u32[]{:S(2)}) collective-permute-start(bf16[16,128,128]{2,1,0:T(8,128)(2,1)S(1)} %columns.1.own_ref), channel_id=1, source_target_pairs={{0,1},{1,0},{2,3},{3,2},{4,5},{5,4},{6,7},{7,6},{8,9},{9,8},{10,11... | collective-permute-start | bytes 1572872 | tf_op jit(solution)/shard_map/ppermute | solution.py:331
  32.4 11.0 %collective-permute-start.2 = (bf16[16,128,128]{2,1,0:T(8,128)(2,1)S(1)}, bf16[16,128,128]{2,1,0:T(8,128)(2,1)S(1)}, u32[]{:S(2)}, u32[]{:S(2)}) collective-permute-start(bf16[16,128,128]{2,1,0:T(8,128)(2,1)S(1)} %columns.1.own_ref), channel_id=1, source_target_pairs={{0,4},{1,5},{2,6},{3,7},{4,0},{5,1},{6,2},{7,3},{8,12},{9,13},{10,... | collective-permute-start | bytes 1572872 | tf_op jit(solution)/shard_map/ppermute | solution.py:331
  65.0 24.8 %all-to-all-start.2 = ((bf16[16,32,128]{2,1,0:T(8,128)(2,1)}), bf16[16,32,128]{2,1,0:T(8,128)(2,1)S(1)}, u32[]{:S(2)}, u32[]{:S(2)}) async-start(bf16[16,32,128]{2,1,0:T(8,128)(2,1)} %get-tuple-element.25), calls=%async_computation.2 | async-start | bytes 262144 | tf_op jit(solution)/shard_map/all_to_all | solution.py:410
  90.4 8.2 %all-to-all-start.3 = ((f32[4,48,128]{2,1,0:T(8,128)}), f32[4,48,128]{2,1,0:T(8,128)S(1)}, u32[]{:S(2)}, u32[]{:S(2)}) async-start(f32[4,48,128]{2,1,0:T(8,128)} %far_sum.1), calls=%async_computation.3 | async-start | bytes 196608 | tf_op jit(solution)/shard_map/all_to_all | solution.py:387

commit v5 on v4

--- a/solution.py
+++ b/solution.py
@@ -25,6 +25,7 @@
 SM = pl.BlockSpec(memory_space=pltpu.SMEM)
 VM = pl.BlockSpec(memory_space=pltpu.VMEM)
 ANY = pl.BlockSpec(memory_space=pl.ANY)
+HBM = pl.BlockSpec(memory_space=pltpu.HBM)
 
 
 def group_of(place):
@@ -116,7 +117,7 @@
 
 
 def attention_kernel(
-    mask_ref, x_ref, back_ref, grad_ref, list_ref, keys, duo, expo, gprob, peak, top, total, inner,
+    mask_ref, x_ref, back_hbm, grad_ref, back_ref, sem, list_ref, keys, duo, expo, gprob, peak, top, total, inner,
     out_acc, q_acc, k_acc, v_acc,
 ):
     count = jnp.int32(0)
@@ -199,13 +200,17 @@
     lax.fori_loop(0, steps, grads, (jnp.int32(-1), wide, wide))
 
     for b in range(NB):
+        back_ref[b] = out_acc[b].astype(BF)
+    copy = pltpu.make_async_copy(back_ref, back_hbm, sem)
+    copy.start()
+    for b in range(NB):
         cols = slice(b * BLK, (b + 1) * BLK)
-        back_ref[b] = out_acc[b].astype(BF)
         grad_ref[0:32, cols] = q_acc[b].astype(BF)
         grad_ref[32:64, cols] = k_acc[b].astype(BF)
         grad_ref[64:96, cols] = (
             v_acc[b].astype(BF).astype(F32) + x_ref[b, BLK + 128 : BLK + 160, :].astype(F32)
         ).astype(BF)
+    copy.wait()
 
 
 def weights_kernel(
@@ -231,13 +236,12 @@
 
 
 def near_kernel(terms_ref, att_ref, sum_ref, att_out):
-    att_out[...] = att_ref[...]
     sum_ref[...] = (terms_ref[0] + terms_ref[1]) + (terms_ref[2] + terms_ref[3])
 
 
 def far_kernel(back_ref, terms_ref, copies_ref):
     total = (terms_ref[0] + terms_ref[1]) + (terms_ref[2] + terms_ref[3])
-    for n in range(NEAR):
+    for n in range(2 * NEAR):
         copies_ref[n] = total
 
 
@@ -245,7 +249,8 @@
     for lane in range(4):
         for half in range(2):
             rows = slice(half * CHUNK, (half + 1) * CHUNK)
-            full[rows, lane * 128 : (lane + 1) * 128] = all_ref[lane * 2 + half]
+            chunk = lane * 2 + half
+            full[rows, lane * 128 : (lane + 1) * 128] = all_ref[chunk % NEAR, chunk // NEAR]
     for place, ref in enumerate((q_ref, k_ref, v_ref)):
         ref[...] = full[place * HD : (place + 1) * HD, :]
 
@@ -261,14 +266,20 @@
     mixed_ref[0] = (attended + graph_ref[...]).astype(BF)
 
 
-def call(kernel, name, shapes, in_specs, scratch=(), limit=16, flops=0, moved=0):
-    out = tuple(jax.ShapeDtypeStruct(shape, kind) for shape, kind in shapes)
+def call(
+    kernel, name, shapes, in_specs, scratch=(), limit=16, flops=0, moved=0, outs=None, aliases=None
+):
+    outs = outs or [VM] * len(shapes)
     return pl.pallas_call(
         kernel,
-        out_shape=out,
+        out_shape=tuple(
+            (pltpu.HBM if spec is HBM else jax.ShapeDtypeStruct)(shape, kind)
+            for (shape, kind), spec in zip(shapes, outs)
+        ),
         in_specs=in_specs,
-        out_specs=tuple(VM for _ in out),
+        out_specs=tuple(outs),
         scratch_shapes=scratch,
+        input_output_aliases=aliases or {},
         compiler_params=pltpu.CompilerParams(vmem_limit_bytes=limit * 1024 * 1024),
         cost_estimate=pl.CostEstimate(flops=flops, bytes_accessed=moved, transcendentals=0),
         name=name,
@@ -345,7 +356,10 @@
         "attention",
         [((NB, HD, BLK), BF), ((3 * HD, NB * BLK), BF)],
         [SM, VM],
+        outs=[HBM, VM],
         scratch=[
+            pltpu.VMEM((NB, HD, BLK), BF),
+            pltpu.SemaphoreType.DMA,
             pltpu.SMEM((SLOTS + UNROLL,), jnp.int32),
             pltpu.VMEM((NB, BLK, 2 * HD), BF),
             pltpu.VMEM((NB + 1, 2 * HD, 2 * BLK), BF),
@@ -403,7 +417,9 @@
         near_kernel,
         "near_sum",
         [((CHUNK, 128), F32), ((NB, HD, BLK), BF)],
-        [VM, VM],
+        [VM, HBM],
+        outs=[VM, HBM],
+        aliases={1: 1},
         flops=100_000,
         moved=300_000,
     )(exchange(chip_sum, near), back)
@@ -412,12 +428,14 @@
     (copies,) = call(
         far_kernel,
         "far_sum",
-        [((NEAR, CHUNK, 128), F32)],
+        [((2 * NEAR, CHUNK, 128), F32)],
         [ANY, VM],
         flops=100_000,
         moved=300_000,
     )(back, terms)
-    reduced = gather(exchange(copies, near), cores)
+    block = [[g * span + n for n in range(span)] for g in range(clusters // span)]
+    order = exchange(copies, block)
+    reduced = order.reshape(NEAR, 2, CHUNK, 128)
     (mixed,) = call(
         mixed_kernel,
         "mixed",

time: 107 us -> 107 us (level); the launches traced: 107 us -> 105 us
  blocking collectives: 48.2 us -> 40.6 us
  starting transfers between devices: 29.7 us -> 34.6 us
  waiting for transfers between devices: 15.6 us -> 16.8 us
    all_gather x2 -> x1, blocking collectives: 14.5 us -> 6.91 us  [gather(): lax.all_gather(item, 'dp', axis=0, tiled=True, axis_index_groups=groups)]
    all_to_all x1, starting transfers between devices: 3.48 us -> 8.32 us  [exchange(): lax.all_to_all(item, 'dp', split_axis=0, concat_axis=0, tiled=True, axis_...]
    all_to_all x1, waiting for transfers between devices: 3.92 us -> 5.71 us  [exchange(): lax.all_to_all(item, 'dp', split_axis=0, concat_axis=0, tiled=True, axis_...]
  transfers between devices with their start and end apart: 8 -> 8, of which waited for: 5 -> 5; matrix products, arithmetic and copies ran while one was open for 0% -> 0% of each run, Pallas kernels for 6% -> 7%
where the time goes in v5:
time: 107 us; the launch traced here: 105 us
  blocking collectives  40.6 us (38%)
  starting transfers between devices  34.6 us (32%)
  waiting for transfers between devices  16.8 us (16%)
  Pallas kernels  12.6 us (12%)
    all_gather x1, blocking collectives, on_device(): lax.all_gather(near_sum, 'dp', axis=0, tiled=False, axis_index_groups=far)  20.2 us
    all_to_all x1, blocking collectives, exchange(): lax.all_to_all(item, 'dp', split_axis=0, concat_axis=0, tiled=True, axis_...  13.5 us
    all_to_all x1, starting transfers between devices, exchange(): lax.all_to_all(item, 'dp', split_axis=0, concat_axis=0, tiled=True, axis_...  8.32 us
    ppermute x3, starting transfers between devices, neighbour(): lax.ppermute(columns, 'seq', [(4 * y + x, 4 * ((turn(y) if down else y) %...  7.79 us
    all_to_all x1, starting transfers between devices, on_device(): x = lax.all_to_all(heads, 'seq', split_axis=0, concat_axis=0, tiled=True)  7.59 us
    all_gather x1, blocking collectives, gather(): lax.all_gather(item, 'dp', axis=0, tiled=True, axis_index_groups=groups)  6.91 us
    pallas_call x1, Pallas kernels, on_device(): call(attention_kernel, 'attention', [((NB, HD, BLK), BF), ((3 * HD, NB *...  6.26 us
    all_to_all x1, waiting for transfers between devices, on_device(): x = lax.all_to_all(heads, 'seq', split_axis=0, concat_axis=0, tiled=True)  5.87 us
  transfers between devices with their start and end apart: 8, of which 5 were waited for; matrix products, arithmetic and copies ran while one was open for 0% of the time, Pallas kernels for 7%

profile of v5, /device:TPU:1, one launch (start us, length us, event | category | flops | bytes accessed | tf_op | source)
XLA Modules:
  0.0 105.3 jit_solution(9023845198110641310)
XLA Ops:
  0.6 3.5 %rows.1 = (bf16[16,288,128]{2,1,0:T(8,128)(2,1)}, bf16[1,32,512]{2,1,0:T(8,128)(2,1)S(1)}, bf16[1,32,512]{2,1,0:T(8,128)(2,1)S(1)}, f32[128,512]{1,0:T(8,128)S(1...) custom-call(s32[1,1024]{1,0:T(1,128)} %refs_0_.1, s32[1,1,2]{2,1,0:T(1,128)} %bitcast.8, bf16[512]{0:T(512)(128)(2,1)} %refs_2_.1, ...), custom_call_target="tpu_custom_call" | custom-call | flops 400000000 | bytes 3000000 | tf_op jit(solution)/shard_map/rows/pallas_call | solution.py:299
  4.1 7.6 %all-to-all-start = ((bf16[16,288,128]{2,1,0:T(8,128)(2,1)}), bf16[16,288,128]{2,1,0:T(8,128)(2,1)S(1)}, u32[]{:S(2)}, u32[]{:S(2)}) async-start(bf16[16,288,128]{2,1,0:T(8,128)(2,1)} %get-tuple-element.17), calls=%async_computation | async-start | bytes 2359296 | tf_op jit(solution)/shard_map/all_to_all | solution.py:317
  11.7 4.4 %collective-permute-start = (bf16[1,32,512]{2,1,0:T(8,128)(2,1)S(1)}, bf16[1,32,512]{2,1,0:T(8,128)(2,1)S(1)}, u32[]{:S(2)}, u32[]{:S(2)}) collective-permute-start(bf16[1,32,512]{2,1,0:T(8,128)(2,1)S(1)} %get-tuple-element.22), channel_id=1, source_target_pairs={{0,16},{16,32},{32,48},{48,64},{64,80},{80,96},{96,112},{112,128},... | collective-permute-start | bytes 98312 | tf_op jit(solution)/shard_map/ppermute | solution.py:319
  16.1 1.9 %collective-permute-start.1 = (bf16[1,32,512]{2,1,0:T(8,128)(2,1)S(1)}, bf16[1,32,512]{2,1,0:T(8,128)(2,1)S(1)}, u32[]{:S(2)}, u32[]{:S(2)}) collective-permute-start(bf16[1,32,512]{2,1,0:T(8,128)(2,1)S(1)} %get-tuple-element.23), channel_id=1, source_target_pairs={{16,0},{32,16},{48,32},{64,48},{80,64},{96,80},{112,96},{128,112},... | collective-permute-start | bytes 98312 | tf_op jit(solution)/shard_map/ppermute | solution.py:320
  18.1 0.0 collective-permute-done.lower_ref
  18.1 3.6 %collective-permute-done.1.upper_ref = bf16[1,32,512]{2,1,0:T(8,128)(2,1)S(1)} collective-permute-done((bf16[1,32,512]{2,1,0:T(8,128)(2,1)S(1)}, bf16[1,32,512]{2,1,0:T(8,128)(2,1)S(1)}, u32[]{:S(2)}, u32[]{:S(2)}) %collective-permute-start.1) | collective-permute-done | bytes 32800 | tf_op jit(solution)/shard_map/ppermute | solution.py:320
  21.7 0.2 graph.1.graph_ref
  21.8 5.9 %all-to-all-done.x_ref = bf16[16,288,128]{2,1,0:T(8,128)(2,1)S(1)} async-done(((bf16[16,288,128]{2,1,0:T(8,128)(2,1)}), bf16[16,288,128]{2,1,0:T(8,128)(2,1)S(1)}, u32[]{:S(2)}, u32[]{:S(2)}) %all-to-all-start) | async-done | bytes 1179680 | tf_op jit(solution)/shard_map/all_to_all | solution.py:317
  27.7 2.7 %collective-permute-start.4 = (bf16[16,128,128]{2,1,0:T(8,128)(2,1)S(1)}, bf16[16,128,128]{2,1,0:T(8,128)(2,1)S(1)}, u32[]{:S(2)}, u32[]{:S(2)}) collective-permute-start(bf16[16,128,128]{2,1,0:T(8,128)(2,1)S(1)} %columns.1.own_ref), channel_id=1, source_target_pairs={{0,15},{1,14},{2,13},{3,12},{4,11},{5,10},{6,9},{7,8},{8,7},{9,6},... | collective-permute-start | bytes 1572872 | tf_op jit(solution)/shard_map/ppermute | solution.py:342
  30.4 1.9 %collective-permute-start.3 = (bf16[16,128,128]{2,1,0:T(8,128)(2,1)S(1)}, bf16[16,128,128]{2,1,0:T(8,128)(2,1)S(1)}, u32[]{:S(2)}, u32[]{:S(2)}) collective-permute-start(bf16[16,128,128]{2,1,0:T(8,128)(2,1)S(1)} %columns.1.own_ref), channel_id=1, source_target_pairs={{0,1},{1,0},{2,3},{3,2},{4,5},{5,4},{6,7},{7,6},{8,9},{9,8},{10,11... | collective-permute-start | bytes 1572872 | tf_op jit(solution)/shard_map/ppermute | solution.py:342
  32.4 3.2 %collective-permute-start.2 = (bf16[16,128,128]{2,1,0:T(8,128)(2,1)S(1)}, bf16[16,128,128]{2,1,0:T(8,128)(2,1)S(1)}, u32[]{:S(2)}, u32[]{:S(2)}) collective-permute-start(bf16[16,128,128]{2,1,0:T(8,128)(2,1)S(1)} %columns.1.own_ref), channel_id=1, source_target_pairs={{0,4},{1,5},{2,6},{3,7},{4,0},{5,1},{6,2},{7,3},{8,12},{9,13},{10,... | collective-permute-start | bytes 1572872 | tf_op jit(solution)/shard_map/ppermute | solution.py:342
  35.6 6.3 %attention.1 = (bf16[16,32,128]{2,1,0:T(8,128)(2,1)}, bf16[96,2048]{1,0:T(8,128)(2,1)S(1)}) custom-call(s32[1,16,16]{2,1,0:T(8,128)S(1)} %copy-done, bf16[16,288,128]{2,1,0:T(8,128)(2,1)S(1)} %all-to-all-done.x_ref), custom_call_target="tpu_custom_call" | custom-call | flops 5000000000 | bytes 20000000 | tf_op jit(solution)/shard_map/attention/pallas_call | solution.py:354
  41.8 0.4 collective-permute-done.4.far_ref
  42.3 1.2 %collective-permute-done.2.down_ref = bf16[16,128,128]{2,1,0:T(8,128)(2,1)S(1)} collective-permute-done((bf16[16,128,128]{2,1,0:T(8,128)(2,1)S(1)}, bf16[16,128,128]{2,1,0:T(8,128)(2,1)S(1)}, u32[]{:S(2)}, u32[]{:S(2)}) %collective-permute-start.2) | collective-permute-done | bytes 524320 | tf_op jit(solution)/shard_map/ppermute | solution.py:342
  43.4 0.5 weights.1
  43.9 6.9 %all_gather.9.both_ref = f32[16,48,128]{2,1,0:T(8,128)S(1)} all-gather(f32[8,48,128]{2,1,0:T(8,128)S(1)} %weights.1), channel_id=1, replica_groups={{0,16},{32,48},{64,80},{96,112},{128,144},{160,176},{192,208},{224,240}..., dimensions={0}, use_global_device_ids=true | all-gather | bytes 589824 | tf_op jit(solution)/shard_map/all_gather | solution.py:406
  50.8 13.5 %all_to_all.20.terms_ref = f32[4,48,128]{2,1,0:T(8,128)S(1)} all-to-all(f32[4,48,128]{2,1,0:T(8,128)S(1)} %chip_sum.1), channel_id=1, replica_groups={{0,32,64,96},{16,48,80,112},{128,160,192,224},{144,176,208,240},{256,28..., dimensions={0} | all-to-all | bytes 196608 | tf_op jit(solution)/shard_map/all_to_all | solution.py:401
  64.4 4.6 %all-to-all-start.2 = ((bf16[16,32,128]{2,1,0:T(8,128)(2,1)}), bf16[16,32,128]{2,1,0:T(8,128)(2,1)S(1)}, u32[]{:S(2)}, u32[]{:S(2)}) async-start(bf16[16,32,128]{2,1,0:T(8,128)(2,1)} %get-tuple-element.25), calls=%async_computation.2 | async-start | bytes 262144 | tf_op jit(solution)/shard_map/all_to_all | solution.py:426
  68.9 20.2 %all-gather = f32[192,128]{1,0:T(8,128)S(1)} all-gather(f32[48,128]{1,0:T(8,128)S(1)} %get-tuple-element.26), channel_id=2, replica_groups={{0,128,256,384},{16,144,272,400},{32,160,288,416},{48,176,304,432},{64,..., dimensions={0}, use_global_device_ids=true | all-gather | bytes 122880 | tf_op jit(solution)/shard_map/all_gather | solution.py:427
  89.1 0.7 far_sum.1
  89.8 8.3 %all-to-all-start.3 = ((f32[8,48,128]{2,1,0:T(8,128)}), f32[8,48,128]{2,1,0:T(8,128)S(1)}, u32[]{:S(2)}, u32[]{:S(2)}) async-start(f32[8,48,128]{2,1,0:T(8,128)} %far_sum.1), calls=%async_computation.3 | async-start | bytes 393216 | tf_op jit(solution)/shard_map/all_to_all | solution.py:401
  98.2 0.8 mixed.1
  98.9 5.7 %all-to-all-done.3 = f32[8,48,128]{2,1,0:T(8,128)S(1)} async-done(((f32[8,48,128]{2,1,0:T(8,128)}), f32[8,48,128]{2,1,0:T(8,128)S(1)}, u32[]{:S(2)}, u32[]{:S(2)}) %all-to-all-start.3) | async-done | bytes 196640 | tf_op jit(solution)/shard_map/all_to_all | solution.py:401
  104.6 0.7 outputs.1
  (7 shorter events, 0.1 us)
Async XLA Ops:
  4.1 23.6 %all-to-all-start = ((bf16[16,288,128]{2,1,0:T(8,128)(2,1)}), bf16[16,288,128]{2,1,0:T(8,128)(2,1)S(1)}, u32[]{:S(2)}, u32[]{:S(2)}) async-start(bf16[16,288,128]{2,1,0:T(8,128)(2,1)} %get-tuple-element.17), calls=%async_computation | async-start | bytes 2359296 | tf_op jit(solution)/shard_map/all_to_all | solution.py:317
  11.7 6.3 %collective-permute-start = (bf16[1,32,512]{2,1,0:T(8,128)(2,1)S(1)}, bf16[1,32,512]{2,1,0:T(8,128)(2,1)S(1)}, u32[]{:S(2)}, u32[]{:S(2)}) collective-permute-start(bf16[1,32,512]{2,1,0:T(8,128)(2,1)S(1)} %get-tuple-element.22), channel_id=1, source_target_pairs={{0,16},{16,32},{32,48},{48,64},{64,80},{80,96},{96,112},{112,128},... | collective-permute-start | bytes 98312 | tf_op jit(solution)/shard_map/ppermute | solution.py:319
  16.1 5.5 %collective-permute-start.1 = (bf16[1,32,512]{2,1,0:T(8,128)(2,1)S(1)}, bf16[1,32,512]{2,1,0:T(8,128)(2,1)S(1)}, u32[]{:S(2)}, u32[]{:S(2)}) collective-permute-start(bf16[1,32,512]{2,1,0:T(8,128)(2,1)S(1)} %get-tuple-element.23), channel_id=1, source_target_pairs={{16,0},{32,16},{48,32},{64,48},{80,64},{96,80},{112,96},{128,112},... | collective-permute-start | bytes 98312 | tf_op jit(solution)/shard_map/ppermute | solution.py:320
  21.7 13.9 %copy-start = (s32[1,16,16]{2,1,0:T(8,128)S(1)}, s32[1,16,16]{2,1,0:T(8,128)}, u32[]{:S(2)}) copy-start(s32[1,16,16]{2,1,0:T(8,128)} %mask_ref.1) | copy-start | bytes 3076
  27.7 14.5 %collective-permute-start.4 = (bf16[16,128,128]{2,1,0:T(8,128)(2,1)S(1)}, bf16[16,128,128]{2,1,0:T(8,128)(2,1)S(1)}, u32[]{:S(2)}, u32[]{:S(2)}) collective-permute-start(bf16[16,128,128]{2,1,0:T(8,128)(2,1)S(1)} %columns.1.own_ref), channel_id=1, source_target_pairs={{0,15},{1,14},{2,13},{3,12},{4,11},{5,10},{6,9},{7,8},{8,7},{9,6},... | collective-permute-start | bytes 1572872 | tf_op jit(solution)/shard_map/ppermute | solution.py:342
  30.4 11.8 %collective-permute-start.3 = (bf16[16,128,128]{2,1,0:T(8,128)(2,1)S(1)}, bf16[16,128,128]{2,1,0:T(8,128)(2,1)S(1)}, u32[]{:S(2)}, u32[]{:S(2)}) collective-permute-start(bf16[16,128,128]{2,1,0:T(8,128)(2,1)S(1)} %columns.1.own_ref), channel_id=1, source_target_pairs={{0,1},{1,0},{2,3},{3,2},{4,5},{5,4},{6,7},{7,6},{8,9},{9,8},{10,11... | collective-permute-start | bytes 1572872 | tf_op jit(solution)/shard_map/ppermute | solution.py:342
  32.4 11.0 %collective-permute-start.2 = (bf16[16,128,128]{2,1,0:T(8,128)(2,1)S(1)}, bf16[16,128,128]{2,1,0:T(8,128)(2,1)S(1)}, u32[]{:S(2)}, u32[]{:S(2)}) collective-permute-start(bf16[16,128,128]{2,1,0:T(8,128)(2,1)S(1)} %columns.1.own_ref), channel_id=1, source_target_pairs={{0,4},{1,5},{2,6},{3,7},{4,0},{5,1},{6,2},{7,3},{8,12},{9,13},{10,... | collective-permute-start | bytes 1572872 | tf_op jit(solution)/shard_map/ppermute | solution.py:342
  64.4 24.8 %all-to-all-start.2 = ((bf16[16,32,128]{2,1,0:T(8,128)(2,1)}), bf16[16,32,128]{2,1,0:T(8,128)(2,1)S(1)}, u32[]{:S(2)}, u32[]{:S(2)}) async-start(bf16[16,32,128]{2,1,0:T(8,128)(2,1)} %get-tuple-element.25), calls=%async_computation.2 | async-start | bytes 262144 | tf_op jit(solution)/shard_map/all_to_all | solution.py:426
  89.8 14.8 %all-to-all-start.3 = ((f32[8,48,128]{2,1,0:T(8,128)}), f32[8,48,128]{2,1,0:T(8,128)S(1)}, u32[]{:S(2)}, u32[]{:S(2)}) async-start(f32[8,48,128]{2,1,0:T(8,128)} %far_sum.1), calls=%async_computation.3 | async-start | bytes 393216 | tf_op jit(solution)/shard_map/all_to_all | solution.py:401

commit v6 on v5

--- a/solution.py
+++ b/solution.py
@@ -44,8 +44,22 @@
 
 def rows_kernel(*refs):
     sources, refs = refs[:11], refs[11:]
-    heads_ref, lower_ref, upper_ref, local_ref, degree_ref, pick_ref = refs[:6]
-    holds, sems = refs[6:17], refs[17]
+    heads_hbm, lower_ref, upper_ref, local_ref, degree_ref, pick_ref = refs[:6]
+    holds, (sems, heads_ref, heads_sems) = refs[6:17], refs[17:]
+
+    def leave(first, count, n):
+        rows = pl.ds(first, count)
+        copy = pltpu.make_async_copy(heads_ref.at[:, rows], heads_hbm.at[:, rows], heads_sems.at[n])
+        copy.start()
+        return copy
+
+    def put(item, place):
+        for head in range(HEADS):
+            heads_ref[head, BLK + place * HD : BLK + (place + 1) * HD, :] = item[
+                head * HD : (head + 1) * HD
+            ]
+        return leave(BLK + place * HD, HD, place)
+
     copies = [
         pltpu.make_async_copy(source, hold, sems.at[n])
         for n, (source, hold) in enumerate(zip(sources, holds))
@@ -68,20 +82,19 @@
         group = group_of(head)
         heads_ref[head, 0:BLK, :] = masked[:, group * 128 : (group + 1) * 128]
 
+    leaving = [leave(0, BLK, 5)]
     value_wide = jnp.dot(masked, wv_ref[...], preferred_element_type=F32)
     value = value_wide.astype(BF)
     for copy in copies[5:]:
         copy.wait()
-    links_low = links_ref[0].astype(F32).astype(BF)
-    local_ref[...] = value.astype(F32) + jnp.dot(links_low, value, preferred_element_type=F32)
+    key = jnp.dot(masked, wk_ref[...], preferred_element_type=F32).T.astype(BF)
+    query = jnp.dot(masked, wq_ref[...], preferred_element_type=F32).T.astype(BF)
+    leaving.append(put(value_wide.T.astype(BF), 1))
+    leaving.append(put(grad_ref[0].astype(F32).T.astype(BF), 3))
+    leaving.append(put(key, 0))
+    leaving.append(put(query, 2))
+
     slots = sends_ref.shape[2]
-    rows = lax.broadcasted_iota(jnp.int32, (ROWS, slots), 0)
-    for side, ref in ((0, lower_ref), (1, upper_ref)):
-        onehot = jnp.where(sends_ref[0, side : side + 1, :] == rows, 1.0, 0.0).astype(BF)
-        ref[0] = lax.dot_general(
-            onehot, value, (((0,), (0,)), ((), ())), preferred_element_type=F32
-        ).astype(BF)
-
     degree = 1.0 + jnp.sum(links_ref[0].astype(F32), axis=1, keepdims=True)
     for side in range(2):
         here = attach(
@@ -91,6 +104,7 @@
         degree = degree + jnp.sum(here, axis=1, keepdims=True)
     degree_ref[...] = degree
 
+    links_low = links_ref[0].astype(F32).astype(BF)
     scaled = (grad_ref[0].astype(F32) / degree).T
     high = scaled.astype(BF)
     rest = scaled - high.astype(F32)
@@ -99,17 +113,17 @@
     spread = jnp.dot(low, links_low, preferred_element_type=F32)
     spread = spread + jnp.dot(mid, links_low, preferred_element_type=F32)
     spread = spread + jnp.dot(high, links_low, preferred_element_type=F32)
-    graph_grad = (scaled + spread).astype(BF)
-
-    key = jnp.dot(masked, wk_ref[...], preferred_element_type=F32).T.astype(BF)
-    query = jnp.dot(masked, wq_ref[...], preferred_element_type=F32).T.astype(BF)
-    value_t = value_wide.T.astype(BF)
-    grad_t = grad_ref[0].astype(F32).T.astype(BF)
-    for place, item in enumerate((key, value_t, query, grad_t, graph_grad)):
-        for head in range(HEADS):
-            heads_ref[head, BLK + place * HD : BLK + (place + 1) * HD, :] = item[
-                head * HD : (head + 1) * HD
-            ]
+    leaving.append(put((scaled + spread).astype(BF), 4))
+
+    local_ref[...] = value.astype(F32) + jnp.dot(links_low, value, preferred_element_type=F32)
+    rows = lax.broadcasted_iota(jnp.int32, (ROWS, slots), 0)
+    for side, ref in ((0, lower_ref), (1, upper_ref)):
+        onehot = jnp.where(sends_ref[0, side : side + 1, :] == rows, 1.0, 0.0).astype(BF)
+        ref[0] = lax.dot_general(
+            onehot, value, (((0,), (0,)), ((), ())), preferred_element_type=F32
+        ).astype(BF)
+    for copy in leaving:
+        copy.wait()
 
 
 def columns_kernel(graph_ref, x_ref, columns_ref):
@@ -239,10 +253,12 @@
     sum_ref[...] = (terms_ref[0] + terms_ref[1]) + (terms_ref[2] + terms_ref[3])
 
 
-def far_kernel(back_ref, terms_ref, copies_ref):
+def far_kernel(terms_ref, att_ref, graph_ref, copies_ref, mixed_ref):
     total = (terms_ref[0] + terms_ref[1]) + (terms_ref[2] + terms_ref[3])
     for n in range(2 * NEAR):
         copies_ref[n] = total
+    attended = att_ref[...].reshape(WIDTH, ROWS).astype(F32).T
+    mixed_ref[0] = (attended + graph_ref[...]).astype(BF)
 
 
 def output_kernel(all_ref, q_ref, k_ref, v_ref, full):
@@ -259,11 +275,6 @@
     rows = jnp.concatenate([lower_ref[0], upper_ref[0]], axis=0)
     border = jnp.dot(pick_ref[...], rows, preferred_element_type=F32)
     graph_ref[...] = (local_ref[...] + border) / degree_ref[...]
-
-
-def mixed_kernel(att_ref, graph_ref, mixed_ref):
-    attended = att_ref[...].reshape(WIDTH, ROWS).astype(F32).T
-    mixed_ref[0] = (attended + graph_ref[...]).astype(BF)
 
 
 def call(
@@ -309,7 +320,12 @@
         ],
         [pl.BlockSpec(memory_space=pltpu.HBM)] * len(sources),
         scratch=[pltpu.VMEM(item.shape, item.dtype) for item in sources]
-        + [pltpu.SemaphoreType.DMA((len(sources),))],
+        + [
+            pltpu.SemaphoreType.DMA((len(sources),)),
+            pltpu.VMEM((HEADS, BLK + 5 * HD, ROWS), BF),
+            pltpu.SemaphoreType.DMA((6,)),
+        ],
+        outs=[HBM] + [VM] * 5,
         flops=400_000_000,
         moved=3_000_000,
     )(*[pltpu.with_memory_space_constraint(item, pltpu.HBM) for item in sources])
@@ -425,26 +441,17 @@
     )(exchange(chip_sum, near), back)
     back = lax.all_to_all(back, "seq", split_axis=0, concat_axis=0, tiled=True)
     terms = lax.all_gather(near_sum, "dp", axis=0, tiled=False, axis_index_groups=far)
-    (copies,) = call(
+    copies, mixed = call(
         far_kernel,
         "far_sum",
-        [((2 * NEAR, CHUNK, 128), F32)],
-        [ANY, VM],
+        [((2 * NEAR, CHUNK, 128), F32), ((1, ROWS, WIDTH), BF)],
+        [VM, VM, VM],
         flops=100_000,
         moved=300_000,
-    )(back, terms)
+    )(terms, back, graph)
     block = [[g * span + n for n in range(span)] for g in range(clusters // span)]
     order = exchange(copies, block)
     reduced = order.reshape(NEAR, 2, CHUNK, 128)
-    (mixed,) = call(
-        mixed_kernel,
-        "mixed",
-        [((1, ROWS, WIDTH), BF)],
-        [VM, VM],
-        flops=20_000_000,
-        moved=1_000_000,
-    )(back, graph)
-
     grad_query, grad_key, grad_value = call(
         output_kernel,
         "outputs",

time: 107 us -> 106 us (level)
  blocking collectives: 40.6 us -> 54.5 us
  starting transfers between devices: 34.6 us -> 26.3 us
  waiting for transfers between devices: 16.8 us -> 11 us
  Pallas kernels: 12.6 us -> 11.5 us
    all_to_all x1 -> x2, blocking collectives: 13.5 us -> 27.4 us  [exchange(): lax.all_to_all(item, 'dp', split_axis=0, concat_axis=0, tiled=True, axis_...]
    all_to_all x1 -> x0, starting transfers between devices: 8.32 us -> none  [exchange(): lax.all_to_all(item, 'dp', split_axis=0, concat_axis=0, tiled=True, axis_...]
    all_to_all x1 -> x0, waiting for transfers between devices: 5.71 us -> none  [exchange(): lax.all_to_all(item, 'dp', split_axis=0, concat_axis=0, tiled=True, axis_...]
  transfers between devices with their start and end apart: 8 -> 7, of which waited for: 5 -> 4; matrix products, arithmetic and copies ran while one was open for 0% -> 0% of each run, Pallas kernels for 7% -> 6%
where the time goes in v6:
time: 106 us; the launch traced here: 104 us
  blocking collectives  54.5 us (51%)
  starting transfers between devices  26.3 us (25%)
  Pallas kernels  11.5 us (11%)
  waiting for transfers between devices  11 us (10%)
    all_to_all x2, blocking collectives, exchange(): lax.all_to_all(item, 'dp', split_axis=0, concat_axis=0, tiled=True, axis_...  27.4 us
    all_gather x1, blocking collectives, on_device(): lax.all_gather(near_sum, 'dp', axis=0, tiled=False, axis_index_groups=far)  20.2 us
    ppermute x3, starting transfers between devices, neighbour(): lax.ppermute(columns, 'seq', [(4 * y + x, 4 * ((turn(y) if down else y) %...  7.79 us
    all_to_all x1, starting transfers between devices, on_device(): x = lax.all_to_all(heads, 'seq', split_axis=0, concat_axis=0, tiled=True)  7.59 us
    all_gather x1, blocking collectives, gather(): lax.all_gather(item, 'dp', axis=0, tiled=True, axis_index_groups=groups)  6.91 us
    pallas_call x1, Pallas kernels, on_device(): call(attention_kernel, 'attention', [((NB, HD, BLK), BF), ((3 * HD, NB *...  6.26 us
    all_to_all x1, waiting for transfers between devices, on_device(): x = lax.all_to_all(heads, 'seq', split_axis=0, concat_axis=0, tiled=True)  5.86 us
    all_to_all x1, starting transfers between devices, on_device(): back = lax.all_to_all(back, 'seq', split_axis=0, concat_axis=0, tiled=True)  4.58 us
  transfers between devices with their start and end apart: 7, of which 4 were waited for; matrix products, arithmetic and copies ran while one was open for 0% of the time, Pallas kernels for 6%

profile of v6, /device:TPU:1, one launch (start us, length us, event | category | flops | bytes accessed | tf_op | source)
XLA Modules:
  0.0 104.1 jit_solution(17648191159479431386)
XLA Ops:
  0.6 3.1 %rows.1 = (bf16[16,288,128]{2,1,0:T(8,128)(2,1)}, bf16[1,32,512]{2,1,0:T(8,128)(2,1)S(1)}, bf16[1,32,512]{2,1,0:T(8,128)(2,1)S(1)}, f32[128,512]{1,0:T(8,128)S(1...) custom-call(s32[1,1024]{1,0:T(1,128)} %refs_0_.1, s32[1,1,2]{2,1,0:T(1,128)} %bitcast.8, bf16[512]{0:T(512)(128)(2,1)} %refs_2_.1, ...), custom_call_target="tpu_custom_call" | custom-call | flops 400000000 | bytes 3000000 | tf_op jit(solution)/shard_map/rows/pallas_call | solution.py:310
  3.7 7.6 %all-to-all-start = ((bf16[16,288,128]{2,1,0:T(8,128)(2,1)}), bf16[16,288,128]{2,1,0:T(8,128)(2,1)S(1)}, u32[]{:S(2)}, u32[]{:S(2)}) async-start(bf16[16,288,128]{2,1,0:T(8,128)(2,1)} %get-tuple-element.19), calls=%async_computation | async-start | bytes 2359296 | tf_op jit(solution)/shard_map/all_to_all | solution.py:333
  11.3 4.4 %collective-permute-start = (bf16[1,32,512]{2,1,0:T(8,128)(2,1)S(1)}, bf16[1,32,512]{2,1,0:T(8,128)(2,1)S(1)}, u32[]{:S(2)}, u32[]{:S(2)}) collective-permute-start(bf16[1,32,512]{2,1,0:T(8,128)(2,1)S(1)} %get-tuple-element.24), channel_id=1, source_target_pairs={{0,16},{16,32},{32,48},{48,64},{64,80},{80,96},{96,112},{112,128},... | collective-permute-start | bytes 98312 | tf_op jit(solution)/shard_map/ppermute | solution.py:335
  15.7 1.9 %collective-permute-start.1 = (bf16[1,32,512]{2,1,0:T(8,128)(2,1)S(1)}, bf16[1,32,512]{2,1,0:T(8,128)(2,1)S(1)}, u32[]{:S(2)}, u32[]{:S(2)}) collective-permute-start(bf16[1,32,512]{2,1,0:T(8,128)(2,1)S(1)} %get-tuple-element.25), channel_id=1, source_target_pairs={{16,0},{32,16},{48,32},{64,48},{80,64},{96,80},{112,96},{128,112},... | collective-permute-start | bytes 98312 | tf_op jit(solution)/shard_map/ppermute | solution.py:336
  17.7 0.0 collective-permute-done.lower_ref
  17.7 3.6 %collective-permute-done.1.upper_ref = bf16[1,32,512]{2,1,0:T(8,128)(2,1)S(1)} collective-permute-done((bf16[1,32,512]{2,1,0:T(8,128)(2,1)S(1)}, bf16[1,32,512]{2,1,0:T(8,128)(2,1)S(1)}, u32[]{:S(2)}, u32[]{:S(2)}) %collective-permute-start.1) | collective-permute-done | bytes 32800 | tf_op jit(solution)/shard_map/ppermute | solution.py:336
  21.3 0.2 graph.1.graph_ref
  21.4 5.9 %all-to-all-done.x_ref = bf16[16,288,128]{2,1,0:T(8,128)(2,1)S(1)} async-done(((bf16[16,288,128]{2,1,0:T(8,128)(2,1)}), bf16[16,288,128]{2,1,0:T(8,128)(2,1)S(1)}, u32[]{:S(2)}, u32[]{:S(2)}) %all-to-all-start) | async-done | bytes 1179680 | tf_op jit(solution)/shard_map/all_to_all | solution.py:333
  27.3 2.7 %collective-permute-start.4 = (bf16[16,128,128]{2,1,0:T(8,128)(2,1)S(1)}, bf16[16,128,128]{2,1,0:T(8,128)(2,1)S(1)}, u32[]{:S(2)}, u32[]{:S(2)}) collective-permute-start(bf16[16,128,128]{2,1,0:T(8,128)(2,1)S(1)} %columns.1.own_ref), channel_id=1, source_target_pairs={{0,15},{1,14},{2,13},{3,12},{4,11},{5,10},{6,9},{7,8},{8,7},{9,6},... | collective-permute-start | bytes 1572872 | tf_op jit(solution)/shard_map/ppermute | solution.py:358
  30.0 1.9 %collective-permute-start.3 = (bf16[16,128,128]{2,1,0:T(8,128)(2,1)S(1)}, bf16[16,128,128]{2,1,0:T(8,128)(2,1)S(1)}, u32[]{:S(2)}, u32[]{:S(2)}) collective-permute-start(bf16[16,128,128]{2,1,0:T(8,128)(2,1)S(1)} %columns.1.own_ref), channel_id=1, source_target_pairs={{0,1},{1,0},{2,3},{3,2},{4,5},{5,4},{6,7},{7,6},{8,9},{9,8},{10,11... | collective-permute-start | bytes 1572872 | tf_op jit(solution)/shard_map/ppermute | solution.py:358
  32.0 3.2 %collective-permute-start.2 = (bf16[16,128,128]{2,1,0:T(8,128)(2,1)S(1)}, bf16[16,128,128]{2,1,0:T(8,128)(2,1)S(1)}, u32[]{:S(2)}, u32[]{:S(2)}) collective-permute-start(bf16[16,128,128]{2,1,0:T(8,128)(2,1)S(1)} %columns.1.own_ref), channel_id=1, source_target_pairs={{0,4},{1,5},{2,6},{3,7},{4,0},{5,1},{6,2},{7,3},{8,12},{9,13},{10,... | collective-permute-start | bytes 1572872 | tf_op jit(solution)/shard_map/ppermute | solution.py:358
  35.2 6.3 %attention.1 = (bf16[16,32,128]{2,1,0:T(8,128)(2,1)}, bf16[96,2048]{1,0:T(8,128)(2,1)S(1)}) custom-call(s32[1,16,16]{2,1,0:T(8,128)S(1)} %copy-done, bf16[16,288,128]{2,1,0:T(8,128)(2,1)S(1)} %all-to-all-done.x_ref), custom_call_target="tpu_custom_call" | custom-call | flops 5000000000 | bytes 20000000 | tf_op jit(solution)/shard_map/attention/pallas_call | solution.py:370
  41.4 0.4 collective-permute-done.4.far_ref
  41.9 0.0 collective-permute-done.3.right_ref
  41.9 1.2 %collective-permute-done.2.down_ref = bf16[16,128,128]{2,1,0:T(8,128)(2,1)S(1)} collective-permute-done((bf16[16,128,128]{2,1,0:T(8,128)(2,1)S(1)}, bf16[16,128,128]{2,1,0:T(8,128)(2,1)S(1)}, u32[]{:S(2)}, u32[]{:S(2)}) %collective-permute-start.2) | collective-permute-done | bytes 524320 | tf_op jit(solution)/shard_map/ppermute | solution.py:358
  43.0 0.5 weights.1
  43.5 6.9 %all_gather.9.both_ref = f32[16,48,128]{2,1,0:T(8,128)S(1)} all-gather(f32[8,48,128]{2,1,0:T(8,128)S(1)} %weights.1), channel_id=1, replica_groups={{0,16},{32,48},{64,80},{96,112},{128,144},{160,176},{192,208},{224,240}..., dimensions={0}, use_global_device_ids=true | all-gather | bytes 589824 | tf_op jit(solution)/shard_map/all_gather | solution.py:422
  50.4 13.5 %all_to_all.20.terms_ref = f32[4,48,128]{2,1,0:T(8,128)S(1)} all-to-all(f32[4,48,128]{2,1,0:T(8,128)S(1)} %chip_sum.1), channel_id=1, replica_groups={{0,32,64,96},{16,48,80,112},{128,160,192,224},{144,176,208,240},{256,28..., dimensions={0} | all-to-all | bytes 196608 | tf_op jit(solution)/shard_map/all_to_all | solution.py:417
  64.0 4.6 %all-to-all-start.2 = ((bf16[16,32,128]{2,1,0:T(8,128)(2,1)}), bf16[16,32,128]{2,1,0:T(8,128)(2,1)S(1)}, u32[]{:S(2)}, u32[]{:S(2)}) async-start(bf16[16,32,128]{2,1,0:T(8,128)(2,1)} %get-tuple-element.28), calls=%async_computation.2 | async-start | bytes 262144 | tf_op jit(solution)/shard_map/all_to_all | solution.py:442
  68.6 20.2 %all-gather = f32[192,128]{1,0:T(8,128)S(1)} all-gather(f32[48,128]{1,0:T(8,128)S(1)} %get-tuple-element.27), channel_id=2, replica_groups={{0,128,256,384},{16,144,272,400},{32,160,288,416},{48,176,304,432},{64,..., dimensions={0}, use_global_device_ids=true | all-gather | bytes 122880 | tf_op jit(solution)/shard_map/all_gather | solution.py:443
  88.7 0.0 all-to-all-done.2.att_ref
  88.7 0.8 far_sum.1
  89.5 13.9 %all_to_all.21 = f32[8,48,128]{2,1,0:T(8,128)S(1)} all-to-all(f32[8,48,128]{2,1,0:T(8,128)S(1)} %get-tuple-element.30), channel_id=1, replica_groups={{0,16,32,48,64,80,96,112},{128,144,160,176,192,208,224,240},{256,272,28..., dimensions={0} | all-to-all | bytes 393216 | tf_op jit(solution)/shard_map/all_to_all | solution.py:417
  103.4 0.7 outputs.1
  (5 shorter events, 0.1 us)
Async XLA Ops:
  3.7 23.6 %all-to-all-start = ((bf16[16,288,128]{2,1,0:T(8,128)(2,1)}), bf16[16,288,128]{2,1,0:T(8,128)(2,1)S(1)}, u32[]{:S(2)}, u32[]{:S(2)}) async-start(bf16[16,288,128]{2,1,0:T(8,128)(2,1)} %get-tuple-element.19), calls=%async_computation | async-start | bytes 2359296 | tf_op jit(solution)/shard_map/all_to_all | solution.py:333
  11.3 6.3 %collective-permute-start = (bf16[1,32,512]{2,1,0:T(8,128)(2,1)S(1)}, bf16[1,32,512]{2,1,0:T(8,128)(2,1)S(1)}, u32[]{:S(2)}, u32[]{:S(2)}) collective-permute-start(bf16[1,32,512]{2,1,0:T(8,128)(2,1)S(1)} %get-tuple-element.24), channel_id=1, source_target_pairs={{0,16},{16,32},{32,48},{48,64},{64,80},{80,96},{96,112},{112,128},... | collective-permute-start | bytes 98312 | tf_op jit(solution)/shard_map/ppermute | solution.py:335
  15.7 5.5 %collective-permute-start.1 = (bf16[1,32,512]{2,1,0:T(8,128)(2,1)S(1)}, bf16[1,32,512]{2,1,0:T(8,128)(2,1)S(1)}, u32[]{:S(2)}, u32[]{:S(2)}) collective-permute-start(bf16[1,32,512]{2,1,0:T(8,128)(2,1)S(1)} %get-tuple-element.25), channel_id=1, source_target_pairs={{16,0},{32,16},{48,32},{64,48},{80,64},{96,80},{112,96},{128,112},... | collective-permute-start | bytes 98312 | tf_op jit(solution)/shard_map/ppermute | solution.py:336
  21.3 13.9 %copy-start = (s32[1,16,16]{2,1,0:T(8,128)S(1)}, s32[1,16,16]{2,1,0:T(8,128)}, u32[]{:S(2)}) copy-start(s32[1,16,16]{2,1,0:T(8,128)} %mask_ref.1) | copy-start | bytes 3076
  27.3 14.5 %collective-permute-start.4 = (bf16[16,128,128]{2,1,0:T(8,128)(2,1)S(1)}, bf16[16,128,128]{2,1,0:T(8,128)(2,1)S(1)}, u32[]{:S(2)}, u32[]{:S(2)}) collective-permute-start(bf16[16,128,128]{2,1,0:T(8,128)(2,1)S(1)} %columns.1.own_ref), channel_id=1, source_target_pairs={{0,15},{1,14},{2,13},{3,12},{4,11},{5,10},{6,9},{7,8},{8,7},{9,6},... | collective-permute-start | bytes 1572872 | tf_op jit(solution)/shard_map/ppermute | solution.py:358
  30.0 11.8 %collective-permute-start.3 = (bf16[16,128,128]{2,1,0:T(8,128)(2,1)S(1)}, bf16[16,128,128]{2,1,0:T(8,128)(2,1)S(1)}, u32[]{:S(2)}, u32[]{:S(2)}) collective-permute-start(bf16[16,128,128]{2,1,0:T(8,128)(2,1)S(1)} %columns.1.own_ref), channel_id=1, source_target_pairs={{0,1},{1,0},{2,3},{3,2},{4,5},{5,4},{6,7},{7,6},{8,9},{9,8},{10,11... | collective-permute-start | bytes 1572872 | tf_op jit(solution)/shard_map/ppermute | solution.py:358
  32.0 11.0 %collective-permute-start.2 = (bf16[16,128,128]{2,1,0:T(8,128)(2,1)S(1)}, bf16[16,128,128]{2,1,0:T(8,128)(2,1)S(1)}, u32[]{:S(2)}, u32[]{:S(2)}) collective-permute-start(bf16[16,128,128]{2,1,0:T(8,128)(2,1)S(1)} %columns.1.own_ref), channel_id=1, source_target_pairs={{0,4},{1,5},{2,6},{3,7},{4,0},{5,1},{6,2},{7,3},{8,12},{9,13},{10,... | collective-permute-start | bytes 1572872 | tf_op jit(solution)/shard_map/ppermute | solution.py:358
  64.0 24.8 %all-to-all-start.2 = ((bf16[16,32,128]{2,1,0:T(8,128)(2,1)}), bf16[16,32,128]{2,1,0:T(8,128)(2,1)S(1)}, u32[]{:S(2)}, u32[]{:S(2)}) async-start(bf16[16,32,128]{2,1,0:T(8,128)(2,1)} %get-tuple-element.28), calls=%async_computation.2 | async-start | bytes 262144 | tf_op jit(solution)/shard_map/all_to_all | solution.py:442

commit v7 on v6

--- a/solution.py
+++ b/solution.py
@@ -241,16 +241,15 @@
             full[lax.bitwise_xor(group, flip)] = both[:, n * 128 : (n + 1) * 128]
     for lane in range(4):
         for half in range(2):
-            part_ref[lane * 2 + half] = full[lane, half * CHUNK : (half + 1) * CHUNK, :]
-
-
-def chip_kernel(both_ref, sum_ref):
-    start = lax.bitwise_and(lax.axis_index("dp"), 1) * NEAR
-    sum_ref[...] = both_ref[pl.ds(start, NEAR)] + both_ref[pl.ds(2 * NEAR + start, NEAR)]
+            chunk = lane * 2 + half
+            part_ref[chunk % NEAR * 2 + chunk // NEAR] = full[
+                lane, half * CHUNK : (half + 1) * CHUNK, :
+            ]
 
 
 def near_kernel(terms_ref, att_ref, sum_ref, att_out):
-    sum_ref[...] = (terms_ref[0] + terms_ref[1]) + (terms_ref[2] + terms_ref[3])
+    pairs = [terms_ref[2 * n] + terms_ref[2 * n + 1] for n in range(NEAR)]
+    sum_ref[...] = (pairs[0] + pairs[1]) + (pairs[2] + pairs[3])
 
 
 def far_kernel(terms_ref, att_ref, graph_ref, copies_ref, mixed_ref):
@@ -421,14 +420,7 @@
     def gather(item, groups):
         return lax.all_gather(item, "dp", axis=0, tiled=True, axis_index_groups=groups)
 
-    (chip_sum,) = call(
-        chip_kernel,
-        "chip_sum",
-        [((NEAR, CHUNK, 128), F32)],
-        [VM],
-        flops=100_000,
-        moved=300_000,
-    )(gather(part, cores))
+    block = [[g * span + n for n in range(span)] for g in range(clusters // span)]
     near_sum, back = call(
         near_kernel,
         "near_sum",
@@ -438,7 +430,7 @@
         aliases={1: 1},
         flops=100_000,
         moved=300_000,
-    )(exchange(chip_sum, near), back)
+    )(exchange(part, block), back)
     back = lax.all_to_all(back, "seq", split_axis=0, concat_axis=0, tiled=True)
     terms = lax.all_gather(near_sum, "dp", axis=0, tiled=False, axis_index_groups=far)
     copies, mixed = call(
@@ -449,7 +441,6 @@
         flops=100_000,
         moved=300_000,
     )(terms, back, graph)
-    block = [[g * span + n for n in range(span)] for g in range(clusters // span)]
     order = exchange(copies, block)
     reduced = order.reshape(NEAR, 2, CHUNK, 128)
     grad_query, grad_key, grad_value = call(

time: 106 us -> 106 us (level)
    all_to_all x2, blocking collectives: 27.4 us -> 34.6 us  [exchange(): lax.all_to_all(item, 'dp', split_axis=0, concat_axis=0, tiled=True, axis_...]
    all_gather x1 -> x0, blocking collectives: 6.91 us -> none  [gather(): lax.all_gather(item, 'dp', axis=0, tiled=True, axis_index_groups=groups)]
where the time goes in v7:
time: 106 us; the launch traced here: 105 us
  blocking collectives  55 us (52%)
  starting transfers between devices  26.3 us (25%)
  Pallas kernels  11.5 us (11%)
  waiting for transfers between devices  11 us (10%)
    all_to_all x2, blocking collectives, exchange(): lax.all_to_all(item, 'dp', split_axis=0, concat_axis=0, tiled=True, axis_...  34.6 us
    all_gather x1, blocking collectives, on_device(): lax.all_gather(near_sum, 'dp', axis=0, tiled=False, axis_index_groups=far)  20.4 us
    ppermute x3, starting transfers between devices, neighbour(): lax.ppermute(columns, 'seq', [(4 * y + x, 4 * ((turn(y) if down else y) %...  7.79 us
    all_to_all x1, starting transfers between devices, on_device(): x = lax.all_to_all(heads, 'seq', split_axis=0, concat_axis=0, tiled=True)  7.59 us
    pallas_call x1, Pallas kernels, on_device(): call(attention_kernel, 'attention', [((NB, HD, BLK), BF), ((3 * HD, NB *...  6.26 us
    all_to_all x1, waiting for transfers between devices, on_device(): x = lax.all_to_all(heads, 'seq', split_axis=0, concat_axis=0, tiled=True)  5.86 us
    all_to_all x1, starting transfers between devices, on_device(): back = lax.all_to_all(back, 'seq', split_axis=0, concat_axis=0, tiled=True)  4.58 us
    ppermute x1, starting transfers between devices, on_device(): lower = lax.ppermute(send_lower, 'dp', up)  4.39 us
  transfers between devices with their start and end apart: 7, of which 4 were waited for; matrix products, arithmetic and copies ran while one was open for 0% of the time, Pallas kernels for 6%

profile of v7, /device:TPU:1, one launch (start us, length us, event | category | flops | bytes accessed | tf_op | source)
XLA Modules:
  0.0 104.6 jit_solution(1394371825712226925)
XLA Ops:
  0.6 3.1 %rows.1 = (bf16[16,288,128]{2,1,0:T(8,128)(2,1)}, bf16[1,32,512]{2,1,0:T(8,128)(2,1)S(1)}, bf16[1,32,512]{2,1,0:T(8,128)(2,1)S(1)}, f32[128,512]{1,0:T(8,128)S(1...) custom-call(s32[1,1024]{1,0:T(1,128)} %refs_0_.1, s32[1,1,2]{2,1,0:T(1,128)} %bitcast.8, bf16[512]{0:T(512)(128)(2,1)} %refs_2_.1, ...), custom_call_target="tpu_custom_call" | custom-call | flops 400000000 | bytes 3000000 | tf_op jit(solution)/shard_map/rows/pallas_call | solution.py:309
  3.7 7.6 %all-to-all-start = ((bf16[16,288,128]{2,1,0:T(8,128)(2,1)}), bf16[16,288,128]{2,1,0:T(8,128)(2,1)S(1)}, u32[]{:S(2)}, u32[]{:S(2)}) async-start(bf16[16,288,128]{2,1,0:T(8,128)(2,1)} %get-tuple-element.19), calls=%async_computation | async-start | bytes 2359296 | tf_op jit(solution)/shard_map/all_to_all | solution.py:332
  11.3 4.4 %collective-permute-start = (bf16[1,32,512]{2,1,0:T(8,128)(2,1)S(1)}, bf16[1,32,512]{2,1,0:T(8,128)(2,1)S(1)}, u32[]{:S(2)}, u32[]{:S(2)}) collective-permute-start(bf16[1,32,512]{2,1,0:T(8,128)(2,1)S(1)} %get-tuple-element.24), channel_id=1, source_target_pairs={{0,16},{16,32},{32,48},{48,64},{64,80},{80,96},{96,112},{112,128},... | collective-permute-start | bytes 98312 | tf_op jit(solution)/shard_map/ppermute | solution.py:334
  15.7 1.9 %collective-permute-start.1 = (bf16[1,32,512]{2,1,0:T(8,128)(2,1)S(1)}, bf16[1,32,512]{2,1,0:T(8,128)(2,1)S(1)}, u32[]{:S(2)}, u32[]{:S(2)}) collective-permute-start(bf16[1,32,512]{2,1,0:T(8,128)(2,1)S(1)} %get-tuple-element.25), channel_id=1, source_target_pairs={{16,0},{32,16},{48,32},{64,48},{80,64},{96,80},{112,96},{128,112},... | collective-permute-start | bytes 98312 | tf_op jit(solution)/shard_map/ppermute | solution.py:335
  17.7 0.0 collective-permute-done.lower_ref
  17.7 3.6 %collective-permute-done.1.upper_ref = bf16[1,32,512]{2,1,0:T(8,128)(2,1)S(1)} collective-permute-done((bf16[1,32,512]{2,1,0:T(8,128)(2,1)S(1)}, bf16[1,32,512]{2,1,0:T(8,128)(2,1)S(1)}, u32[]{:S(2)}, u32[]{:S(2)}) %collective-permute-start.1) | collective-permute-done | bytes 32800 | tf_op jit(solution)/shard_map/ppermute | solution.py:335
  21.3 0.2 graph.1.graph_ref
  21.4 5.9 %all-to-all-done.x_ref = bf16[16,288,128]{2,1,0:T(8,128)(2,1)S(1)} async-done(((bf16[16,288,128]{2,1,0:T(8,128)(2,1)}), bf16[16,288,128]{2,1,0:T(8,128)(2,1)S(1)}, u32[]{:S(2)}, u32[]{:S(2)}) %all-to-all-start) | async-done | bytes 1179680 | tf_op jit(solution)/shard_map/all_to_all | solution.py:332
  27.3 2.7 %collective-permute-start.4 = (bf16[16,128,128]{2,1,0:T(8,128)(2,1)S(1)}, bf16[16,128,128]{2,1,0:T(8,128)(2,1)S(1)}, u32[]{:S(2)}, u32[]{:S(2)}) collective-permute-start(bf16[16,128,128]{2,1,0:T(8,128)(2,1)S(1)} %columns.1.own_ref), channel_id=1, source_target_pairs={{0,15},{1,14},{2,13},{3,12},{4,11},{5,10},{6,9},{7,8},{8,7},{9,6},... | collective-permute-start | bytes 1572872 | tf_op jit(solution)/shard_map/ppermute | solution.py:357
  30.0 1.9 %collective-permute-start.3 = (bf16[16,128,128]{2,1,0:T(8,128)(2,1)S(1)}, bf16[16,128,128]{2,1,0:T(8,128)(2,1)S(1)}, u32[]{:S(2)}, u32[]{:S(2)}) collective-permute-start(bf16[16,128,128]{2,1,0:T(8,128)(2,1)S(1)} %columns.1.own_ref), channel_id=1, source_target_pairs={{0,1},{1,0},{2,3},{3,2},{4,5},{5,4},{6,7},{7,6},{8,9},{9,8},{10,11... | collective-permute-start | bytes 1572872 | tf_op jit(solution)/shard_map/ppermute | solution.py:357
  32.0 3.2 %collective-permute-start.2 = (bf16[16,128,128]{2,1,0:T(8,128)(2,1)S(1)}, bf16[16,128,128]{2,1,0:T(8,128)(2,1)S(1)}, u32[]{:S(2)}, u32[]{:S(2)}) collective-permute-start(bf16[16,128,128]{2,1,0:T(8,128)(2,1)S(1)} %columns.1.own_ref), channel_id=1, source_target_pairs={{0,4},{1,5},{2,6},{3,7},{4,0},{5,1},{6,2},{7,3},{8,12},{9,13},{10,... | collective-permute-start | bytes 1572872 | tf_op jit(solution)/shard_map/ppermute | solution.py:357
  35.2 0.0 copy-done
  35.2 6.3 %attention.1 = (bf16[16,32,128]{2,1,0:T(8,128)(2,1)}, bf16[96,2048]{1,0:T(8,128)(2,1)S(1)}) custom-call(s32[1,16,16]{2,1,0:T(8,128)S(1)} %copy-done, bf16[16,288,128]{2,1,0:T(8,128)(2,1)S(1)} %all-to-all-done.x_ref), custom_call_target="tpu_custom_call" | custom-call | flops 5000000000 | bytes 20000000 | tf_op jit(solution)/shard_map/attention/pallas_call | solution.py:369
  41.4 0.4 collective-permute-done.4.far_ref
  41.9 0.0 collective-permute-done.3.right_ref
  41.9 1.2 %collective-permute-done.2.down_ref = bf16[16,128,128]{2,1,0:T(8,128)(2,1)S(1)} collective-permute-done((bf16[16,128,128]{2,1,0:T(8,128)(2,1)S(1)}, bf16[16,128,128]{2,1,0:T(8,128)(2,1)S(1)}, u32[]{:S(2)}, u32[]{:S(2)}) %collective-permute-start.2) | collective-permute-done | bytes 524320 | tf_op jit(solution)/shard_map/ppermute | solution.py:357
  43.0 0.5 weights.1
  43.5 20.8 %all_to_all.20.terms_ref = f32[8,48,128]{2,1,0:T(8,128)S(1)} all-to-all(f32[8,48,128]{2,1,0:T(8,128)S(1)} %weights.1), channel_id=1, replica_groups={{0,16,32,48,64,80,96,112},{128,144,160,176,192,208,224,240},{256,272,28..., dimensions={0} | all-to-all | bytes 393216 | tf_op jit(solution)/shard_map/all_to_all | solution.py:416
  64.3 4.6 %all-to-all-start.2 = ((bf16[16,32,128]{2,1,0:T(8,128)(2,1)}), bf16[16,32,128]{2,1,0:T(8,128)(2,1)S(1)}, u32[]{:S(2)}, u32[]{:S(2)}) async-start(bf16[16,32,128]{2,1,0:T(8,128)(2,1)} %get-tuple-element.28), calls=%async_computation.2 | async-start | bytes 262144 | tf_op jit(solution)/shard_map/all_to_all | solution.py:434
  68.9 20.4 %all-gather = f32[192,128]{1,0:T(8,128)S(1)} all-gather(f32[48,128]{1,0:T(8,128)S(1)} %get-tuple-element.27), channel_id=2, replica_groups={{0,128,256,384},{16,144,272,400},{32,160,288,416},{48,176,304,432},{64,..., dimensions={0}, use_global_device_ids=true | all-gather | bytes 122880 | tf_op jit(solution)/shard_map/all_gather | solution.py:435
  89.3 0.0 all-to-all-done.2.att_ref
  89.3 0.8 far_sum.1
  90.0 13.9 %all_to_all.21 = f32[8,48,128]{2,1,0:T(8,128)S(1)} all-to-all(f32[8,48,128]{2,1,0:T(8,128)S(1)} %get-tuple-element.30), channel_id=1, replica_groups={{0,16,32,48,64,80,96,112},{128,144,160,176,192,208,224,240},{256,272,28..., dimensions={0} | all-to-all | bytes 393216 | tf_op jit(solution)/shard_map/all_to_all | solution.py:416
  103.9 0.7 outputs.1
  (3 shorter events, 0.0 us)
Async XLA Ops:
  3.7 23.6 %all-to-all-start = ((bf16[16,288,128]{2,1,0:T(8,128)(2,1)}), bf16[16,288,128]{2,1,0:T(8,128)(2,1)S(1)}, u32[]{:S(2)}, u32[]{:S(2)}) async-start(bf16[16,288,128]{2,1,0:T(8,128)(2,1)} %get-tuple-element.19), calls=%async_computation | async-start | bytes 2359296 | tf_op jit(solution)/shard_map/all_to_all | solution.py:332
  11.3 6.3 %collective-permute-start = (bf16[1,32,512]{2,1,0:T(8,128)(2,1)S(1)}, bf16[1,32,512]{2,1,0:T(8,128)(2,1)S(1)}, u32[]{:S(2)}, u32[]{:S(2)}) collective-permute-start(bf16[1,32,512]{2,1,0:T(8,128)(2,1)S(1)} %get-tuple-element.24), channel_id=1, source_target_pairs={{0,16},{16,32},{32,48},{48,64},{64,80},{80,96},{96,112},{112,128},... | collective-permute-start | bytes 98312 | tf_op jit(solution)/shard_map/ppermute | solution.py:334
  15.7 5.5 %collective-permute-start.1 = (bf16[1,32,512]{2,1,0:T(8,128)(2,1)S(1)}, bf16[1,32,512]{2,1,0:T(8,128)(2,1)S(1)}, u32[]{:S(2)}, u32[]{:S(2)}) collective-permute-start(bf16[1,32,512]{2,1,0:T(8,128)(2,1)S(1)} %get-tuple-element.25), channel_id=1, source_target_pairs={{16,0},{32,16},{48,32},{64,48},{80,64},{96,80},{112,96},{128,112},... | collective-permute-start | bytes 98312 | tf_op jit(solution)/shard_map/ppermute | solution.py:335
  21.3 13.9 %copy-start = (s32[1,16,16]{2,1,0:T(8,128)S(1)}, s32[1,16,16]{2,1,0:T(8,128)}, u32[]{:S(2)}) copy-start(s32[1,16,16]{2,1,0:T(8,128)} %mask_ref.1) | copy-start | bytes 3076
  27.3 14.5 %collective-permute-start.4 = (bf16[16,128,128]{2,1,0:T(8,128)(2,1)S(1)}, bf16[16,128,128]{2,1,0:T(8,128)(2,1)S(1)}, u32[]{:S(2)}, u32[]{:S(2)}) collective-permute-start(bf16[16,128,128]{2,1,0:T(8,128)(2,1)S(1)} %columns.1.own_ref), channel_id=1, source_target_pairs={{0,15},{1,14},{2,13},{3,12},{4,11},{5,10},{6,9},{7,8},{8,7},{9,6},... | collective-permute-start | bytes 1572872 | tf_op jit(solution)/shard_map/ppermute | solution.py:357
  30.0 11.8 %collective-permute-start.3 = (bf16[16,128,128]{2,1,0:T(8,128)(2,1)S(1)}, bf16[16,128,128]{2,1,0:T(8,128)(2,1)S(1)}, u32[]{:S(2)}, u32[]{:S(2)}) collective-permute-start(bf16[16,128,128]{2,1,0:T(8,128)(2,1)S(1)} %columns.1.own_ref), channel_id=1, source_target_pairs={{0,1},{1,0},{2,3},{3,2},{4,5},{5,4},{6,7},{7,6},{8,9},{9,8},{10,11... | collective-permute-start | bytes 1572872 | tf_op jit(solution)/shard_map/ppermute | solution.py:357
  32.0 11.0 %collective-permute-start.2 = (bf16[16,128,128]{2,1,0:T(8,128)(2,1)S(1)}, bf16[16,128,128]{2,1,0:T(8,128)(2,1)S(1)}, u32[]{:S(2)}, u32[]{:S(2)}) collective-permute-start(bf16[16,128,128]{2,1,0:T(8,128)(2,1)S(1)} %columns.1.own_ref), channel_id=1, source_target_pairs={{0,4},{1,5},{2,6},{3,7},{4,0},{5,1},{6,2},{7,3},{8,12},{9,13},{10,... | collective-permute-start | bytes 1572872 | tf_op jit(solution)/shard_map/ppermute | solution.py:357
  64.3 25.0 %all-to-all-start.2 = ((bf16[16,32,128]{2,1,0:T(8,128)(2,1)}), bf16[16,32,128]{2,1,0:T(8,128)(2,1)S(1)}, u32[]{:S(2)}, u32[]{:S(2)}) async-start(bf16[16,32,128]{2,1,0:T(8,128)(2,1)} %get-tuple-element.28), calls=%async_computation.2 | async-start | bytes 262144 | tf_op jit(solution)/shard_map/all_to_all | solution.py:434
